TPU v7x, 256 devices: a whole 4x4x8 slice. The times are simulated.
256 devices in a mesh: spatial: 64 (over y, z, core), dp: 4 (over x).
Axes of the slice: x: 4, y: 4, z: 8, core: 2. Of those that a mesh axis runs over, the one named last changes fastest.
Arguments:
- features: bfloat16 [4, 384, 8, 8, 512], P('dp', 'spatial'), may hold values from -6 to 6
- masks: int32 [4, 384, 512], P('dp', 'spatial'), may hold values 0 or 1
- rulebook: int32 [4, 384, 27], P('dp', 'spatial'), may hold values from 0 to 134, as said below
- send_lists: int32 [4, 64, 64, 2], P('dp', 'spatial'), may hold values from 0 to 6, as said below
- conv_weight: bfloat16 [27, 64, 64], replicated, may hold values from -0.15625 to 0.15625
- down_weight: bfloat16 [8, 64, 128], replicated, may hold values from -0.25 to 0.25
- cotangent: bfloat16 [4, 384, 4, 4, 512], P('dp', 'spatial'), may hold values from -6 to 6
Outputs:
- coarse_out: bfloat16 [4, 384, 4, 4, 512], P('dp', 'spatial')
- grad_features: bfloat16 [4, 384, 8, 8, 512], P('dp', 'spatial')
- grad_conv: float32 [27, 64, 64], replicated
- grad_down: float32 [8, 64, 128], replicated
Inputs may be any that keep to these rules, and one draw needn't show every extreme that they name: `send_lists`: with q = d // 16, device d of spatial is region ((q % 2) (2) + q // 2, (d // 4) % 4, d % 4) of a 4^3 grid without wrap. A device sends 2 distinct bricks to each region sharing a face with it, one brick (slot 0) to each sharing only an edge or a corner, and nothing to itself or to other regions; empty slots hold 6. Entries index the owning device's extended list; entry 13 of a brick is the brick's own local index; entries name only own bricks, filled received slots and 134, and each of these appears in the device's rulebook.
All inputs are finite; a program needn't handle non-finite values. No bound on the sum of `masks` on one device may be relied on, other than what follows from the above.
Results may differ from a plain program's by a relative error of at most 0.0095.
Values may be sent and summed in bfloat16 or wider, within the bound.
No kernel may reach another device: no remote copies, remote signals or barrier semaphores. Data moves between devices by JAX's collectives and lax.ppermute only.
A program may use at most 192 MiB of HBM per device.

v0:
```python
import jax
import jax.numpy as jnp
import numpy as np
from jax import lax
from jax.sharding import PartitionSpec as P


def rim_range(pos, edge):
    if pos == 0:
        return (edge - 1, edge)
    if pos == 1:
        return (0, edge)
    return (0, 1)


def pad_range(pos, edge):
    if pos == 0:
        return (0, 1)
    if pos == 1:
        return (1, edge + 1)
    return (edge + 1, edge + 2)


def assemble(extended, table, edge, width):
    planes = []
    for x_pos in range(3):
        rows = []
        for y_pos in range(3):
            cols = []
            for z_pos in range(3):
                x_lo, x_hi = rim_range(x_pos, edge)
                y_lo, y_hi = rim_range(y_pos, edge)
                z_lo, z_hi = rim_range(z_pos, edge)
                part = extended[:, x_lo:x_hi, y_lo:y_hi, z_lo * width : z_hi * width]
                cols.append(jnp.take(part, table[:, x_pos * 9 + y_pos * 3 + z_pos], axis=0))
            rows.append(jnp.concatenate(cols, axis=3))
        planes.append(jnp.concatenate(rows, axis=2))
    return jnp.concatenate(planes, axis=1)


def spread(grad_padded, table, edge, width, total_count):
    count = grad_padded.shape[0]
    datas = []
    targets = []
    for x_pos in range(3):
        for y_pos in range(3):
            for z_pos in range(3):
                x_lo, x_hi = rim_range(x_pos, edge)
                y_lo, y_hi = rim_range(y_pos, edge)
                z_lo, z_hi = rim_range(z_pos, edge)
                px_lo, px_hi = pad_range(x_pos, edge)
                py_lo, py_hi = pad_range(y_pos, edge)
                pz_lo, pz_hi = pad_range(z_pos, edge)
                piece = grad_padded[:, px_lo:px_hi, py_lo:py_hi, pz_lo * width : pz_hi * width]
                voxels_here = (x_hi - x_lo) * (y_hi - y_lo) * (z_hi - z_lo)
                datas.append(piece.reshape(count, voxels_here, width))
                grid_x, grid_y, grid_z = np.meshgrid(
                    np.arange(x_lo, x_hi),
                    np.arange(y_lo, y_hi),
                    np.arange(z_lo, z_hi),
                    indexing="ij",
                )
                local = ((grid_x * edge + grid_y) * edge + grid_z).reshape(-1).astype(np.int32)
                dest = (
                    table[:, x_pos * 9 + y_pos * 3 + z_pos][:, None] * edge**3
                    + jnp.asarray(local)[None, :]
                )
                targets.append(dest.astype(jnp.int32))
    data_all = jnp.concatenate(datas, axis=1).reshape(-1, width)
    target_all = jnp.concatenate(targets, axis=1).reshape(-1)
    summed = jax.ops.segment_sum(data_all, target_all, num_segments=total_count * edge**3)
    return summed.reshape(total_count, edge, edge, edge * width)


def pair_weights(conv_weight, width):
    taps = conv_weight.reshape(3, 3, 3, width, width)
    zero = jnp.zeros((3, 3, 1, width, width), conv_weight.dtype)
    first = jnp.concatenate([taps, zero], axis=2)
    second = jnp.concatenate([zero, taps], axis=2)
    return jnp.stack([first, second], axis=4).reshape(9, 4 * width, 2 * width)


def pair_to_taps(pair_grad, width):
    blocks = pair_grad.reshape(3, 3, 4, width, 2, width)
    taps = [blocks[:, :, depth, :, 0, :] + blocks[:, :, depth + 1, :, 1, :] for depth in range(3)]
    return jnp.stack(taps, axis=2).reshape(27, width, width)


def slab_list(padded, edge, width, pair_idx):
    count = padded.shape[0]
    slabs = []
    for x_pos in range(3):
        for y_pos in range(3):
            slab = padded[
                :,
                x_pos : x_pos + edge,
                y_pos : y_pos + edge,
                2 * pair_idx * width : (2 * pair_idx + 4) * width,
            ]
            slabs.append(slab.reshape(count * edge * edge, 4 * width))
    return slabs


def conv_forward(padded, pairs, edge, width):
    count = padded.shape[0]
    results = []
    for pair_idx in range(edge // 2):
        slabs = slab_list(padded, edge, width, pair_idx)
        summed = jnp.dot(slabs[0], pairs[0], preferred_element_type=jnp.float32)
        for tap_pair in range(1, 9):
            summed = summed + jnp.dot(
                slabs[tap_pair], pairs[tap_pair], preferred_element_type=jnp.float32
            )
        results.append(summed.reshape(count, edge, edge, 2 * width))
    return jnp.concatenate(results, axis=3)


def shift_sum(pieces, count, edge, width):
    block = None
    for x_pos in range(3):
        row = None
        for y_pos in range(3):
            piece = pieces[x_pos * 3 + y_pos].reshape(count, edge, edge, 4 * width)
            shifted = jnp.pad(piece, ((0, 0), (0, 0), (y_pos, 2 - y_pos), (0, 0)))
            row = shifted if row is None else row + shifted
        placed = jnp.pad(row, ((0, 0), (x_pos, 2 - x_pos), (0, 0), (0, 0)))
        block = placed if block is None else block + placed
    return block


def conv_backward(grad_out, padded, pairs, edge, width):
    count = padded.shape[0]
    pair_count = edge // 2
    blocks = []
    tap_sums = [None] * 9
    for pair_idx in range(pair_count):
        slabs = slab_list(padded, edge, width, pair_idx)
        upstream = grad_out[:, :, :, 2 * pair_idx * width : (2 * pair_idx + 2) * width].reshape(
            count * edge * edge, 2 * width
        )
        pieces = []
        for tap_pair in range(9):
            term = jnp.einsum(
                "rk,rn->kn", slabs[tap_pair], upstream, preferred_element_type=jnp.float32
            )
            tap_sums[tap_pair] = term if tap_sums[tap_pair] is None else tap_sums[tap_pair] + term
            pieces.append(jnp.dot(upstream, pairs[tap_pair].T, preferred_element_type=jnp.float32))
        blocks.append(shift_sum(pieces, count, edge, width))
    columns = []
    for column in range(pair_count + 1):
        part = None
        if column < pair_count:
            part = blocks[column][..., : 2 * width]
        if column > 0:
            later = blocks[column - 1][..., 2 * width :]
            part = later if part is None else part + later
        columns.append(part)
    grad_padded = jnp.concatenate(columns, axis=3)
    pair_grad = jnp.stack(tap_sums, axis=0)
    return (grad_padded, pair_grad)


def silu_grad(value):
    sig = jax.nn.sigmoid(value)
    return sig * (1.0 + value * (1.0 - sig))


def to_children(hidden, count, half, width):
    split = hidden.reshape(count, half, 2, half, 2, half, 2 * width)
    return split.transpose(0, 1, 3, 5, 2, 4, 6).reshape(count * half**3, 8 * width)


def from_children(grads, count, half, width):
    split = grads.reshape(count, half, half, half, 2, 2, 2 * width)
    return split.transpose(0, 1, 4, 2, 5, 3, 6).reshape(count, 2 * half, 2 * half, 2 * half * width)


def shards(features, masks, rulebook, send_lists, conv_weight, down_weight, cotangent):
    bricks = features[0]
    count = bricks.shape[0]
    edge = bricks.shape[1]
    width = bricks.shape[3] // edge
    half = edge // 2
    out_width = down_weight.shape[2]
    peers = lax.axis_size("spatial")
    slots = send_lists.shape[3]
    table = rulebook[0]
    chosen = send_lists[0, 0].reshape(peers * slots)
    voxels = masks[0].reshape(count, edge, edge, edge)
    keep = jnp.repeat(voxels, width, axis=3).astype(jnp.bfloat16)
    keep32 = keep.astype(jnp.float32)
    masked = bricks * keep
    zero_brick = jnp.zeros((1, edge, edge, edge * width), jnp.bfloat16)
    masked_ext = jnp.concatenate([masked, zero_brick], axis=0)
    outgoing = jnp.take(masked_ext, chosen, axis=0).reshape(peers, slots, edge, edge, edge * width)
    arrived = lax.all_to_all(outgoing, "spatial", split_axis=0, concat_axis=0, tiled=True)
    extended = jnp.concatenate(
        [masked, arrived.reshape(peers * slots, edge, edge, edge * width), zero_brick], axis=0
    )
    padded = assemble(extended, table, edge, width)
    pairs = pair_weights(conv_weight, width)
    pre_hidden = conv_forward(padded, pairs, edge, width) * keep32
    hidden = jax.nn.silu(pre_hidden).astype(jnp.bfloat16)
    children = to_children(hidden, count, half, width)
    flat_down = down_weight.reshape(8 * width, out_width)
    pre_out = jnp.dot(children, flat_down, preferred_element_type=jnp.float32)
    coarse = voxels.reshape(count, half, 2, half, 2, half, 2).max(axis=(2, 4, 6))
    coarse_keep = coarse.reshape(-1, 1).astype(jnp.float32)
    coarse_out = (
        (jax.nn.silu(pre_out) * coarse_keep)
        .astype(jnp.bfloat16)
        .reshape(count, half, half, half * out_width)
    )
    incoming = cotangent[0].reshape(count * half**3, out_width).astype(jnp.float32)
    grad_pre = (incoming * coarse_keep * silu_grad(pre_out)).astype(jnp.bfloat16)
    down_part = jnp.einsum("rk,rn->kn", children, grad_pre, preferred_element_type=jnp.float32)
    grad_children = jnp.dot(grad_pre, flat_down.T, preferred_element_type=jnp.float32)
    grad_hidden = from_children(grad_children, count, half, width)
    grad_pre_hidden = (grad_hidden * silu_grad(pre_hidden) * keep32).astype(jnp.bfloat16)
    grad_padded, pair_grad = conv_backward(grad_pre_hidden, padded, pairs, edge, width)
    conv_part = pair_to_taps(pair_grad, width)
    grad_ext = spread(grad_padded, table, edge, width, count + peers * slots + 1)
    returning = (
        grad_ext[count : count + peers * slots]
        .astype(jnp.bfloat16)
        .reshape(peers, slots, edge, edge, edge * width)
    )
    came_back = lax.all_to_all(returning, "spatial", split_axis=0, concat_axis=0, tiled=True)
    own_grads = jnp.concatenate(
        [grad_ext[:count], jnp.zeros((1, edge, edge, edge * width), jnp.float32)], axis=0
    )
    grad_local = own_grads.at[chosen].add(
        came_back.reshape(peers * slots, edge, edge, edge * width).astype(jnp.float32)
    )[:count]
    grad_features = (grad_local * keep32).astype(jnp.bfloat16)
    down_part = down_part.reshape(8, width, out_width)
    conv_sum, down_sum = lax.psum((conv_part, down_part), ("spatial", "dp"))
    scale = float(lax.axis_size("dp") * peers * count * edge**3) ** (-0.5)
    return (coarse_out[None], grad_features[None], conv_sum * scale, down_sum * scale)


def solution(mesh):
    placed = (
        P("dp", "spatial", None, None, None),
        P("dp", "spatial", None),
        P("dp", "spatial", None),
        P("dp", "spatial", None, None),
        P(),
        P(),
        P("dp", "spatial", None, None, None),
    )
    return jax.shard_map(
        shards,
        mesh=mesh,
        in_specs=placed,
        out_specs=(
            P("dp", "spatial", None, None, None),
            P("dp", "spatial", None, None, None),
            P(),
            P(),
        ),
        check_vma=False,
    )
```

profile of v0, /device:TPU:41, one launch (start us, length us, event | category | flops | bytes accessed | tf_op | source)
XLA Modules:
  0.0 919.9 jit_solution(14593449646879176346)
XLA Ops:
  12.5 6.3 gather_fusion
  18.8 7.4 broadcast_select_fusion
  26.4 12.3 %all-to-all-start = ((bf16[64,2,8,8,512]{4,3,2,1,0:T(8,128)(2,1)}), bf16[64,2,8,8,512]{4,3,2,1,0:T(8,128)(2,1)}, u32[]{:S(2)}, u32[]{:S(2)}) async-start(bf16[64,2,8,8,512]{4,3,2,1,0:T(8,128)(2,1)} %broadcast_select_fusion), calls=%async_computation | async-start | bytes 16777216 | tf_op jit(solution)/shard_map/all_to_all | solution.py:196
  44.9 2.2 copy.173
  47.1 2.8 reshape.680
  70.9 152.6 %all-to-all-done = bf16[64,2,8,8,512]{4,3,2,1,0:T(8,128)(2,1)} async-done(((bf16[64,2,8,8,512]{4,3,2,1,0:T(8,128)(2,1)}), bf16[64,2,8,8,512]{4,3,2,1,0:T(8,128)(2,1)}, u32[]{:S(2)}, u32[]{:S(2)}) %all-to-all-start) | async-done | bytes 8388640 | tf_op jit(solution)/shard_map/all_to_all | solution.py:196
  223.4 11.4 %copy.241 = bf16[128,8,8,512]{3,0,2,1:T(8,128)(2,1)} copy(bf16[128,8,8,512]{3,2,1,0:T(8,128)(2,1)} %bitcast.4) | data formatting | bytes 16777216 | tf_op jit(solution)/shard_map/reshape | solution.py:198
  234.9 11.7 %maximum_maximum_fusion = bf16[135,8,8,512]{3,0,2,1:T(8,128)(2,1)} fusion(bf16[128,8,8,512]{3,0,2,1:T(8,128)(2,1)} %copy.241, bf16[6,8,8,512]{3,0,2,1:T(8,128)(2,1)S(1)} %copy-done.10, bf16[135]{0:T(256)(128)(2,1)S(1)} %pad.265.clone), kind=kLoop, calls=%fused_computation.33 | loop fusion | flops 26542080 | bytes 17629454 | tf_op jit(solution)/shard_map/concatenate | solution.py:197
  246.6 1.6 slice_bitcast_fusion.21
  248.2 2.0 slice_bitcast_fusion.15
  250.2 3.1 slice_bitcast_fusion.9
  253.3 2.4 slice_bitcast_fusion.5
  255.8 3.2 slice_bitcast_fusion
  258.9 12.1 %slice_bitcast_fusion.2 = (bf16[135,8,512]{2,0,1:T(8,128)(2,1)}, bf16[135,8,512]{2,0,1:T(8,128)(2,1)}) fusion(bf16[135,8,8,512]{3,0,2,1:T(8,128)(2,1)S(1)} %copy-done.2), kind=kLoop, calls=%fused_computation.156 | loop fusion | bytes 4423680 | tf_op jit(solution)/shard_map/jit(_take)/Arg_0.17 | solution.py:35
  271.1 2.4 fusion.344
  273.4 10.1 %copy.165 = bf16[135,8,8,512]{3,2,1,0:T(8,128)(2,1)} copy(bf16[135,8,8,512]{3,0,2,1:T(8,128)(2,1)} %maximum_maximum_fusion) | data formatting | bytes 17694720 | tf_op jit(solution)/shard_map/concatenate | solution.py:197
  283.6 1.9 copy.158
  285.4 1.7 copy.171
  287.1 1.7 copy.167
  288.8 1.7 copy.162
  293.2 1.9 copy.164
  295.2 2.0 copy.166
  297.2 1.5 gather_fusion.11
  298.8 1.5 gather_fusion.18
  300.4 1.5 gather_fusion.16
  302.7 1.5 gather_fusion.13
  305.0 1.9 gather_fusion.12
  307.8 1.9 gather_fusion.17
  310.5 4.2 gather_fusion.1
  315.5 2.3 gather_fusion.14
  317.9 2.3 gather_fusion.15
  321.7 1.6 maximum_maximum_fusion.7
  323.3 1.9 fusion.55
  335.3 1.5 gather_fusion.10
  337.1 1.6 gather_fusion.9
  339.7 1.6 gather_fusion.7
  341.4 1.6 gather_fusion.5
  343.1 1.9 gather_fusion.6
  345.2 2.2 maximum_maximum_fusion.1
  355.3 1.5 gather_fusion.19
  356.7 1.5 gather_fusion.27
  358.5 1.6 gather_fusion.20
  360.2 1.6 gather_fusion.26
  361.9 1.6 gather_fusion.22
  363.7 1.6 gather_fusion.24
  365.4 1.9 gather_fusion.23
  367.4 3.5 maximum_maximum_fusion.2
  380.4 2.3 concatenate.135
  382.7 1.8 fusion.54
  386.8 2.0 multiply_convert_fusion
  390.5 2.3 reshape.722
  392.8 1.6 fusion.47
  416.3 2.6 reshape.736
  418.9 42.7 %concatenate.138 = f32[6,1000,64]{2,1,0:T(8,128)} concatenate(f32[6,1,64]{2,1,0:T(1,128)} %get-tuple-element.105, f32[6,8,64]{2,1,0:T(8,128)S(1)} %copy-done.64, f32[6,1,64]{2,1,0:T(1,128)S(1)} %get-tuple-element.101, f32[6,8,64]{2,1,0:T(8,128)} %get-tuple-element.109, f32[6,64,64]{2,1,0:T(8,128)} %reshape.727, f32[6,8,64]{2,1,0:T(8,128)S(1)} %get-tuple-element.107, ...), dimensions={1} | concatenate | bytes 3072000 | tf_op jit(solution)/shard_map/concatenate | solution.py:69
  461.6 47.5 %scatter_custom_fusion = f32[69120,64]{1,0:T(8,128)} fusion(s32[6000]{0:T(1024)} %reshape.1053, f32[6000,64]{1,0:T(8,128)} %bitcast.733, f32[]{:T(128)} %constant.124.clone.1), kind=kCustom, calls=%fused_computation.31 | custom fusion | flops 384000 | bytes 17695232 | tf_op jit(solution)/shard_map/scatter-add | solution.py:71
  509.1 17.3 %slice.1511 = bf16[65536,64]{1,0:T(8,128)(2,1)} slice(f32[69120,64]{1,0:T(8,128)} %scatter_custom_fusion), slice={[3072:68608], [0:64]} | slice | bytes 16777216 | tf_op jit(solution)/shard_map/slice | solution.py:224
  526.4 22.4 %convert_element_type.137 = bf16[64,2,8,8,512]{4,3,2,1,0:T(8,128)(2,1)} reshape(bf16[65536,64]{1,0:T(8,128)(2,1)} %slice.1511) | data formatting | bytes 16777216 | tf_op jit(solution)/shard_map/convert_element_type | solution.py:225
  548.9 7.3 all-to-all-start.1
  575.1 2.9 reshape.751
  583.6 288.7 %all-reduce.55.cloned.1.call-done = (f32[27,64,64]{2,1,0:T(8,128)}, f32[8,64,128]{2,1,0:T(8,128)}) async-done(((f32[27,64,64]{2,1,0:T(8,128)}, f32[8,64,128]{2,1,0:T(8,128)}), (f32[27,64,64]{2,1,0:T(8,128)}, f32[8,64,128]{2,1,0:T(8,128)})) %all-reduce.55.cloned.1.call-update) | async-done | bytes 704528 | tf_op jit(solution)/shard_map/psum | solution.py:237
  872.3 1.7 broadcast_multiply_fusion.1
  874.0 2.2 broadcast_multiply_fusion
  876.2 11.6 %bitcast_convert_fusion = f32[128,8,8,512]{3,2,1,0:T(8,128)} fusion(bf16[64,2,8,8,512]{4,3,2,1,0:T(8,128)(2,1)} %all-to-all-done.1), kind=kLoop, calls=%fused_computation.34 | loop fusion | flops 4194304 | bytes 25165824 | tf_op jit(solution)/shard_map/convert_element_type | solution.py:233
  887.8 24.0 %scatter_fusion = f32[7,8,8,512]{3,2,1,0:T(8,128)S(1)} fusion(f32[7,8,8,512]{3,2,1,0:T(8,128)S(1)} %concatenate.139, s32[128]{0:T(128)S(1)} %copy-done.69, f32[128,8,8,512]{3,2,1,0:T(8,128)} %bitcast_convert_fusion), kind=kCustom, calls=%fused_computation.29 | custom fusion | flops 4194304 | bytes 50332160 | tf_op jit(solution)/shard_map/scatter-add | solution.py:232
  (518 shorter events, 120.4 us)
Async XLA Ops:
  7.2 379.7 %copy-start = (bf16[8,64,128]{2,1,0:T(8,128)(2,1)S(1)}, bf16[8,64,128]{2,1,0:T(8,128)(2,1)}, u32[]{:S(2)}) copy-start(bf16[8,64,128]{2,1,0:T(8,128)(2,1)} %param.53) | copy-start | bytes 393220
  7.2 5.2 copy-start.60
  26.2 12.5 %copy-start.67 = (s32[1,6,512]{2,0,1:T(1,128)S(1)}, s32[1,6,512]{2,0,1:T(1,128)}, u32[]{:S(2)}) copy-start(s32[1,6,512]{2,0,1:T(1,128)} %param.49) | copy-start | bytes 36868
  26.2 14.8 %copy-start.103 = (s32[64]{0:T(128)S(1)}, s32[64]{0:T(128)}, u32[]{:S(2)}) copy-start(s32[64]{0:T(128)} %constant.196.clone) | copy-start | bytes 772
  26.2 14.9 %copy-start.102 = (s32[64]{0:T(128)S(1)}, s32[64]{0:T(128)}, u32[]{:S(2)}) copy-start(s32[64]{0:T(128)} %constant.193.clone) | copy-start | bytes 772
  26.2 14.9 %copy-start.101 = (s32[8]{0:T(128)S(1)}, s32[8]{0:T(128)}, u32[]{:S(2)}) copy-start(s32[8]{0:T(128)} %constant.195.clone) | copy-start | bytes 100
  26.2 15.0 %copy-start.99 = (s32[8]{0:T(128)S(1)}, s32[8]{0:T(128)}, u32[]{:S(2)}) copy-start(s32[8]{0:T(128)} %constant.136.clone) | copy-start | bytes 100
  26.2 15.0 %copy-start.100 = (s32[8]{0:T(128)S(1)}, s32[8]{0:T(128)}, u32[]{:S(2)}) copy-start(s32[8]{0:T(128)} %constant.128.clone) | copy-start | bytes 100
  26.3 15.1 %copy-start.97 = (s32[64]{0:T(128)S(1)}, s32[64]{0:T(128)}, u32[]{:S(2)}) copy-start(s32[64]{0:T(128)} %constant.150.clone) | copy-start | bytes 772
  26.3 15.0 %copy-start.98 = (s32[64]{0:T(128)S(1)}, s32[64]{0:T(128)}, u32[]{:S(2)}) copy-start(s32[64]{0:T(128)} %constant.137.clone) | copy-start | bytes 772
  26.3 15.1 %copy-start.95 = (s32[8]{0:T(128)S(1)}, s32[8]{0:T(128)}, u32[]{:S(2)}) copy-start(s32[8]{0:T(128)} %constant.140.clone) | copy-start | bytes 100
  26.3 15.1 %copy-start.96 = (s32[8]{0:T(128)S(1)}, s32[8]{0:T(128)}, u32[]{:S(2)}) copy-start(s32[8]{0:T(128)} %constant.138.clone) | copy-start | bytes 100
  26.3 15.2 %copy-start.93 = (s32[8]{0:T(128)S(1)}, s32[8]{0:T(128)}, u32[]{:S(2)}) copy-start(s32[8]{0:T(128)} %constant.192.clone) | copy-start | bytes 100
  26.3 15.2 %copy-start.94 = (s32[8]{0:T(128)S(1)}, s32[8]{0:T(128)}, u32[]{:S(2)}) copy-start(s32[8]{0:T(128)} %constant.148.clone) | copy-start | bytes 100
  26.3 15.2 %copy-start.91 = (s32[8]{0:T(128)S(1)}, s32[8]{0:T(128)}, u32[]{:S(2)}) copy-start(s32[8]{0:T(128)} %constant.201.clone) | copy-start | bytes 100
  26.3 15.2 %copy-start.92 = (s32[8]{0:T(128)S(1)}, s32[8]{0:T(128)}, u32[]{:S(2)}) copy-start(s32[8]{0:T(128)} %constant.199.clone) | copy-start | bytes 100
  26.4 16.2 %copy-start.66 = (bf16[1,6,4,4,512]{4,3,2,1,0:T(4,128)(2,1)S(1)}, bf16[1,6,4,4,512]{4,3,2,1,0:T(4,128)(2,1)}, u32[]{:S(2)}) copy-start(bf16[1,6,4,4,512]{4,3,2,1,0:T(4,128)(2,1)} %param.54) | copy-start | bytes 294916
  26.4 197.0 %all-to-all-start = ((bf16[64,2,8,8,512]{4,3,2,1,0:T(8,128)(2,1)}), bf16[64,2,8,8,512]{4,3,2,1,0:T(8,128)(2,1)}, u32[]{:S(2)}, u32[]{:S(2)}) async-start(bf16[64,2,8,8,512]{4,3,2,1,0:T(8,128)(2,1)} %broadcast_select_fusion), calls=%async_computation | async-start | bytes 16777216 | tf_op jit(solution)/shard_map/all_to_all | solution.py:196
  38.7 5.7 copy-start.59
  223.4 11.4 %copy-start.10 = (bf16[6,8,8,512]{3,0,2,1:T(8,128)(2,1)S(1)}, bf16[6,8,8,512]{3,0,2,1:T(8,128)(2,1)}, u32[]{:S(2)}) copy-start(bf16[6,8,8,512]{3,0,2,1:T(8,128)(2,1)} %copy.148) | copy-start | bytes 1179652
  248.2 10.7 %copy-start.2 = (bf16[135,8,8,512]{3,0,2,1:T(8,128)(2,1)S(1)}, bf16[135,8,8,512]{3,0,2,1:T(8,128)(2,1)}, u32[]{:S(2)}) copy-start(bf16[135,8,8,512]{3,0,2,1:T(8,128)(2,1)} %maximum_maximum_fusion) | copy-start | bytes 26542084
  283.6 7.0 copy-start.9
  283.6 8.3 copy-start.8
  297.2 20.6 %copy-start.73 = (pred[6]{0:T(512)(128)(4,1)S(1)}, pred[6]{0:T(512)(128)(4,1)}, u32[]{:S(2)}) copy-start(pred[6]{0:T(512)(128)(4,1)} %get-tuple-element.201) | copy-start | bytes 22
  297.2 23.1 %copy-start.72 = (pred[6]{0:T(512)(128)(4,1)S(1)}, pred[6]{0:T(512)(128)(4,1)}, u32[]{:S(2)}) copy-start(pred[6]{0:T(512)(128)(4,1)} %get-tuple-element.200) | copy-start | bytes 22
  300.4 44.7 %copy-start.53 = (bf16[6,8,1,64]{3,2,1,0:T(2,128)(2,1)}, bf16[6,8,1,64]{3,2,1,0:T(2,128)(2,1)S(1)}, u32[]{:S(2)}) copy-start(bf16[6,8,1,64]{3,2,1,0:T(2,128)(2,1)S(1)} %broadcast_select_fusion.6) | copy-start | bytes 18436
  302.7 42.5 %copy-start.55 = (bf16[6,8,1,64]{3,2,1,0:T(2,128)(2,1)}, bf16[6,8,1,64]{3,2,1,0:T(2,128)(2,1)S(1)}, u32[]{:S(2)}) copy-start(bf16[6,8,1,64]{3,2,1,0:T(2,128)(2,1)S(1)} %broadcast_select_fusion.7) | copy-start | bytes 18436
  305.0 40.2 %copy-start.57 = (bf16[6,8,1,64]{3,2,1,0:T(2,128)(2,1)}, bf16[6,8,1,64]{3,2,1,0:T(2,128)(2,1)S(1)}, u32[]{:S(2)}) copy-start(bf16[6,8,1,64]{3,2,1,0:T(2,128)(2,1)S(1)} %broadcast_select_fusion.8) | copy-start | bytes 18436
  321.7 4.3 copy-start.18
  321.7 5.0 copy-start.17
  323.3 4.2 copy-start.16
  323.3 5.0 copy-start.7
  325.2 4.4 copy-start.6
  328.2 8.6 copy-start.84
  328.2 8.6 copy-start.86
  328.2 8.7 copy-start.83
  328.3 8.8 copy-start.85
  328.3 10.5 %copy-start.90 = (pred[6]{0:T(512)(128)(4,1)S(1)}, pred[6]{0:T(512)(128)(4,1)}, u32[]{:S(2)}) copy-start(pred[6]{0:T(512)(128)(4,1)} %get-tuple-element.234) | copy-start | bytes 22
  328.3 11.3 %copy-start.89 = (pred[6]{0:T(512)(128)(4,1)S(1)}, pred[6]{0:T(512)(128)(4,1)}, u32[]{:S(2)}) copy-start(pred[6]{0:T(512)(128)(4,1)} %get-tuple-element.240) | copy-start | bytes 22
  328.3 13.0 %copy-start.78 = (pred[6]{0:T(512)(128)(4,1)S(1)}, pred[6]{0:T(512)(128)(4,1)}, u32[]{:S(2)}) copy-start(pred[6]{0:T(512)(128)(4,1)} %get-tuple-element.236) | copy-start | bytes 22
  328.3 14.7 %copy-start.77 = (pred[6]{0:T(512)(128)(4,1)S(1)}, pred[6]{0:T(512)(128)(4,1)}, u32[]{:S(2)}) copy-start(pred[6]{0:T(512)(128)(4,1)} %get-tuple-element.238) | copy-start | bytes 22
  328.3 16.7 %copy-start.71 = (pred[6]{0:T(512)(128)(4,1)S(1)}, pred[6]{0:T(512)(128)(4,1)}, u32[]{:S(2)}) copy-start(pred[6]{0:T(512)(128)(4,1)} %get-tuple-element.237) | copy-start | bytes 22
  347.3 10.8 %copy-start.82 = (pred[6]{0:T(512)(128)(4,1)S(1)}, pred[6]{0:T(512)(128)(4,1)}, u32[]{:S(2)}) copy-start(pred[6]{0:T(512)(128)(4,1)} %get-tuple-element.196) | copy-start | bytes 22
  347.3 10.9 %copy-start.79 = (pred[6]{0:T(512)(128)(4,1)S(1)}, pred[6]{0:T(512)(128)(4,1)}, u32[]{:S(2)}) copy-start(pred[6]{0:T(512)(128)(4,1)} %get-tuple-element.188) | copy-start | bytes 22
  347.3 11.0 %copy-start.80 = (pred[6]{0:T(512)(128)(4,1)S(1)}, pred[6]{0:T(512)(128)(4,1)}, u32[]{:S(2)}) copy-start(pred[6]{0:T(512)(128)(4,1)} %get-tuple-element.190) | copy-start | bytes 22
  347.3 11.1 %copy-start.81 = (pred[6]{0:T(512)(128)(4,1)S(1)}, pred[6]{0:T(512)(128)(4,1)}, u32[]{:S(2)}) copy-start(pred[6]{0:T(512)(128)(4,1)} %get-tuple-element.194) | copy-start | bytes 22
  347.4 12.8 %copy-start.88 = (pred[6]{0:T(512)(128)(4,1)S(1)}, pred[6]{0:T(512)(128)(4,1)}, u32[]{:S(2)}) copy-start(pred[6]{0:T(512)(128)(4,1)} %get-tuple-element.195) | copy-start | bytes 22
  347.4 14.5 %copy-start.87 = (pred[6]{0:T(512)(128)(4,1)S(1)}, pred[6]{0:T(512)(128)(4,1)}, u32[]{:S(2)}) copy-start(pred[6]{0:T(512)(128)(4,1)} %get-tuple-element.189) | copy-start | bytes 22
  347.4 16.2 %copy-start.76 = (pred[6]{0:T(512)(128)(4,1)S(1)}, pred[6]{0:T(512)(128)(4,1)}, u32[]{:S(2)}) copy-start(pred[6]{0:T(512)(128)(4,1)} %get-tuple-element.193) | copy-start | bytes 22
  348.7 16.6 %copy-start.75 = (pred[6]{0:T(512)(128)(4,1)S(1)}, pred[6]{0:T(512)(128)(4,1)}, u32[]{:S(2)}) copy-start(pred[6]{0:T(512)(128)(4,1)} %get-tuple-element.191) | copy-start | bytes 22
  348.7 18.6 %copy-start.70 = (pred[6]{0:T(512)(128)(4,1)S(1)}, pred[6]{0:T(512)(128)(4,1)}, u32[]{:S(2)}) copy-start(pred[6]{0:T(512)(128)(4,1)} %get-tuple-element.192) | copy-start | bytes 22
  348.7 18.7 %copy-start.54 = (bf16[6,8,1,64]{3,2,1,0:T(2,128)(2,1)S(1)}, bf16[6,8,1,64]{3,2,1,0:T(2,128)(2,1)}, u32[]{:S(2)}) copy-start(bf16[6,8,1,64]{3,2,1,0:T(2,128)(2,1)} %copy-done.53) | copy-start | bytes 18436
  348.7 18.7 %copy-start.56 = (bf16[6,8,1,64]{3,2,1,0:T(2,128)(2,1)S(1)}, bf16[6,8,1,64]{3,2,1,0:T(2,128)(2,1)}, u32[]{:S(2)}) copy-start(bf16[6,8,1,64]{3,2,1,0:T(2,128)(2,1)} %copy-done.55) | copy-start | bytes 18436
  348.7 18.7 %copy-start.58 = (bf16[6,8,1,64]{3,2,1,0:T(2,128)(2,1)S(1)}, bf16[6,8,1,64]{3,2,1,0:T(2,128)(2,1)}, u32[]{:S(2)}) copy-start(bf16[6,8,1,64]{3,2,1,0:T(2,128)(2,1)} %copy-done.57) | copy-start | bytes 18436
  379.2 5.3 copy-start.11
  379.5 5.0 copy-start.12
  380.4 6.4 copy-start.74
  386.8 3.7 copy-start.13
  548.9 7.3 copy-start.14
  548.9 8.3 copy-start.50
  548.9 327.3 %all-to-all-start.1 = ((bf16[64,2,8,8,512]{4,3,2,1,0:T(8,128)(2,1)}), bf16[64,2,8,8,512]{4,3,2,1,0:T(8,128)(2,1)}, u32[]{:S(2)}, u32[]{:S(2)}) async-start(bf16[64,2,8,8,512]{4,3,2,1,0:T(8,128)(2,1)} %convert_element_type.137), calls=%async_computation.1 | async-start | bytes 16777216 | tf_op jit(solution)/shard_map/all_to_all | solution.py:228
  556.2 316.1 %all-reduce.55.cloned.1.call-start = ((), (), s32[]{:S(2)}) async-start(), calls=%async_computation.2 | async-start | bytes 2293760 | tf_op jit(solution)/shard_map/psum | solution.py:237
  876.2 11.6 %copy-start.69 = (s32[128]{0:T(128)S(1)}, s32[128]{0:T(128)}, u32[]{:S(2)}) copy-start(s32[128]{0:T(128)} %copy-done.68) | copy-start | bytes 1540
  887.8 24.9 %copy-start.1 = (bf16[8,64,128]{2,1,0:T(8,128)(2,1)S(1)}, bf16[8,64,128]{2,1,0:T(8,128)(2,1)}, u32[]{:S(2)}) copy-start(bf16[8,64,128]{2,1,0:T(8,128)(2,1)} %param.53) | copy-start | bytes 393220
  (44 other events, 70.4 us)
Sparse Core Ops, SparseCore 0:
  581.7 290.5 all-reduce.54
where the time goes:
time: 936 us; the launch traced here: 920 us
  waiting for transfers between devices  441 us (47%)
  local copies, waits for them, and re-layouts  246 us (26%)
  other arithmetic  159 us (17%)
  matrix products  37.2 us (4%)
  starting transfers between devices  19.6 us (2%)
  between operations  16.5 us (2%)
    psum x1, waiting for transfers between devices, shards(): conv_sum, down_sum = lax.psum((conv_part, down_part), ('spatial', 'dp'))  289 us
    all_to_all x1, waiting for transfers between devices, shards(): lax.all_to_all(outgoing, 'spatial', split_axis=0, concat_axis=0, tiled=True)  153 us
    scatter-add x1, other arithmetic, spread(): jax.ops.segment_sum(data_all, target_all, num_segments=total_count * edge...  47.5 us
    gather x27, local copies, waits for them, and re-layouts, assemble(): cols.append(jnp.take(part, table[:, x_pos * 9 + y_pos * 3 + z_pos], axis=0))  46.3 us
    concatenate x1, local copies, waits for them, and re-layouts, spread(): data_all = jnp.concatenate(datas, axis=1).reshape(-1, width)  42.7 us
    another operation x18, local copies, waits for them, and re-layouts, assemble(): cols.append(jnp.take(part, table[:, x_pos * 9 + y_pos * 3 + z_pos], axis=0))  39.8 us
    scatter-add x1, other arithmetic, shards(): own_grads.at[chosen]  24 us
    convert_element_type x1, local copies, waits for them, and re-layouts, shards(): returning = grad_ext[count:count + peers * slots].astype(jnp.bfloat16).re...  22.4 us
  transfers between devices with their start and end apart: 3, of which 2 were waited for; matrix products, arithmetic and copies ran while one was open for 7% of the time, Pallas kernels for 0%

commit v1 on v0

v1 whole, which is shorter than its diff:
```python
import jax
import jax.numpy as jnp
import numpy as np
from jax import lax
from jax.experimental import pallas as pl
from jax.experimental.pallas import tpu as pltpu
from jax.sharding import PartitionSpec as P

F32, BF16 = jnp.float32, jnp.bfloat16
BD = 6
EDGE = 8
HALF = 4
ROWS = EDGE * EDGE
LANES = 512
SHELL = 176
PADR = 112
PADL = 640
EXT = 61
EMPTY = 60
SIDE = 4
GROUP = 9 * 128
VMEM = 58 * 2**20

X_LO, X_HI, Y_LO, Y_HI, Z_AT = 0, 32, 64, 96, 128

PLANE = [(a, b) for a in (-1, 0, 1) for b in (-1, 0, 1) if (a, b) != (0, 0)]


def slots_of(a, b, c):
    return 2 if abs(a) + abs(b) + abs(c) == 1 else 1


def plane_items(a, b):
    own = [(a, b, 0, s) for s in range(slots_of(a, b, 0))]
    return own + [(a, b, -1, 0), (a, b, 1, 0)]


def place(a, b, c):
    return 9 * (a + 1) + 3 * (b + 1) + c + 1


def region(d):
    q = d // 16
    return (q % 2) * 2 + q // 2, (d // 4) % 4, d % 4


def shift_pairs(count, a, b, c):
    where = {region(d): d for d in range(count)}
    pairs = []
    for d in range(count):
        r = region(d)
        to = (r[0] + a, r[1] + b, r[2] + c)
        if to in where:
            pairs.append((d, where[to]))
    return pairs


def pad_row(x, y):
    if 1 <= y <= 8:
        return x * 8 + y - 1
    base = 80 if y == 0 else 96
    return base + (x - 1 if 1 <= x <= 8 else (8 if x == 0 else 9))


def selections():
    sel = np.zeros((9, 4, 16, PADR), np.float32)
    for dx in range(3):
        for dy in range(3):
            for ox in range(2):
                for oy in range(2):
                    for hx in range(4):
                        for hy in range(4):
                            row = pad_row(2 * hx + ox + dx, 2 * hy + oy + dy)
                            sel[dx * 3 + dy, ox * 2 + oy, hx * 4 + hy, row] = 1
    sel = sel.reshape(9, ROWS, PADR)
    return sel.reshape(9 * ROWS, PADR), sel.transpose(0, 2, 1).reshape(9 * PADR, ROWS)


def dot(a, b, ca=1, cb=0):
    return lax.dot_general(a, b, (((ca,), (cb,)), ((), ())), preferred_element_type=F32)


def iota(shape, dim):
    return lax.broadcasted_iota(jnp.int32, shape, dim)


def spread_mask(voxels, width):
    hit = iota((8, LANES), 1) // width == iota((8, LANES), 0) // (width // 64)
    return dot(voxels, hit.astype(F32).astype(BF16))


def low_half(shape):
    return iota(shape, len(shape) - 1) < 64


def row_is(row):
    return iota((8, 128), 0) == row


def choice(me_ref, send_ref, a, b, c, s):
    me = me_ref[0]
    q = me // 16
    r0, r1, r2 = (q % 2) * 2 + q // 2 + a, (me // 4) % 4 + b, me % 4 + c
    inside = (r0 >= 0) & (r0 < SIDE) & (r1 >= 0) & (r1 < SIDE) & (r2 >= 0) & (r2 < SIDE)
    to = ((r0 % 2) * 2 + r0 // 2) * 16 + r1 * 4 + r2
    to = jnp.where(inside, to, 0)
    got = send_ref[to * 2 + s]
    return jnp.clip(jnp.where(inside, got, BD), 0, BD)


def all_items():
    lists = [plane_items(a, b) for a, b in PLANE]
    lists += [[(0, 0, -1, s) for s in range(2)], [(0, 0, 1, s) for s in range(2)]]
    return lists


def pack_kernel(me_ref, send_ref, feat_ref, vox_ref, masked_ref, own_ref, *rest):
    outs, held = rest[:10], rest[10]
    pick = iota((16, ROWS), 1) == (iota((16, ROWS), 0) % 8) * 8 + (iota((16, ROWS), 0) // 8) * 7
    pick = pick.astype(F32).astype(BF16)
    for b in range(BD):
        keep = spread_mask(vox_ref[b * ROWS : (b + 1) * ROWS, :], 64)
        m = feat_ref[b].astype(F32) * keep
        mb = m.astype(BF16)
        masked_ref[b] = mb
        ys = dot(pick, mb)
        tiles = []
        for block in (m[0:8], m[56:64], ys[0:8], ys[8:16]):
            tiles += [block[:, 128 * q : 128 * (q + 1)] for q in range(4)]
        both = jnp.where(low_half((ROWS, 128)), m[:, 0:128], m[:, 384:512])
        tiles.append(both[8:56])
        shell = jnp.concatenate(tiles, axis=0).astype(BF16)
        own_ref[b] = shell
        held[b] = shell
    held[BD] = jnp.zeros((SHELL, 128), BF16)
    for out, items in zip(outs, all_items()):
        for k, item in enumerate(items):
            out[k] = held[choice(me_ref, send_ref, *item)]


def brick_blocks():
    groups = []
    for x, y in ((0, 1), (2, 1), (1, 0), (1, 2)):
        if y == 1:
            first, at = (0, X_HI) if x == 0 else (72, X_LO)
        else:
            first, at = (80, Y_HI) if y == 0 else (96, Y_LO)
        groups.append((first, 9 * x + 3 * y, at))
    return groups


def silu_slope(value, sig):
    return sig * (1.0 + value * (1.0 - sig))


def main_kernel(
    idx_ref, own_ref, masked_ref, voxp_ref, cot_ref, sel_ref, selt_ref, wf_ref, wb_ref, down_ref, *rest
):
    recv = rest[:10]
    coarse_ref, center_ref, gown_ref, sums_ref = rest[10:14]
    outs = rest[14:24]
    ext, gext, pad, cols, slope, kids, grads, gcols, gpad = rest[24:]
    low8 = low_half((8, 128))

    for b in range(BD):
        ext[b] = own_ref[b].astype(F32)
    ext[EMPTY] = jnp.zeros((SHELL, 128), F32)
    for (a, b), ref in zip(PLANE, recv):
        for s in range(slots_of(a, b, 0)):
            ext[BD + 2 * place(-a, -b, 0) + s] = ref[s].astype(F32)
    for c, ref in zip((-1, 1), recv[8:]):
        for s in range(2):
            ext[BD + 2 * place(0, 0, -c) + s] = ref[s].astype(F32)
        for k, (a, b) in enumerate(PLANE):
            ext[BD + 2 * place(-a, -b, -c)] = ref[2 + k].astype(F32)
    gext[...] = jnp.zeros_like(gext)

    @pl.loop(0, BD)
    def _(b):
        base = b * 27

        def src(t, row, size):
            return ext[idx_ref[base + t], row : row + size, :]

        for first, t, at in brick_blocks():
            for q in range(4):
                pad[first : first + 8, 128 * q : 128 * (q + 1)] = src(t + 1, at + 8 * q, 8)
            pad[first : first + 8, 512:640] = jnp.where(low8, src(t + 2, at, 8), src(t, at + 24, 8))
        pad[8:72, 0:512] = masked_ref[b].astype(F32)
        for x in range(8):
            hi_at, lo_at = (X_LO, X_LO + 24) if x == 0 else (X_HI, X_HI + 24) if x == 7 else (Z_AT + 8 * x - 8,) * 2
            pad[8 + 8 * x : 16 + 8 * x, 512:640] = jnp.where(low8, src(14, hi_at, 8), src(12, lo_at, 8))
        for y in (0, 2):
            first = 88 if y == 0 else 104
            row = 7 if y == 0 else 0
            for q in range(5):
                lines = []
                for x in (0, 2):
                    t = 9 * x + 3 * y
                    at = (X_HI if x == 0 else X_LO) + row
                    if q < 4:
                        line = src(t + 1, at + 8 * q, 1)
                    else:
                        line = jnp.where(low_half((1, 128)), src(t + 2, at, 1), src(t, at + 24, 1))
                    lines.append(jnp.broadcast_to(line, (8, 128)))
                pad[first : first + 8, 128 * q : 128 * (q + 1)] = jnp.where(
                    row_is(0), lines[0], jnp.where(row_is(1), lines[1], 0.0)
                )
        turned = pltpu.roll(pad[...], 64, 1).astype(BF16)
        picked = dot(sel_ref[...], turned).astype(BF16)
        for t in range(9):
            for q in range(4):
                rows = picked[t * 64 + q * 16 : t * 64 + q * 16 + 16]
                to = pl.ds(pl.multiple_of(q * 96 + b * 16, 16), 16)
                for k in range(5):
                    cols[to, k * GROUP + t * 128 : k * GROUP + (t + 1) * 128] = rows[:, k * 128 : (k + 1) * 128]

    voxp = voxp_ref[...]
    keep = spread_mask(voxp, 64)
    for p in range(4):
        pre = dot(cols[:, GROUP * p : GROUP * (p + 2)], wf_ref[...])
        kept = keep[:, 128 * p : 128 * (p + 1)]
        pre = pre * kept
        sig = jax.nn.sigmoid(pre)
        slope[:, 128 * p : 128 * (p + 1)] = silu_slope(pre, sig) * kept
        hidden = (pre * sig).astype(BF16)
        for q in range(4):
            kids[p * 96 : (p + 1) * 96, q * 128 : (q + 1) * 128] = hidden[q * 96 : (q + 1) * 96]
    v32 = voxp.astype(F32)
    number = v32[0:96] + v32[96:192] + v32[192:288] + v32[288:384]
    active = (spread_mask(number.astype(BF16), 128) > 0.5).astype(F32)
    pre_out = dot(kids[...], down_ref[...])
    sig = jax.nn.sigmoid(pre_out)
    value = pre_out * sig
    bend = silu_slope(pre_out, sig)
    pieces, parts = [], []
    for p in range(4):
        rows, lanes = slice(96 * p, 96 * (p + 1)), slice(128 * p, 128 * (p + 1))
        pieces.append((value[rows] * active[:, lanes]).astype(BF16))
        parts.append((cot_ref[:, lanes].astype(F32) * active[:, lanes] * bend[rows]).astype(BF16))
    coarse_ref[...] = jnp.concatenate(pieces, axis=1)
    grad_pre = jnp.concatenate(parts, axis=0)

    back = dot(grad_pre, down_ref[...], 1, 1)
    for p in range(4):
        for q in range(4):
            rows, lanes = slice(96 * q, 96 * (q + 1)), slice(128 * p, 128 * (p + 1))
            part = back[96 * p : 96 * (p + 1), 128 * q : 128 * (q + 1)]
            grads[rows, lanes] = (part * slope[rows, lanes]).astype(BF16)

    down_sum = dot(grad_pre, kids[...], 0, 0)
    for q in range(4):
        sums_ref[896 + 128 * q : 1024 + 128 * q, :] = down_sum[:, 128 * q : 128 * (q + 1)]
    total = None
    for p in range(4):
        term = dot(grads[:, 128 * p : 128 * (p + 1)], cols[:, GROUP * p : GROUP * (p + 2)], 0, 0)
        total = term if total is None else total + term
    third = []
    low64 = low_half((64, 128))
    for t in range(9):
        first = total[:, t * 128 : (t + 1) * 128]
        later = total[:, GROUP + t * 128 : GROUP + (t + 1) * 128]
        mixed = pltpu.roll(jnp.where(low64, later[64:], first[64:]), 64, 1)
        sums_ref[64 * t : 64 * (t + 1), :] = first[:64] + mixed
        third.append(later[:64] + pltpu.roll(later[64:], 64, 1))
    third.append(jnp.zeros((64, 128), F32))
    for m in range(5):
        sums_ref[576 + 64 * m : 640 + 64 * m, :] = jnp.where(
            low64, third[2 * m], pltpu.roll(third[2 * m + 1], 64, 1)
        )

    @pl.loop(0, BD)
    def _(b):
        mine = jnp.concatenate(
            [grads[pl.ds(pl.multiple_of(q * 96 + b * 16, 16), 16), :] for q in range(4)], axis=0
        )
        placed = dot(selt_ref[...], mine).astype(BF16)
        to = pl.ds(pl.multiple_of(b * PADR, 16), PADR)
        for t in range(9):
            for k in range(4):
                gcols[to, k * GROUP + t * 128 : k * GROUP + (t + 1) * 128] = placed[
                    t * PADR : (t + 1) * PADR, k * 128 : (k + 1) * 128
                ]

    for j in range(5):
        lo, hi = max(j - 1, 0), min(j + 1, 4)
        w_lo = GROUP if j == 0 else 0
        w_hi = GROUP if j == 4 else 2 * GROUP
        gpad[:, 128 * j : 128 * (j + 1)] = dot(gcols[:, GROUP * lo : GROUP * hi], wb_ref[w_lo:w_hi, :])

    @pl.loop(0, BD)
    def _(b):
        base = b * 27
        g = pltpu.roll(gpad[pl.ds(pl.multiple_of(b * PADR, 8), PADR), :], PADL - 64, 1)
        center_ref[b] = g[8:72, 0:512]

        def add(t, row, data):
            at = idx_ref[base + t]
            gext[at, row : row + data.shape[0], :] = gext[at, row : row + data.shape[0], :] + data

        for first, t, at in brick_blocks():
            for q in range(4):
                add(t + 1, at + 8 * q, g[first : first + 8, 128 * q : 128 * (q + 1)])
            rim = g[first : first + 8, 512:640]
            add(t + 2, at, jnp.where(low8, rim, 0.0))
            add(t, at + 24, jnp.where(low8, 0.0, rim))
        for x in range(8):
            hi_at, lo_at = (X_LO, X_LO + 24) if x == 0 else (X_HI, X_HI + 24) if x == 7 else (Z_AT + 8 * x - 8,) * 2
            rim = g[8 + 8 * x : 16 + 8 * x, 512:640]
            add(14, hi_at, jnp.where(low8, rim, 0.0))
            add(12, lo_at, jnp.where(low8, 0.0, rim))
        for y in (0, 2):
            first = 88 if y == 0 else 104
            row = 7 if y == 0 else 0
            for n, x in enumerate((0, 2)):
                t = 9 * x + 3 * y
                at = X_HI if x == 0 else X_LO
                for q in range(5):
                    line = jnp.broadcast_to(g[first + n : first + n + 1, 128 * q : 128 * (q + 1)], (8, 128))
                    line = jnp.where(row_is(row), line, 0.0)
                    if q < 4:
                        add(t + 1, at + 8 * q, line)
                    else:
                        add(t + 2, at, jnp.where(low8, line, 0.0))
                        add(t, at + 24, jnp.where(low8, 0.0, line))

    for b in range(BD):
        gown_ref[b] = gext[b]
    for out, items in zip(outs, all_items()):
        for k, (a, b, c, s) in enumerate(items):
            out[k] = gext[BD + 2 * place(a, b, c) + s].astype(BF16)


def last_kernel(me_ref, send_ref, vox_ref, center_ref, gown_ref, *rest):
    recv, out_ref, acc = rest[:10], rest[10], rest[11]
    for b in range(BD):
        acc[b] = gown_ref[b]
    acc[BD] = jnp.zeros((SHELL, 128), F32)

    def add(data, *item):
        at = choice(me_ref, send_ref, *item)
        acc[at] = acc[at] + data.astype(F32)

    for (a, b), ref in zip(PLANE, recv):
        for s in range(slots_of(a, b, 0)):
            add(ref[s], -a, -b, 0, s)
    for c, ref in zip((-1, 1), recv[8:]):
        for s in range(2):
            add(ref[s], 0, 0, -c, s)
        for k, (a, b) in enumerate(PLANE):
            add(ref[2 + k], -a, -b, -c, 0)
    low8 = low_half((8, 128))
    for b in range(BD):
        keep = spread_mask(vox_ref[b * ROWS : (b + 1) * ROWS, :], 64)
        lines = []
        for x in range(8):
            blocks = []
            for q in range(4):
                v = center_ref[b, 8 * x : 8 * x + 8, 128 * q : 128 * (q + 1)]
                y_lo = acc[b, Y_LO + 8 * q + x : Y_LO + 8 * q + x + 1, :]
                y_hi = acc[b, Y_HI + 8 * q + x : Y_HI + 8 * q + x + 1, :]
                v = v + jnp.where(row_is(0), jnp.broadcast_to(y_lo, (8, 128)), 0.0)
                v = v + jnp.where(row_is(7), jnp.broadcast_to(y_hi, (8, 128)), 0.0)
                if x == 0:
                    v = v + acc[b, X_LO + 8 * q : X_LO + 8 * q + 8, :]
                if x == 7:
                    v = v + acc[b, X_HI + 8 * q : X_HI + 8 * q + 8, :]
                if 1 <= x <= 6 and q in (0, 3):
                    z = acc[b, Z_AT + 8 * x - 8 : Z_AT + 8 * x, :]
                    v = v + (jnp.where(low8, z, 0.0) if q == 0 else jnp.where(low8, 0.0, z))
                blocks.append(v)
            lines.append(jnp.concatenate(blocks, axis=1))
        dense = jnp.concatenate(lines, axis=0)
        out_ref[b] = (dense * keep).astype(BF16)


def finish_kernel(scale, place_ref, near_ref, far_ref, conv_ref, down_ref, held):
    x, core = place_ref[0], place_ref[1]
    for k in range(4):
        at = jnp.bitwise_xor(x, k)
        held[core * 4 + at] = near_ref[k].astype(F32) * scale
        held[(1 - core) * 4 + at] = far_ref[k].astype(F32) * scale
    full = jnp.concatenate([held[k] for k in range(8)], axis=0)
    for t in range(9):
        turned = full[64 * t : 64 * (t + 1)].T
        conv_ref[3 * t] = turned[:64]
        conv_ref[3 * t + 1] = turned[64:]
    for m in range(5):
        turned = full[576 + 64 * m : 640 + 64 * m].T
        conv_ref[6 * m + 2] = turned[:64]
        if m < 4:
            conv_ref[6 * m + 5] = turned[64:]
    for q in range(4):
        turned = full[896 + 128 * q : 1024 + 128 * q].T
        down_ref[2 * q] = turned[:64]
        down_ref[2 * q + 1] = turned[64:]


def call(kernel, outs, args, smem, scratch=(), flops=0):
    spec_s = pl.BlockSpec(memory_space=pltpu.SMEM)
    spec_v = pl.BlockSpec(memory_space=pltpu.VMEM)
    moved = sum(int(np.prod(v.shape)) * v.dtype.itemsize for v in (*args, *outs))
    return pl.pallas_call(
        kernel,
        out_shape=outs,
        in_specs=[spec_s] * smem + [spec_v] * (len(args) - smem),
        out_specs=[spec_v] * len(outs),
        scratch_shapes=list(scratch),
        compiler_params=pltpu.CompilerParams(vmem_limit_bytes=VMEM),
        cost_estimate=pl.CostEstimate(flops=flops, bytes_accessed=moved, transcendentals=0),
    )(*args)


def exchange(parts, peers):
    got = [lax.ppermute(v, "spatial", shift_pairs(peers, a, b, 0)) for (a, b), v in zip(PLANE, parts)]
    along = []
    for n, c in enumerate((-1, 1)):
        pieces = [parts[8 + n]]
        for v in got:
            at = v.shape[0] - 2 + n
            pieces.append(v[at : at + 1])
        along.append(lax.ppermute(jnp.concatenate(pieces, axis=0), "spatial", shift_pairs(peers, 0, 0, c)))
    return got + along


def pair_weights(taps, width):
    zero = jnp.zeros((3, 3, 1, width, width), taps.dtype)
    first = jnp.concatenate([taps, zero], axis=2)
    second = jnp.concatenate([zero, taps], axis=2)
    both = jnp.stack([first, second], axis=4).reshape(9, 2, 2 * width, 2 * width)
    return both.transpose(1, 0, 2, 3).reshape(2 * GROUP, 2 * width)


def reduce_sums(sums, me, x, peers):
    core = me % 2
    halves = sums.reshape(2, 4, SHELL, 128)
    near = lax.dynamic_index_in_dim(halves, core, 0, keepdims=False)
    far = lax.dynamic_index_in_dim(halves, 1 - core, 0, keepdims=False)

    def swap(v, bit):
        return lax.ppermute(v, "spatial", [(d, d ^ bit) for d in range(peers)])

    def swap_x(v, bit):
        return lax.ppermute(v, "dp", [(d, d ^ bit) for d in range(4)])

    mine = near + swap(far.astype(BF16), 1).astype(F32)
    small = mine.astype(BF16)
    v = lax.dynamic_index_in_dim(mine, x, 0, keepdims=False)
    for k in (1, 2, 3):
        part = lax.dynamic_index_in_dim(small, jnp.bitwise_xor(x, k), 0, keepdims=False)
        v = v + swap_x(part, k).astype(F32)

    def pairs(v, bits):
        w = v.astype(BF16)
        got = [w.astype(F32)] + [swap(w, bit).astype(F32) for bit in bits]
        while len(got) > 1:
            got = [got[i] + got[i + 1] for i in range(0, len(got), 2)]
        return got[0]

    v = pairs(v, (16, 32, 48))
    v = pairs(v, (2,))
    v = pairs(v, (4, 8, 12))
    w = v.astype(BF16)
    near = jnp.stack([w] + [swap_x(w, k) for k in (1, 2, 3)])
    return near, swap(near, 1)


def shards(features, masks, rulebook, send_lists, conv_weight, down_weight, cotangent):
    peers = lax.axis_size("spatial")
    me = lax.axis_index("spatial").astype(jnp.int32)
    x = lax.axis_index("dp").astype(jnp.int32)
    me_s = me.reshape(1)
    sends = send_lists.reshape(peers * 2)
    feat = features.reshape(BD, ROWS, LANES)
    cot = cotangent.reshape(BD * 16, LANES)
    vox = masks.reshape(BD * ROWS, 8).astype(BF16)
    voxp = vox.reshape(BD, 4, 2, 4, 2, 8).transpose(2, 4, 0, 1, 3, 5).reshape(BD * ROWS, 8)

    brick = jax.ShapeDtypeStruct((BD, ROWS, LANES), BF16)
    parts = [jax.ShapeDtypeStruct((len(items), SHELL, 128), BF16) for items in all_items()]
    held = pltpu.VMEM((BD + 1, SHELL, 128), BF16)
    own_shape = jax.ShapeDtypeStruct((BD, SHELL, 128), BF16)
    masked, own, *sent = call(pack_kernel, [brick, own_shape, *parts], [me_s, sends, feat, vox], 2, [held])
    recv = exchange(sent, peers)

    entry = rulebook.reshape(BD * 27)
    other = jnp.clip(entry - BD, 0, 2 * peers - 1)
    p = other // 2
    apart = []
    for theirs, ours in zip(region(p), region(me)):
        apart.append(jnp.clip(theirs - ours, -1, 1))
    there = BD + 2 * place(*apart) + other % 2
    idx = jnp.where(entry < BD, entry, jnp.where(entry >= BD + 2 * peers, EMPTY, there)).astype(jnp.int32)
    idx = jnp.clip(idx, 0, EMPTY)

    taps = conv_weight.reshape(3, 3, 3, 64, 64)
    wf = pair_weights(taps, 64)
    wb = pair_weights(taps[:, :, ::-1].transpose(0, 1, 2, 4, 3), 64)
    down = down_weight.reshape(512, 128)
    sel, selt = (jnp.asarray(v, BF16) for v in selections())
    outs = [
        jax.ShapeDtypeStruct((BD * 16, LANES), BF16),
        jax.ShapeDtypeStruct((BD, ROWS, LANES), F32),
        jax.ShapeDtypeStruct((BD, SHELL, 128), F32),
        jax.ShapeDtypeStruct((8 * SHELL, 128), F32),
        *parts,
    ]
    scratch = [
        pltpu.VMEM((EXT, SHELL, 128), F32),
        pltpu.VMEM((EXT, SHELL, 128), F32),
        pltpu.VMEM((PADR, PADL), F32),
        pltpu.VMEM((BD * ROWS, 5 * GROUP), BF16),
        pltpu.VMEM((BD * ROWS, LANES), F32),
        pltpu.VMEM((BD * ROWS, LANES), BF16),
        pltpu.VMEM((BD * ROWS, LANES), BF16),
        pltpu.VMEM((BD * PADR, 4 * GROUP), BF16),
        pltpu.VMEM((BD * PADR, PADL), F32),
    ]
    coarse, center, gown, sums, *back = call(
        main_kernel, outs, [idx, own, masked, voxp, cot, sel, selt, wf, wb, down, *recv], 1, scratch, 10**10
    )
    came = exchange(back, peers)
    near, far = reduce_sums(sums, me, x, peers)
    [grad] = call(
        last_kernel,
        [brick],
        [me_s, sends, vox, center, gown, *came],
        2,
        [pltpu.VMEM((BD + 1, SHELL, 128), F32)],
    )
    scale = float(lax.axis_size("dp") * peers * BD * EDGE**3) ** (-0.5)
    spot = jnp.stack([x, me % 2])
    conv_sum, down_sum = call(
        lambda *refs: finish_kernel(scale, *refs),
        [jax.ShapeDtypeStruct((27, 64, 64), F32), jax.ShapeDtypeStruct((8, 64, 128), F32)],
        [spot, near, far],
        1,
        [pltpu.VMEM((8, SHELL, 128), F32)],
    )
    return (
        coarse.reshape(cotangent.shape),
        grad.reshape(features.shape),
        conv_sum,
        down_sum,
    )


def solution(mesh):
    placed = (
        P("dp", "spatial", None, None, None),
        P("dp", "spatial", None),
        P("dp", "spatial", None),
        P("dp", "spatial", None, None),
        P(),
        P(),
        P("dp", "spatial", None, None, None),
    )
    return jax.shard_map(
        shards,
        mesh=mesh,
        in_specs=placed,
        out_specs=(
            P("dp", "spatial", None, None, None),
            P("dp", "spatial", None, None, None),
            P(),
            P(),
        ),
        check_vma=False,
    )
```

time: 936 us -> 172 us (0.18); the launches traced: 920 us -> 171 us
  waiting for transfers between devices: 441 us -> 11.9 us
  local copies, waits for them, and re-layouts: 246 us -> 21.8 us
  other arithmetic: 159 us -> 3.68 us
  starting transfers between devices: 19.6 us -> 103 us
  matrix products: 37.2 us -> 0 us
  Pallas kernels: 0 us -> 28.4 us
  between operations: 16.5 us -> 1.5 us
    psum x1 -> x0, waiting for transfers between devices: 289 us -> none  [shards(): conv_sum, down_sum = lax.psum((conv_part, down_part), ('spatial', 'dp'))]
    all_to_all x2 -> x0, waiting for transfers between devices: 153 us -> none  [the longest x1 153 us: shards(): lax.all_to_all(outgoing, 'spatial', split_axis=0, concat_axis=0, tiled=True)]
    ppermute x0 -> x35, starting transfers between devices: none -> 103 us  [the longest x16 61.7 us: exchange(): lax.ppermute(v, 'spatial', shift_pairs(peers, a, b, 0))]
    scatter-add x2 -> x0, other arithmetic: 71.5 us -> none  [the longest x1 47.5 us: spread(): jax.ops.segment_sum(data_all, target_all, num_segments=total_count * edge...]
    concatenate x8 -> x2, local copies, waits for them, and re-layouts: 55.5 us -> 0.69 us  [exchange(): jnp.concatenate(pieces, axis=0)]
    gather x28 -> x0, local copies, waits for them, and re-layouts: 52.6 us -> none  [the longest x27 46.3 us: assemble(): cols.append(jnp.take(part, table[:, x_pos * 9 + y_pos * 3 + z_pos], axis=0))]
    another operation x24 -> x4, local copies, waits for them, and re-layouts: 44.8 us -> 2.63 us  [pair_weights(): jnp.stack([first, second], axis=4).reshape(9, 2, 2 * width, 2 * width)]
    dot_general x111 -> x0, matrix products: 37.2 us -> none  [the longest x36 16.2 us: conv_backward(): jnp.einsum('rk,rn->kn', slabs[tap_pair], upstream, preferred_element_type...]
  transfers between devices with their start and end apart: 3 -> 35, of which waited for: 2 -> 6; matrix products, arithmetic and copies ran while one was open for 7% -> 11% of each run, Pallas kernels for 0% -> 1%
where the time goes in v1:
time: 172 us; the launch traced here: 171 us
  starting transfers between devices  103 us (60%)
  Pallas kernels  28.4 us (17%)
  local copies, waits for them, and re-layouts  21.8 us (13%)
  waiting for transfers between devices  11.9 us (7%)
  other arithmetic  3.68 us (2%)
    ppermute x16, starting transfers between devices, exchange(): lax.ppermute(v, 'spatial', shift_pairs(peers, a, b, 0))  61.7 us
    pallas_call x4, Pallas kernels, call(): pl.pallas_call(kernel, out_shape=outs, in_specs=[spec_s] * smem + [spec_v...  28.4 us
    ppermute x9, starting transfers between devices, swap(): return lax.ppermute(v, 'spatial', [(d, d ^ bit) for d in range(peers)])  17.1 us
    ppermute x4, starting transfers between devices, exchange(): lax.ppermute(jnp.concatenate(pieces, axis=0), 'spatial', shift_pairs(peer...  15.6 us
    unnamed x80, local copies, waits for them, and re-layouts  9.79 us
    ppermute x6, starting transfers between devices, swap_x(): return lax.ppermute(v, 'dp', [(d, d ^ bit) for d in range(4)])  8.82 us
    ppermute x9, waiting for transfers between devices, swap(): return lax.ppermute(v, 'spatial', [(d, d ^ bit) for d in range(peers)])  6.44 us
    ppermute x6, waiting for transfers between devices, swap_x(): return lax.ppermute(v, 'dp', [(d, d ^ bit) for d in range(4)])  4.25 us
  transfers between devices with their start and end apart: 35, of which 6 were waited for; matrix products, arithmetic and copies ran while one was open for 11% of the time, Pallas kernels for 1%

profile of v1, /device:TPU:41, one launch (start us, length us, event | category | flops | bytes accessed | tf_op | source)
XLA Modules:
  0.0 170.5 jit_solution(4492973769068017742)
XLA Ops:
  0.6 0.7 convert_reduce_fusion
  1.4 0.8 convert_element_type.71.vox_ref
  2.2 0.8 copy.22
  2.9 0.7 reshape.61.send_ref
  3.6 3.3 %shard_map.120 = (bf16[6,64,512]{2,1,0:T(8,128)(2,1)}, bf16[6,176,128]{2,1,0:T(8,128)(2,1)}, bf16[3,176,128]{2,1,0:T(8,128)(2,1)}, bf16[4,176,128]{2,1,0:T(8,128...) custom-call(s32[1]{0:T(128)} %bitcast.me_ref, ...), custom_call_target="tpu_custom_call" | custom-call | bytes 2505220 | tf_op jit(solution)/shard_map/pallas_call | solution.py:403
  7.0 1.3 collective-permute-start
  8.3 3.2 %collective-permute-start.1 = (bf16[4,176,128]{2,1,0:T(8,128)(2,1)}, bf16[4,176,128]{2,1,0:T(8,128)(2,1)S(1)}, u32[]{:S(2)}, u32[]{:S(2)}) collective-permute-start(bf16[4,176,128]{2,1,0:T(8,128)(2,1)} %get-tuple-element.35), channel_id=1, source_target_pairs={{64,128},{68,132},{72,136},{76,140},{80,144},{84,148},{88,152},{92... | collective-permute-start | bytes 540680 | tf_op jit(solution)/shard_map/ppermute | solution.py:415
  11.5 5.3 %collective-permute-start.2 = (bf16[3,176,128]{2,1,0:T(8,128)(2,1)}, bf16[3,176,128]{2,1,0:T(8,128)(2,1)S(1)}, u32[]{:S(2)}, u32[]{:S(2)}) collective-permute-start(bf16[3,176,128]{2,1,0:T(8,128)(2,1)} %get-tuple-element.36), channel_id=1, source_target_pairs={{64,144},{68,148},{72,152},{76,156},{80,160},{84,164},{88,168},{92... | collective-permute-start | bytes 405512 | tf_op jit(solution)/shard_map/ppermute | solution.py:415
  16.7 1.3 collective-permute-start.3
  18.0 5.9 %collective-permute-start.4 = (bf16[4,176,128]{2,1,0:T(8,128)(2,1)}, bf16[4,176,128]{2,1,0:T(8,128)(2,1)S(1)}, u32[]{:S(2)}, u32[]{:S(2)}) collective-permute-start(bf16[4,176,128]{2,1,0:T(8,128)(2,1)} %get-tuple-element.38), channel_id=1, source_target_pairs={{0,16},{4,20},{8,24},{12,28},{16,32},{20,36},{24,40},{28,44},{32,4... | collective-permute-start | bytes 540680 | tf_op jit(solution)/shard_map/ppermute | solution.py:415
  23.9 1.0 reverse_bitcast_fusion
  26.0 0.9 copy.28
  27.5 0.9 copy.29
  28.4 0.7 constant_dynamic-update-slice_fusion.8
  29.1 1.3 collective-permute-start.5
  31.1 4.9 %collective-permute-start.6 = (bf16[4,176,128]{2,1,0:T(8,128)(2,1)S(1)}, bf16[4,176,128]{2,1,0:T(8,128)(2,1)S(1)}, u32[]{:S(2)}, u32[]{:S(2)}) collective-permute-start(bf16[4,176,128]{2,1,0:T(8,128)(2,1)S(1)} %copy-done.26), channel_id=1, source_target_pairs={{0,128},{4,132},{8,136},{12,140},{16,144},{20,148},{24,152},{28,15... | collective-permute-start | bytes 540680 | tf_op jit(solution)/shard_map/ppermute | solution.py:415
  36.6 4.6 %collective-permute-start.7 = (bf16[3,176,128]{2,1,0:T(8,128)(2,1)S(1)}, bf16[3,176,128]{2,1,0:T(8,128)(2,1)S(1)}, u32[]{:S(2)}, u32[]{:S(2)}) collective-permute-start(bf16[3,176,128]{2,1,0:T(8,128)(2,1)S(1)} %copy-done.28), channel_id=1, source_target_pairs={{0,144},{4,148},{8,152},{12,156},{16,160},{20,164},{24,168},{28,17... | collective-permute-start | bytes 405512 | tf_op jit(solution)/shard_map/ppermute | solution.py:415
  41.8 0.7 constant_dynamic-update-slice_fusion.13
  42.5 0.7 constant_dynamic-update-slice_fusion.12
  43.2 0.7 constant_dynamic-update-slice_fusion.11
  43.9 0.7 constant_dynamic-update-slice_fusion.10
  44.5 1.1 collective-permute-done.7.rest_7_
  45.7 0.7 constant_dynamic-update-slice_fusion.9
  46.3 4.8 %collective-permute-start.8 = (bf16[10,176,128]{2,1,0:T(8,128)(2,1)}, bf16[10,176,128]{2,1,0:T(8,128)(2,1)}, u32[]{:S(2)}, u32[]{:S(2)}) collective-permute-start(bf16[10,176,128]{2,1,0:T(8,128)(2,1)} %get-tuple-element.94), channel_id=1, source_target_pairs={{4,0},{8,4},{12,8},{20,16},{24,20},{28,24},{36,32},{40,36},{44,40}... | collective-permute-start | bytes 1351688 | tf_op jit(solution)/shard_map/ppermute | solution.py:422
  51.2 1.5 collective-permute-start.9
  53.3 1.2 copy.24
  55.1 0.9 copy.25
  56.0 0.7 copy.23
  56.6 0.7 reshape.64.cot_ref
  57.9 19.4 %shard_map.121 = (bf16[96,512]{1,0:T(8,128)(2,1)}, f32[6,64,512]{2,1,0:T(8,128)}, f32[6,176,128]{2,1,0:T(8,128)}, f32[1408,128]{1,0:T(8,128)}, bf16[3,176,128]{2...) custom-call(s32[162]{0:T(256)} %fusion.15.idx_ref, ...), custom_call_target="tpu_custom_call" | custom-call | flops 10000000000 | bytes 8088200 | tf_op jit(solution)/shard_map/pallas_call | solution.py:403
  77.4 1.1 fusion
  78.4 2.6 %collective-permute-start.20 = (bf16[4,176,128]{2,1,0:T(8,128)(2,1)S(1)}, bf16[4,176,128]{2,1,0:T(8,128)(2,1)S(1)}, u32[]{:S(2)}, u32[]{:S(2)}) collective-permute-start(bf16[4,176,128]{2,1,0:T(8,128)(2,1)S(1)} %fusion), channel_id=1, source_target_pairs={{0,4},{4,0},{8,12},{12,8},{16,20},{20,16},{24,28},{28,24},{32,36},... | collective-permute-start | bytes 540680 | tf_op jit(solution)/shard_map/ppermute | solution.py:441
  81.1 1.3 collective-permute-start.10
  82.3 0.9 constant_dynamic-update-slice_fusion.26
  83.2 4.0 %collective-permute-start.11 = (bf16[4,176,128]{2,1,0:T(8,128)(2,1)}, bf16[4,176,128]{2,1,0:T(8,128)(2,1)S(1)}, u32[]{:S(2)}, u32[]{:S(2)}) collective-permute-start(bf16[4,176,128]{2,1,0:T(8,128)(2,1)} %get-tuple-element.48), channel_id=1, source_target_pairs={{64,128},{68,132},{72,136},{76,140},{80,144},{84,148},{88,152},{92... | collective-permute-start | bytes 540680 | tf_op jit(solution)/shard_map/ppermute | solution.py:415
  87.2 8.7 %collective-permute-start.12 = (bf16[3,176,128]{2,1,0:T(8,128)(2,1)}, bf16[3,176,128]{2,1,0:T(8,128)(2,1)S(1)}, u32[]{:S(2)}, u32[]{:S(2)}) collective-permute-start(bf16[3,176,128]{2,1,0:T(8,128)(2,1)} %get-tuple-element.49), channel_id=1, source_target_pairs={{64,144},{68,148},{72,152},{76,156},{80,160},{84,164},{88,168},{92... | collective-permute-start | bytes 405512 | tf_op jit(solution)/shard_map/ppermute | solution.py:415
  96.0 1.3 collective-permute-start.13
  97.3 0.9 constant_dynamic-update-slice_fusion.35
  98.2 7.3 %collective-permute-start.14 = (bf16[4,176,128]{2,1,0:T(8,128)(2,1)}, bf16[4,176,128]{2,1,0:T(8,128)(2,1)S(1)}, u32[]{:S(2)}, u32[]{:S(2)}) collective-permute-start(bf16[4,176,128]{2,1,0:T(8,128)(2,1)} %get-tuple-element.51), channel_id=1, source_target_pairs={{0,16},{4,20},{8,24},{12,28},{16,32},{20,36},{24,40},{28,44},{32,4... | collective-permute-start | bytes 540680 | tf_op jit(solution)/shard_map/ppermute | solution.py:415
  105.5 1.3 collective-permute-start.15
  106.8 1.0 fusion.16
  107.9 4.9 %collective-permute-start.16 = (bf16[4,176,128]{2,1,0:T(8,128)(2,1)S(1)}, bf16[4,176,128]{2,1,0:T(8,128)(2,1)S(1)}, u32[]{:S(2)}, u32[]{:S(2)}) collective-permute-start(bf16[4,176,128]{2,1,0:T(8,128)(2,1)S(1)} %copy-done.27), channel_id=1, source_target_pairs={{0,128},{4,132},{8,136},{12,140},{16,144},{20,148},{24,152},{28,15... | collective-permute-start | bytes 540680 | tf_op jit(solution)/shard_map/ppermute | solution.py:415
  112.9 1.3 collective-permute-start.21
  114.2 2.8 %collective-permute-start.22 = (bf16[176,128]{1,0:T(8,128)(2,1)S(1)}, bf16[176,128]{1,0:T(8,128)(2,1)S(1)}, u32[]{:S(2)}, u32[]{:S(2)}) collective-permute-start(bf16[176,128]{1,0:T(8,128)(2,1)S(1)} %get-tuple-element.68), channel_id=1, source_target_pairs={{0,2},{1,3},{2,0},{3,1},{4,6},{5,7},{6,4},{7,5},{8,10},{9,11},{10,... | collective-permute-start | bytes 135176 | tf_op jit(solution)/shard_map/ppermute | solution.py:444
  117.3 5.4 %collective-permute-start.17 = (bf16[3,176,128]{2,1,0:T(8,128)(2,1)S(1)}, bf16[3,176,128]{2,1,0:T(8,128)(2,1)S(1)}, u32[]{:S(2)}, u32[]{:S(2)}) collective-permute-start(bf16[3,176,128]{2,1,0:T(8,128)(2,1)S(1)} %copy-done.30), channel_id=1, source_target_pairs={{0,144},{4,148},{8,152},{12,156},{16,160},{20,164},{24,168},{28,17... | collective-permute-start | bytes 405512 | tf_op jit(solution)/shard_map/ppermute | solution.py:415
  122.8 2.3 %collective-permute-start.24 = (bf16[176,128]{1,0:T(8,128)(2,1)S(1)}, bf16[176,128]{1,0:T(8,128)(2,1)S(1)}, u32[]{:S(2)}, u32[]{:S(2)}) collective-permute-start(bf16[176,128]{1,0:T(8,128)(2,1)S(1)} %fusion.3), channel_id=1, source_target_pairs={{0,64},{4,68},{8,72},{12,76},{16,80},{20,84},{24,88},{28,92},{32,9... | collective-permute-start | bytes 135176 | tf_op jit(solution)/shard_map/ppermute | solution.py:441
  125.3 1.0 collective-permute-start.26
  126.5 3.2 %collective-permute-done.25 = bf16[176,128]{1,0:T(8,128)(2,1)S(1)} collective-permute-done((bf16[176,128]{1,0:T(8,128)(2,1)S(1)}, bf16[176,128]{1,0:T(8,128)(2,1)S(1)}, u32[]{:S(2)}, u32[]{:S(2)}) %collective-permute-start.25) | collective-permute-done | bytes 45088 | tf_op jit(solution)/shard_map/ppermute | solution.py:441
  129.8 3.1 %collective-permute-done.27 = bf16[176,128]{1,0:T(8,128)(2,1)S(1)} collective-permute-done((bf16[176,128]{1,0:T(8,128)(2,1)S(1)}, bf16[176,128]{1,0:T(8,128)(2,1)S(1)}, u32[]{:S(2)}, u32[]{:S(2)}) %collective-permute-start.27) | collective-permute-done | bytes 45088 | tf_op jit(solution)/shard_map/ppermute | solution.py:441
  133.0 4.4 %collective-permute-start.28 = (bf16[176,128]{1,0:T(8,128)(2,1)S(1)}, bf16[176,128]{1,0:T(8,128)(2,1)S(1)}, u32[]{:S(2)}, u32[]{:S(2)}) collective-permute-start(bf16[176,128]{1,0:T(8,128)(2,1)S(1)} %add_convert_fusion.1), channel_id=1, source_target_pairs={{0,16},{4,20},{8,24},{12,28},{16,0},{20,4},{24,8},{28,12},{32,48},... | collective-permute-start | bytes 135176 | tf_op jit(solution)/shard_map/ppermute | solution.py:441
  137.4 1.8 %collective-permute-start.29 = (bf16[176,128]{1,0:T(8,128)(2,1)S(1)}, bf16[176,128]{1,0:T(8,128)(2,1)S(1)}, u32[]{:S(2)}, u32[]{:S(2)}) collective-permute-start(bf16[176,128]{1,0:T(8,128)(2,1)S(1)} %add_convert_fusion.1), channel_id=1, source_target_pairs={{0,32},{4,36},{8,40},{12,44},{16,48},{20,52},{24,56},{28,60},{32,0... | collective-permute-start | bytes 135176 | tf_op jit(solution)/shard_map/ppermute | solution.py:441
  139.1 1.6 collective-permute-start.30
  140.8 8.0 %collective-permute-start.18 = (bf16[10,176,128]{2,1,0:T(8,128)(2,1)S(1)}, bf16[10,176,128]{2,1,0:T(8,128)(2,1)S(1)}, u32[]{:S(2)}, u32[]{:S(2)}) collective-permute-start(bf16[10,176,128]{2,1,0:T(8,128)(2,1)S(1)} %get-tuple-element.86), channel_id=1, source_target_pairs={{4,0},{8,4},{12,8},{20,16},{24,20},{28,24},{36,32},{40,36},{44,40}... | collective-permute-start | bytes 1351688 | tf_op jit(solution)/shard_map/ppermute | solution.py:422
  148.8 1.3 collective-permute-start.19
  150.1 0.7 collective-permute-start.31
  150.9 3.8 %collective-permute-start.32 = (bf16[176,128]{1,0:T(8,128)(2,1)S(1)}, bf16[176,128]{1,0:T(8,128)(2,1)S(1)}, u32[]{:S(2)}, u32[]{:S(2)}) collective-permute-start(bf16[176,128]{1,0:T(8,128)(2,1)S(1)} %add_convert_fusion), channel_id=1, source_target_pairs={{0,2},{1,3},{2,0},{3,1},{4,6},{5,7},{6,4},{7,5},{8,10},{9,11},{10,... | collective-permute-start | bytes 135176 | tf_op jit(solution)/shard_map/ppermute | solution.py:444
  154.6 1.9 %collective-permute-done.32 = bf16[176,128]{1,0:T(8,128)(2,1)S(1)} collective-permute-done((bf16[176,128]{1,0:T(8,128)(2,1)S(1)}, bf16[176,128]{1,0:T(8,128)(2,1)S(1)}, u32[]{:S(2)}, u32[]{:S(2)}) %collective-permute-start.32) | collective-permute-done | bytes 45088 | tf_op jit(solution)/shard_map/ppermute | solution.py:444
  156.5 2.3 %collective-permute-done.33 = bf16[176,128]{1,0:T(8,128)(2,1)S(1)} collective-permute-done((bf16[176,128]{1,0:T(8,128)(2,1)S(1)}, bf16[176,128]{1,0:T(8,128)(2,1)S(1)}, u32[]{:S(2)}, u32[]{:S(2)}) %collective-permute-start.33) | collective-permute-done | bytes 45088 | tf_op jit(solution)/shard_map/ppermute | solution.py:444
  158.9 3.0 %collective-permute-start.34 = (bf16[4,176,128]{2,1,0:T(8,128)(2,1)S(1)}, bf16[4,176,128]{2,1,0:T(8,128)(2,1)S(1)}, u32[]{:S(2)}, u32[]{:S(2)}) collective-permute-start(bf16[4,176,128]{2,1,0:T(8,128)(2,1)S(1)} %pad_maximum_fusion.2.refs_1_), channel_id=1, source_target_pairs={{0,4},{4,0},{8,12},{12,8},{16,20},{20,16},{24,28},{28,24},{32,36},... | collective-permute-start | bytes 540680 | tf_op jit(solution)/shard_map/ppermute | solution.py:441
  162.5 0.7 reshape.71
  163.2 0.7 copy-done.12
  163.9 2.4 %shard_map.123 = (f32[27,64,64]{2,1,0:T(8,128)}, f32[8,64,128]{2,1,0:T(8,128)}) custom-call(s32[2]{0:T(128)} %pad_add_fusion.refs_0_, bf16[4,176,128]{2,1,0:T(8,128)(2,1)} %copy-done.1, bf16[4,176,128]{2,1,0:T(8,128)(2,1)} %copy-done.12), custom_call_target="tpu_custom_call" | custom-call | bytes 1064968 | tf_op jit(solution)/shard_map/pallas_call | solution.py:403
  166.3 0.7 copy-done.2
  167.2 3.3 %shard_map.122 = bf16[6,64,512]{2,1,0:T(8,128)(2,1)} custom-call(s32[1]{0:T(128)} %bitcast.me_ref, s32[128]{0:T(128)} %reshape.61.send_ref, bf16[384,8]{1,0:T(8,128)(2,1)} %convert_element_type.71.vox_ref, f32[6,64,512]{2,1,0:T(8,128)} %get-tuple-element.45.center_ref, f32[6,176,128]{2,1,0:T(8,128)} %get-tuple-element.46.gown_ref, ...), custom_call_target="tpu_custom_call" | custom-call | bytes 3889668 | tf_op jit(solution)/shard_map/pallas_call | solution.py:403
  (122 shorter events, 7.0 us)
Async XLA Ops:
  7.0 22.1 %collective-permute-start = (bf16[3,176,128]{2,1,0:T(8,128)(2,1)}, bf16[3,176,128]{2,1,0:T(8,128)(2,1)S(1)}, u32[]{:S(2)}, u32[]{:S(2)}) collective-permute-start(bf16[3,176,128]{2,1,0:T(8,128)(2,1)} %get-tuple-element.34), channel_id=1, source_target_pairs={{80,128},{84,132},{88,136},{92,140},{96,144},{100,148},{104,152},{... | collective-permute-start | bytes 405512 | tf_op jit(solution)/shard_map/ppermute | solution.py:415
  8.3 22.8 %collective-permute-start.1 = (bf16[4,176,128]{2,1,0:T(8,128)(2,1)}, bf16[4,176,128]{2,1,0:T(8,128)(2,1)S(1)}, u32[]{:S(2)}, u32[]{:S(2)}) collective-permute-start(bf16[4,176,128]{2,1,0:T(8,128)(2,1)} %get-tuple-element.35), channel_id=1, source_target_pairs={{64,128},{68,132},{72,136},{76,140},{80,144},{84,148},{88,152},{92... | collective-permute-start | bytes 540680 | tf_op jit(solution)/shard_map/ppermute | solution.py:415
  11.5 25.1 %collective-permute-start.2 = (bf16[3,176,128]{2,1,0:T(8,128)(2,1)}, bf16[3,176,128]{2,1,0:T(8,128)(2,1)S(1)}, u32[]{:S(2)}, u32[]{:S(2)}) collective-permute-start(bf16[3,176,128]{2,1,0:T(8,128)(2,1)} %get-tuple-element.36), channel_id=1, source_target_pairs={{64,144},{68,148},{72,152},{76,156},{80,160},{84,164},{88,168},{92... | collective-permute-start | bytes 405512 | tf_op jit(solution)/shard_map/ppermute | solution.py:415
  16.7 25.1 %collective-permute-start.3 = (bf16[4,176,128]{2,1,0:T(8,128)(2,1)}, bf16[4,176,128]{2,1,0:T(8,128)(2,1)S(1)}, u32[]{:S(2)}, u32[]{:S(2)}) collective-permute-start(bf16[4,176,128]{2,1,0:T(8,128)(2,1)} %get-tuple-element.37), channel_id=1, source_target_pairs={{16,0},{20,4},{24,8},{28,12},{32,16},{36,20},{40,24},{44,28},{48,3... | collective-permute-start | bytes 540680 | tf_op jit(solution)/shard_map/ppermute | solution.py:415
  18.0 24.5 %collective-permute-start.4 = (bf16[4,176,128]{2,1,0:T(8,128)(2,1)}, bf16[4,176,128]{2,1,0:T(8,128)(2,1)S(1)}, u32[]{:S(2)}, u32[]{:S(2)}) collective-permute-start(bf16[4,176,128]{2,1,0:T(8,128)(2,1)} %get-tuple-element.38), channel_id=1, source_target_pairs={{0,16},{4,20},{8,24},{12,28},{16,32},{20,36},{24,40},{28,44},{32,4... | collective-permute-start | bytes 540680 | tf_op jit(solution)/shard_map/ppermute | solution.py:415
  26.9 1.5 copy-start.15
  26.9 1.5 copy-start.16
  27.5 1.6 copy-start.29
  27.5 3.5 %copy-start.26 = (bf16[4,176,128]{2,1,0:T(8,128)(2,1)S(1)}, bf16[4,176,128]{2,1,0:T(8,128)(2,1)}, u32[]{:S(2)}) copy-start(bf16[4,176,128]{2,1,0:T(8,128)(2,1)} %get-tuple-element.40) | copy-start | bytes 540676
  27.5 9.1 %copy-start.28 = (bf16[3,176,128]{2,1,0:T(8,128)(2,1)S(1)}, bf16[3,176,128]{2,1,0:T(8,128)(2,1)}, u32[]{:S(2)}) copy-start(bf16[3,176,128]{2,1,0:T(8,128)(2,1)} %get-tuple-element.41) | copy-start | bytes 405508
  28.4 24.3 %copy-start = (bf16[27,64,64]{2,1,0:T(8,128)(2,1)S(1)}, bf16[27,64,64]{2,1,0:T(8,128)(2,1)}, u32[]{:S(2)}) copy-start(bf16[27,64,64]{2,1,0:T(8,128)(2,1)} %param.13) | copy-start | bytes 663556
  29.1 23.8 %copy-start.17 = (bf16[3,176,128]{2,1,0:T(8,128)(2,1)}, bf16[3,176,128]{2,1,0:T(8,128)(2,1)S(1)}, u32[]{:S(2)}) copy-start(bf16[3,176,128]{2,1,0:T(8,128)(2,1)S(1)} %collective-permute-done.rest_0_) | copy-start | bytes 405508
  29.1 14.1 %collective-permute-start.5 = (bf16[3,176,128]{2,1,0:T(8,128)(2,1)S(1)}, bf16[3,176,128]{2,1,0:T(8,128)(2,1)S(1)}, u32[]{:S(2)}, u32[]{:S(2)}) collective-permute-start(bf16[3,176,128]{2,1,0:T(8,128)(2,1)S(1)} %copy-done.29), channel_id=1, source_target_pairs={{16,128},{20,132},{24,136},{28,140},{32,144},{36,148},{40,152},{44... | collective-permute-start | bytes 405512 | tf_op jit(solution)/shard_map/ppermute | solution.py:415
  31.1 21.9 %copy-start.21 = (bf16[4,176,128]{2,1,0:T(8,128)(2,1)}, bf16[4,176,128]{2,1,0:T(8,128)(2,1)S(1)}, u32[]{:S(2)}) copy-start(bf16[4,176,128]{2,1,0:T(8,128)(2,1)S(1)} %collective-permute-done.1.rest_1_) | copy-start | bytes 540676
  31.1 12.8 %collective-permute-start.6 = (bf16[4,176,128]{2,1,0:T(8,128)(2,1)S(1)}, bf16[4,176,128]{2,1,0:T(8,128)(2,1)S(1)}, u32[]{:S(2)}, u32[]{:S(2)}) collective-permute-start(bf16[4,176,128]{2,1,0:T(8,128)(2,1)S(1)} %copy-done.26), channel_id=1, source_target_pairs={{0,128},{4,132},{8,136},{12,140},{16,144},{20,148},{24,152},{28,15... | collective-permute-start | bytes 540680 | tf_op jit(solution)/shard_map/ppermute | solution.py:415
  36.6 16.4 %copy-start.18 = (bf16[3,176,128]{2,1,0:T(8,128)(2,1)}, bf16[3,176,128]{2,1,0:T(8,128)(2,1)S(1)}, u32[]{:S(2)}) copy-start(bf16[3,176,128]{2,1,0:T(8,128)(2,1)S(1)} %collective-permute-done.2.rest_2_) | copy-start | bytes 405508
  36.6 9.1 %collective-permute-start.7 = (bf16[3,176,128]{2,1,0:T(8,128)(2,1)S(1)}, bf16[3,176,128]{2,1,0:T(8,128)(2,1)S(1)}, u32[]{:S(2)}, u32[]{:S(2)}) collective-permute-start(bf16[3,176,128]{2,1,0:T(8,128)(2,1)S(1)} %copy-done.28), channel_id=1, source_target_pairs={{0,144},{4,148},{8,152},{12,156},{16,160},{20,164},{24,168},{28,17... | collective-permute-start | bytes 405512 | tf_op jit(solution)/shard_map/ppermute | solution.py:415
  41.8 11.2 %copy-start.22 = (bf16[4,176,128]{2,1,0:T(8,128)(2,1)}, bf16[4,176,128]{2,1,0:T(8,128)(2,1)S(1)}, u32[]{:S(2)}) copy-start(bf16[4,176,128]{2,1,0:T(8,128)(2,1)S(1)} %collective-permute-done.3.rest_3_) | copy-start | bytes 540676
  42.5 10.5 %copy-start.23 = (bf16[4,176,128]{2,1,0:T(8,128)(2,1)}, bf16[4,176,128]{2,1,0:T(8,128)(2,1)S(1)}, u32[]{:S(2)}) copy-start(bf16[4,176,128]{2,1,0:T(8,128)(2,1)S(1)} %collective-permute-done.4.rest_4_) | copy-start | bytes 540676
  43.2 10.1 %copy-start.19 = (bf16[3,176,128]{2,1,0:T(8,128)(2,1)}, bf16[3,176,128]{2,1,0:T(8,128)(2,1)S(1)}, u32[]{:S(2)}) copy-start(bf16[3,176,128]{2,1,0:T(8,128)(2,1)S(1)} %collective-permute-done.5.rest_5_) | copy-start | bytes 405508
  43.9 9.4 %copy-start.24 = (bf16[4,176,128]{2,1,0:T(8,128)(2,1)}, bf16[4,176,128]{2,1,0:T(8,128)(2,1)S(1)}, u32[]{:S(2)}) copy-start(bf16[4,176,128]{2,1,0:T(8,128)(2,1)S(1)} %collective-permute-done.6.rest_6_) | copy-start | bytes 540676
  45.7 7.6 %copy-start.20 = (bf16[3,176,128]{2,1,0:T(8,128)(2,1)}, bf16[3,176,128]{2,1,0:T(8,128)(2,1)S(1)}, u32[]{:S(2)}) copy-start(bf16[3,176,128]{2,1,0:T(8,128)(2,1)S(1)} %collective-permute-done.7.rest_7_) | copy-start | bytes 405508
  46.3 11.6 %collective-permute-start.8 = (bf16[10,176,128]{2,1,0:T(8,128)(2,1)}, bf16[10,176,128]{2,1,0:T(8,128)(2,1)}, u32[]{:S(2)}, u32[]{:S(2)}) collective-permute-start(bf16[10,176,128]{2,1,0:T(8,128)(2,1)} %get-tuple-element.94), channel_id=1, source_target_pairs={{4,0},{8,4},{12,8},{20,16},{24,20},{28,24},{36,32},{40,36},{44,40}... | collective-permute-start | bytes 1351688 | tf_op jit(solution)/shard_map/ppermute | solution.py:422
  51.2 6.7 %collective-permute-start.9 = (bf16[10,176,128]{2,1,0:T(8,128)(2,1)}, bf16[10,176,128]{2,1,0:T(8,128)(2,1)}, u32[]{:S(2)}, u32[]{:S(2)}) collective-permute-start(bf16[10,176,128]{2,1,0:T(8,128)(2,1)} %get-tuple-element.93), channel_id=1, source_target_pairs={{0,4},{4,8},{8,12},{16,20},{20,24},{24,28},{32,36},{36,40},{40,44}... | collective-permute-start | bytes 1351688 | tf_op jit(solution)/shard_map/ppermute | solution.py:422
  54.5 2.1 %copy-start.13 = (bf16[1,6,4,4,512]{4,3,2,1,0:T(4,128)(2,1)S(1)}, bf16[1,6,4,4,512]{4,3,2,1,0:T(4,128)(2,1)}, u32[]{:S(2)}) copy-start(bf16[1,6,4,4,512]{4,3,2,1,0:T(4,128)(2,1)} %param.15) | copy-start | bytes 294916
  77.4 30.5 %copy-start.27 = (bf16[4,176,128]{2,1,0:T(8,128)(2,1)S(1)}, bf16[4,176,128]{2,1,0:T(8,128)(2,1)}, u32[]{:S(2)}) copy-start(bf16[4,176,128]{2,1,0:T(8,128)(2,1)} %get-tuple-element.53) | copy-start | bytes 540676
  78.4 27.1 %collective-permute-start.20 = (bf16[4,176,128]{2,1,0:T(8,128)(2,1)S(1)}, bf16[4,176,128]{2,1,0:T(8,128)(2,1)S(1)}, u32[]{:S(2)}, u32[]{:S(2)}) collective-permute-start(bf16[4,176,128]{2,1,0:T(8,128)(2,1)S(1)} %fusion), channel_id=1, source_target_pairs={{0,4},{4,0},{8,12},{12,8},{16,20},{20,16},{24,28},{28,24},{32,36},... | collective-permute-start | bytes 540680 | tf_op jit(solution)/shard_map/ppermute | solution.py:441
  81.1 17.1 %collective-permute-start.10 = (bf16[3,176,128]{2,1,0:T(8,128)(2,1)}, bf16[3,176,128]{2,1,0:T(8,128)(2,1)S(1)}, u32[]{:S(2)}, u32[]{:S(2)}) collective-permute-start(bf16[3,176,128]{2,1,0:T(8,128)(2,1)} %get-tuple-element.47), channel_id=1, source_target_pairs={{80,128},{84,132},{88,136},{92,140},{96,144},{100,148},{104,152},{... | collective-permute-start | bytes 405512 | tf_op jit(solution)/shard_map/ppermute | solution.py:415
  83.2 24.6 %collective-permute-start.11 = (bf16[4,176,128]{2,1,0:T(8,128)(2,1)}, bf16[4,176,128]{2,1,0:T(8,128)(2,1)S(1)}, u32[]{:S(2)}, u32[]{:S(2)}) collective-permute-start(bf16[4,176,128]{2,1,0:T(8,128)(2,1)} %get-tuple-element.48), channel_id=1, source_target_pairs={{64,128},{68,132},{72,136},{76,140},{80,144},{84,148},{88,152},{92... | collective-permute-start | bytes 540680 | tf_op jit(solution)/shard_map/ppermute | solution.py:415
  87.2 25.6 %collective-permute-start.12 = (bf16[3,176,128]{2,1,0:T(8,128)(2,1)}, bf16[3,176,128]{2,1,0:T(8,128)(2,1)S(1)}, u32[]{:S(2)}, u32[]{:S(2)}) collective-permute-start(bf16[3,176,128]{2,1,0:T(8,128)(2,1)} %get-tuple-element.49), channel_id=1, source_target_pairs={{64,144},{68,148},{72,152},{76,156},{80,160},{84,164},{88,168},{92... | collective-permute-start | bytes 405512 | tf_op jit(solution)/shard_map/ppermute | solution.py:415
  96.0 18.2 %collective-permute-start.13 = (bf16[4,176,128]{2,1,0:T(8,128)(2,1)}, bf16[4,176,128]{2,1,0:T(8,128)(2,1)S(1)}, u32[]{:S(2)}, u32[]{:S(2)}) collective-permute-start(bf16[4,176,128]{2,1,0:T(8,128)(2,1)} %get-tuple-element.50), channel_id=1, source_target_pairs={{16,0},{20,4},{24,8},{28,12},{32,16},{36,20},{40,24},{44,28},{48,3... | collective-permute-start | bytes 540680 | tf_op jit(solution)/shard_map/ppermute | solution.py:415
  98.2 19.1 %copy-start.30 = (bf16[3,176,128]{2,1,0:T(8,128)(2,1)S(1)}, bf16[3,176,128]{2,1,0:T(8,128)(2,1)}, u32[]{:S(2)}) copy-start(bf16[3,176,128]{2,1,0:T(8,128)(2,1)} %get-tuple-element.54) | copy-start | bytes 405508
  98.2 24.6 %copy-start.8 = (bf16[3,176,128]{2,1,0:T(8,128)(2,1)}, bf16[3,176,128]{2,1,0:T(8,128)(2,1)S(1)}, u32[]{:S(2)}) copy-start(bf16[3,176,128]{2,1,0:T(8,128)(2,1)S(1)} %collective-permute-done.10.rest_0_) | copy-start | bytes 405508
  98.2 18.8 %collective-permute-start.14 = (bf16[4,176,128]{2,1,0:T(8,128)(2,1)}, bf16[4,176,128]{2,1,0:T(8,128)(2,1)S(1)}, u32[]{:S(2)}, u32[]{:S(2)}) collective-permute-start(bf16[4,176,128]{2,1,0:T(8,128)(2,1)} %get-tuple-element.51), channel_id=1, source_target_pairs={{0,16},{4,20},{8,24},{12,28},{16,32},{20,36},{24,40},{28,44},{32,4... | collective-permute-start | bytes 540680 | tf_op jit(solution)/shard_map/ppermute | solution.py:415
  105.5 19.8 %collective-permute-start.15 = (bf16[3,176,128]{2,1,0:T(8,128)(2,1)}, bf16[3,176,128]{2,1,0:T(8,128)(2,1)S(1)}, u32[]{:S(2)}, u32[]{:S(2)}) collective-permute-start(bf16[3,176,128]{2,1,0:T(8,128)(2,1)} %get-tuple-element.52), channel_id=1, source_target_pairs={{16,128},{20,132},{24,136},{28,140},{32,144},{36,148},{40,152},{44... | collective-permute-start | bytes 405512 | tf_op jit(solution)/shard_map/ppermute | solution.py:415
  107.9 42.2 %copy-start.4 = (bf16[4,176,128]{2,1,0:T(8,128)(2,1)}, bf16[4,176,128]{2,1,0:T(8,128)(2,1)S(1)}, u32[]{:S(2)}) copy-start(bf16[4,176,128]{2,1,0:T(8,128)(2,1)S(1)} %collective-permute-done.11.rest_1_) | copy-start | bytes 540676
  107.9 21.9 %collective-permute-start.16 = (bf16[4,176,128]{2,1,0:T(8,128)(2,1)S(1)}, bf16[4,176,128]{2,1,0:T(8,128)(2,1)S(1)}, u32[]{:S(2)}, u32[]{:S(2)}) collective-permute-start(bf16[4,176,128]{2,1,0:T(8,128)(2,1)S(1)} %copy-done.27), channel_id=1, source_target_pairs={{0,128},{4,132},{8,136},{12,140},{16,144},{20,148},{24,152},{28,15... | collective-permute-start | bytes 540680 | tf_op jit(solution)/shard_map/ppermute | solution.py:415
  112.8 49.7 %copy-start.14 = (bf16[96,512]{1,0:T(8,128)(2,1)S(1)}, bf16[96,512]{1,0:T(8,128)(2,1)}, u32[]{:S(2)}) copy-start(bf16[96,512]{1,0:T(8,128)(2,1)} %get-tuple-element.44) | copy-start | bytes 294916
  112.9 50.4 %copy-start.9 = (bf16[3,176,128]{2,1,0:T(8,128)(2,1)}, bf16[3,176,128]{2,1,0:T(8,128)(2,1)S(1)}, u32[]{:S(2)}) copy-start(bf16[3,176,128]{2,1,0:T(8,128)(2,1)S(1)} %collective-permute-done.12.rest_2_) | copy-start | bytes 405508
  112.9 4.4 %collective-permute-start.21 = (bf16[176,128]{1,0:T(8,128)(2,1)S(1)}, bf16[176,128]{1,0:T(8,128)(2,1)S(1)}, u32[]{:S(2)}, u32[]{:S(2)}) collective-permute-start(bf16[176,128]{1,0:T(8,128)(2,1)S(1)} %get-tuple-element.66), channel_id=1, source_target_pairs={{0,1},{1,0},{2,3},{3,2},{4,5},{5,4},{6,7},{7,6},{8,9},{9,8},{10,11... | collective-permute-start | bytes 135176 | tf_op jit(solution)/shard_map/ppermute | solution.py:444
  114.2 49.0 %copy-start.5 = (bf16[4,176,128]{2,1,0:T(8,128)(2,1)}, bf16[4,176,128]{2,1,0:T(8,128)(2,1)S(1)}, u32[]{:S(2)}) copy-start(bf16[4,176,128]{2,1,0:T(8,128)(2,1)S(1)} %collective-permute-done.13.rest_3_) | copy-start | bytes 540676
  114.2 8.5 %collective-permute-start.22 = (bf16[176,128]{1,0:T(8,128)(2,1)S(1)}, bf16[176,128]{1,0:T(8,128)(2,1)S(1)}, u32[]{:S(2)}, u32[]{:S(2)}) collective-permute-start(bf16[176,128]{1,0:T(8,128)(2,1)S(1)} %get-tuple-element.68), channel_id=1, source_target_pairs={{0,2},{1,3},{2,0},{3,1},{4,6},{5,7},{6,4},{7,5},{8,10},{9,11},{10,... | collective-permute-start | bytes 135176 | tf_op jit(solution)/shard_map/ppermute | solution.py:444
  117.0 49.3 %copy-start.6 = (bf16[4,176,128]{2,1,0:T(8,128)(2,1)}, bf16[4,176,128]{2,1,0:T(8,128)(2,1)S(1)}, u32[]{:S(2)}) copy-start(bf16[4,176,128]{2,1,0:T(8,128)(2,1)S(1)} %collective-permute-done.14.rest_4_) | copy-start | bytes 540676
  117.0 5.7 %collective-permute-start.23 = (bf16[176,128]{1,0:T(8,128)(2,1)S(1)}, bf16[176,128]{1,0:T(8,128)(2,1)S(1)}, u32[]{:S(2)}, u32[]{:S(2)}) collective-permute-start(bf16[176,128]{1,0:T(8,128)(2,1)S(1)} %get-tuple-element.67), channel_id=1, source_target_pairs={{0,3},{1,2},{2,1},{3,0},{4,7},{5,6},{6,5},{7,4},{8,11},{9,10},{10,... | collective-permute-start | bytes 135176 | tf_op jit(solution)/shard_map/ppermute | solution.py:444
  117.3 23.4 %collective-permute-start.17 = (bf16[3,176,128]{2,1,0:T(8,128)(2,1)S(1)}, bf16[3,176,128]{2,1,0:T(8,128)(2,1)S(1)}, u32[]{:S(2)}, u32[]{:S(2)}) collective-permute-start(bf16[3,176,128]{2,1,0:T(8,128)(2,1)S(1)} %copy-done.30), channel_id=1, source_target_pairs={{0,144},{4,148},{8,152},{12,156},{16,160},{20,164},{24,168},{28,17... | collective-permute-start | bytes 405512 | tf_op jit(solution)/shard_map/ppermute | solution.py:415
  122.8 3.7 %collective-permute-start.24 = (bf16[176,128]{1,0:T(8,128)(2,1)S(1)}, bf16[176,128]{1,0:T(8,128)(2,1)S(1)}, u32[]{:S(2)}, u32[]{:S(2)}) collective-permute-start(bf16[176,128]{1,0:T(8,128)(2,1)S(1)} %fusion.3), channel_id=1, source_target_pairs={{0,64},{4,68},{8,72},{12,76},{16,80},{20,84},{24,88},{28,92},{32,9... | collective-permute-start | bytes 135176 | tf_op jit(solution)/shard_map/ppermute | solution.py:441
  125.1 4.6 %collective-permute-start.25 = (bf16[176,128]{1,0:T(8,128)(2,1)S(1)}, bf16[176,128]{1,0:T(8,128)(2,1)S(1)}, u32[]{:S(2)}, u32[]{:S(2)}) collective-permute-start(bf16[176,128]{1,0:T(8,128)(2,1)S(1)} %fusion.3), channel_id=1, source_target_pairs={{0,128},{4,132},{8,136},{12,140},{16,144},{20,148},{24,152},{28,15... | collective-permute-start | bytes 135176 | tf_op jit(solution)/shard_map/ppermute | solution.py:441
  125.3 41.0 %copy-start.10 = (bf16[3,176,128]{2,1,0:T(8,128)(2,1)}, bf16[3,176,128]{2,1,0:T(8,128)(2,1)S(1)}, u32[]{:S(2)}) copy-start(bf16[3,176,128]{2,1,0:T(8,128)(2,1)S(1)} %collective-permute-done.15.rest_5_) | copy-start | bytes 405508
  125.3 4.3 %collective-permute-start.26 = (bf16[176,128]{1,0:T(8,128)(2,1)S(1)}, bf16[176,128]{1,0:T(8,128)(2,1)S(1)}, u32[]{:S(2)}, u32[]{:S(2)}) collective-permute-start(bf16[176,128]{1,0:T(8,128)(2,1)S(1)} %fusion.3), channel_id=1, source_target_pairs={{0,192},{4,196},{8,200},{12,204},{16,208},{20,212},{24,216},{28,22... | collective-permute-start | bytes 135176 | tf_op jit(solution)/shard_map/ppermute | solution.py:441
  129.7 3.3 %collective-permute-start.27 = (bf16[176,128]{1,0:T(8,128)(2,1)S(1)}, bf16[176,128]{1,0:T(8,128)(2,1)S(1)}, u32[]{:S(2)}, u32[]{:S(2)}) collective-permute-start(bf16[176,128]{1,0:T(8,128)(2,1)S(1)} %add_convert_fusion.2), channel_id=1, source_target_pairs={{0,8},{4,12},{8,0},{12,4},{16,24},{20,28},{24,16},{28,20},{32,40},... | collective-permute-start | bytes 135176 | tf_op jit(solution)/shard_map/ppermute | solution.py:441
  129.8 36.5 %copy-start.7 = (bf16[4,176,128]{2,1,0:T(8,128)(2,1)}, bf16[4,176,128]{2,1,0:T(8,128)(2,1)S(1)}, u32[]{:S(2)}) copy-start(bf16[4,176,128]{2,1,0:T(8,128)(2,1)S(1)} %collective-permute-done.16.rest_6_) | copy-start | bytes 540676
  133.0 17.1 %collective-permute-start.28 = (bf16[176,128]{1,0:T(8,128)(2,1)S(1)}, bf16[176,128]{1,0:T(8,128)(2,1)S(1)}, u32[]{:S(2)}, u32[]{:S(2)}) collective-permute-start(bf16[176,128]{1,0:T(8,128)(2,1)S(1)} %add_convert_fusion.1), channel_id=1, source_target_pairs={{0,16},{4,20},{8,24},{12,28},{16,0},{20,4},{24,8},{28,12},{32,48},... | collective-permute-start | bytes 135176 | tf_op jit(solution)/shard_map/ppermute | solution.py:441
  137.4 12.7 %collective-permute-start.29 = (bf16[176,128]{1,0:T(8,128)(2,1)S(1)}, bf16[176,128]{1,0:T(8,128)(2,1)S(1)}, u32[]{:S(2)}, u32[]{:S(2)}) collective-permute-start(bf16[176,128]{1,0:T(8,128)(2,1)S(1)} %add_convert_fusion.1), channel_id=1, source_target_pairs={{0,32},{4,36},{8,40},{12,44},{16,48},{20,52},{24,56},{28,60},{32,0... | collective-permute-start | bytes 135176 | tf_op jit(solution)/shard_map/ppermute | solution.py:441
  139.1 10.9 %collective-permute-start.30 = (bf16[176,128]{1,0:T(8,128)(2,1)S(1)}, bf16[176,128]{1,0:T(8,128)(2,1)S(1)}, u32[]{:S(2)}, u32[]{:S(2)}) collective-permute-start(bf16[176,128]{1,0:T(8,128)(2,1)S(1)} %add_convert_fusion.1), channel_id=1, source_target_pairs={{0,48},{4,52},{8,56},{12,60},{16,32},{20,36},{24,40},{28,44},{32,1... | collective-permute-start | bytes 135176 | tf_op jit(solution)/shard_map/ppermute | solution.py:441
  140.7 25.6 %copy-start.11 = (bf16[3,176,128]{2,1,0:T(8,128)(2,1)}, bf16[3,176,128]{2,1,0:T(8,128)(2,1)S(1)}, u32[]{:S(2)}) copy-start(bf16[3,176,128]{2,1,0:T(8,128)(2,1)S(1)} %collective-permute-done.17.rest_7_) | copy-start | bytes 405508
  140.8 25.5 %collective-permute-start.18 = (bf16[10,176,128]{2,1,0:T(8,128)(2,1)S(1)}, bf16[10,176,128]{2,1,0:T(8,128)(2,1)S(1)}, u32[]{:S(2)}, u32[]{:S(2)}) collective-permute-start(bf16[10,176,128]{2,1,0:T(8,128)(2,1)S(1)} %get-tuple-element.86), channel_id=1, source_target_pairs={{4,0},{8,4},{12,8},{20,16},{24,20},{28,24},{36,32},{40,36},{44,40}... | collective-permute-start | bytes 1351688 | tf_op jit(solution)/shard_map/ppermute | solution.py:422
  148.8 17.5 %collective-permute-start.19 = (bf16[10,176,128]{2,1,0:T(8,128)(2,1)S(1)}, bf16[10,176,128]{2,1,0:T(8,128)(2,1)S(1)}, u32[]{:S(2)}, u32[]{:S(2)}) collective-permute-start(bf16[10,176,128]{2,1,0:T(8,128)(2,1)S(1)} %get-tuple-element.85), channel_id=1, source_target_pairs={{0,4},{4,8},{8,12},{16,20},{20,24},{24,28},{32,36},{36,40},{40,44}... | collective-permute-start | bytes 1351688 | tf_op jit(solution)/shard_map/ppermute | solution.py:422
  150.1 4.5 %collective-permute-start.31 = (bf16[176,128]{1,0:T(8,128)(2,1)S(1)}, bf16[176,128]{1,0:T(8,128)(2,1)S(1)}, u32[]{:S(2)}, u32[]{:S(2)}) collective-permute-start(bf16[176,128]{1,0:T(8,128)(2,1)S(1)} %add_convert_fusion), channel_id=1, source_target_pairs={{0,1},{1,0},{2,3},{3,2},{4,5},{5,4},{6,7},{7,6},{8,9},{9,8},{10,11... | collective-permute-start | bytes 135176 | tf_op jit(solution)/shard_map/ppermute | solution.py:444
  150.9 5.7 %collective-permute-start.32 = (bf16[176,128]{1,0:T(8,128)(2,1)S(1)}, bf16[176,128]{1,0:T(8,128)(2,1)S(1)}, u32[]{:S(2)}, u32[]{:S(2)}) collective-permute-start(bf16[176,128]{1,0:T(8,128)(2,1)S(1)} %add_convert_fusion), channel_id=1, source_target_pairs={{0,2},{1,3},{2,0},{3,1},{4,6},{5,7},{6,4},{7,5},{8,10},{9,11},{10,... | collective-permute-start | bytes 135176 | tf_op jit(solution)/shard_map/ppermute | solution.py:444
  154.6 4.2 %collective-permute-start.33 = (bf16[176,128]{1,0:T(8,128)(2,1)S(1)}, bf16[176,128]{1,0:T(8,128)(2,1)S(1)}, u32[]{:S(2)}, u32[]{:S(2)}) collective-permute-start(bf16[176,128]{1,0:T(8,128)(2,1)S(1)} %add_convert_fusion), channel_id=1, source_target_pairs={{0,3},{1,2},{2,1},{3,0},{4,7},{5,6},{6,5},{7,4},{8,11},{9,10},{10,... | collective-permute-start | bytes 135176 | tf_op jit(solution)/shard_map/ppermute | solution.py:444
  158.9 4.3 %copy-start.1 = (bf16[4,176,128]{2,1,0:T(8,128)(2,1)}, bf16[4,176,128]{2,1,0:T(8,128)(2,1)S(1)}, u32[]{:S(2)}) copy-start(bf16[4,176,128]{2,1,0:T(8,128)(2,1)S(1)} %pad_maximum_fusion.2.refs_1_) | copy-start | bytes 540676
  158.9 4.3 %collective-permute-start.34 = (bf16[4,176,128]{2,1,0:T(8,128)(2,1)S(1)}, bf16[4,176,128]{2,1,0:T(8,128)(2,1)S(1)}, u32[]{:S(2)}, u32[]{:S(2)}) collective-permute-start(bf16[4,176,128]{2,1,0:T(8,128)(2,1)S(1)} %pad_maximum_fusion.2.refs_1_), channel_id=1, source_target_pairs={{0,4},{4,0},{8,12},{12,8},{16,20},{20,16},{24,28},{28,24},{32,36},... | collective-permute-start | bytes 540680 | tf_op jit(solution)/shard_map/ppermute | solution.py:441
  166.3 0.8 copy-start.2
  166.3 0.9 copy-start.3
  (2 other events, 1.4 us)

commit v2 on v1

--- a/solution.py
+++ b/solution.py
@@ -23,16 +23,17 @@
 
 X_LO, X_HI, Y_LO, Y_HI, Z_AT = 0, 32, 64, 96, 128
 
-PLANE = [(a, b) for a in (-1, 0, 1) for b in (-1, 0, 1) if (a, b) != (0, 0)]
+PLANE = [(1, 1), (1, 0), (1, -1), (0, 1), (0, -1), (-1, 1), (-1, 0), (-1, -1)]
 
 
 def slots_of(a, b, c):
     return 2 if abs(a) + abs(b) + abs(c) == 1 else 1
 
 
-def plane_items(a, b):
-    own = [(a, b, 0, s) for s in range(slots_of(a, b, 0))]
-    return own + [(a, b, -1, 0), (a, b, 1, 0)]
+def plane_items(u, w, by):
+    a, b, near = u * by[0], w * by[1], by[2]
+    own = [(a, b, 0, s) for s in range(slots_of(u, w, 0))]
+    return own + [(a, b, near, 0), (a, b, -near, 0)]
 
 
 def place(a, b, c):
@@ -44,12 +45,16 @@
     return (q % 2) * 2 + q // 2, (d // 4) % 4, d % 4
 
 
-def shift_pairs(count, a, b, c):
+def steps(d):
+    return tuple(1 - 2 * (r % 2) for r in region(d))
+
+
+def swap_pairs(count, u, w):
     where = {region(d): d for d in range(count)}
     pairs = []
     for d in range(count):
-        r = region(d)
-        to = (r[0] + a, r[1] + b, r[2] + c)
+        r, by = region(d), steps(d)
+        to = (r[0] + u * by[0], r[1] + w * by[1], r[2])
         if to in where:
             pairs.append((d, where[to]))
     return pairs
@@ -85,8 +90,25 @@
 
 
 def spread_mask(voxels, width):
-    hit = iota((8, LANES), 1) // width == iota((8, LANES), 0) // (width // 64)
+    hit = iota((128, LANES), 1) // width == iota((128, LANES), 0) // (width // 64)
     return dot(voxels, hit.astype(F32).astype(BF16))
+
+
+def voxel_rows(mask_ref, permuted):
+    deep = (iota((LANES, 128), 0) % 8 == iota((LANES, 128), 1)).astype(F32).astype(BF16)
+    masks = [mask_ref[b].astype(F32) for b in range(BD)]
+    pieces = []
+    if permuted:
+        row, lane = iota((16, LANES), 0), iota((16, LANES), 1) // 8
+        for q in range(4):
+            mine = (2 * (row // 4) + q // 2) * 8 + 2 * (row % 4) + q % 2 == lane
+            for b in range(BD):
+                pieces.append(jnp.where(mine, jnp.broadcast_to(masks[b], (16, LANES)), 0.0))
+    else:
+        mine = iota((ROWS, LANES), 0) == iota((ROWS, LANES), 1) // 8
+        for b in range(BD):
+            pieces.append(jnp.where(mine, jnp.broadcast_to(masks[b], (ROWS, LANES)), 0.0))
+    return dot(jnp.concatenate(pieces, axis=0).astype(BF16), deep).astype(BF16)
 
 
 def low_half(shape):
@@ -104,22 +126,30 @@
     inside = (r0 >= 0) & (r0 < SIDE) & (r1 >= 0) & (r1 < SIDE) & (r2 >= 0) & (r2 < SIDE)
     to = ((r0 % 2) * 2 + r0 // 2) * 16 + r1 * 4 + r2
     to = jnp.where(inside, to, 0)
-    got = send_ref[to * 2 + s]
+    got = send_ref[s, to]
     return jnp.clip(jnp.where(inside, got, BD), 0, BD)
 
 
-def all_items():
-    lists = [plane_items(a, b) for a, b in PLANE]
-    lists += [[(0, 0, -1, s) for s in range(2)], [(0, 0, 1, s) for s in range(2)]]
+def all_items(by=(1, 1, 1)):
+    lists = [plane_items(u, w, by) for u, w in PLANE]
+    lists += [[(0, 0, by[2], s) for s in range(2)], [(0, 0, -by[2], s) for s in range(2)]]
     return lists
 
 
-def pack_kernel(me_ref, send_ref, feat_ref, vox_ref, masked_ref, own_ref, *rest):
+def received_items(by):
+    lists = [[(u * by[0], w * by[1], 0, s) for s in range(slots_of(u, w, 0))] for u, w in PLANE]
+    for c in (by[2], -by[2]):
+        lists.append([(0, 0, c, s) for s in range(2)] + [(u * by[0], w * by[1], c, 0) for u, w in PLANE])
+    return lists
+
+
+def pack_kernel(me_ref, send_ref, feat_ref, mask_ref, masked_ref, own_ref, *rest):
     outs, held = rest[:10], rest[10]
     pick = iota((16, ROWS), 1) == (iota((16, ROWS), 0) % 8) * 8 + (iota((16, ROWS), 0) // 8) * 7
     pick = pick.astype(F32).astype(BF16)
+    voxels = voxel_rows(mask_ref, False)
     for b in range(BD):
-        keep = spread_mask(vox_ref[b * ROWS : (b + 1) * ROWS, :], 64)
+        keep = spread_mask(voxels[b * ROWS : (b + 1) * ROWS], 64)
         m = feat_ref[b].astype(F32) * keep
         mb = m.astype(BF16)
         masked_ref[b] = mb
@@ -133,7 +163,7 @@
         own_ref[b] = shell
         held[b] = shell
     held[BD] = jnp.zeros((SHELL, 128), BF16)
-    for out, items in zip(outs, all_items()):
+    for out, items in zip(outs, all_items(steps(me_ref[0]))):
         for k, item in enumerate(items):
             out[k] = held[choice(me_ref, send_ref, *item)]
 
@@ -154,7 +184,7 @@
 
 
 def main_kernel(
-    idx_ref, own_ref, masked_ref, voxp_ref, cot_ref, sel_ref, selt_ref, wf_ref, wb_ref, down_ref, *rest
+    idx_ref, me_ref, own_ref, masked_ref, mask_ref, cot_ref, sel_ref, selt_ref, wf_ref, wb_ref, down_ref, *rest
 ):
     recv = rest[:10]
     coarse_ref, center_ref, gown_ref, sums_ref = rest[10:14]
@@ -165,14 +195,10 @@
     for b in range(BD):
         ext[b] = own_ref[b].astype(F32)
     ext[EMPTY] = jnp.zeros((SHELL, 128), F32)
-    for (a, b), ref in zip(PLANE, recv):
-        for s in range(slots_of(a, b, 0)):
-            ext[BD + 2 * place(-a, -b, 0) + s] = ref[s].astype(F32)
-    for c, ref in zip((-1, 1), recv[8:]):
-        for s in range(2):
-            ext[BD + 2 * place(0, 0, -c) + s] = ref[s].astype(F32)
-        for k, (a, b) in enumerate(PLANE):
-            ext[BD + 2 * place(-a, -b, -c)] = ref[2 + k].astype(F32)
+    by = steps(me_ref[0])
+    for ref, items in zip(recv, received_items(by)):
+        for k, (a, b, c, s) in enumerate(items):
+            ext[BD + 2 * place(a, b, c) + s] = ref[k].astype(F32)
     gext[...] = jnp.zeros_like(gext)
 
     @pl.loop(0, BD)
@@ -215,7 +241,7 @@
                 for k in range(5):
                     cols[to, k * GROUP + t * 128 : k * GROUP + (t + 1) * 128] = rows[:, k * 128 : (k + 1) * 128]
 
-    voxp = voxp_ref[...]
+    voxp = voxel_rows(mask_ref, True)
     keep = spread_mask(voxp, 64)
     for p in range(4):
         pre = dot(cols[:, GROUP * p : GROUP * (p + 2)], wf_ref[...])
@@ -236,9 +262,11 @@
     pieces, parts = [], []
     for p in range(4):
         rows, lanes = slice(96 * p, 96 * (p + 1)), slice(128 * p, 128 * (p + 1))
-        pieces.append((value[rows] * active[:, lanes]).astype(BF16))
+        pieces.append(value[rows] * active[:, lanes])
         parts.append((cot_ref[:, lanes].astype(F32) * active[:, lanes] * bend[rows]).astype(BF16))
-    coarse_ref[...] = jnp.concatenate(pieces, axis=1)
+    coarse = jnp.concatenate(pieces, axis=1)
+    for k in range(BD * HALF):
+        coarse_ref[k] = coarse[HALF * k : HALF * (k + 1)].astype(BF16)
     grad_pre = jnp.concatenate(parts, axis=0)
 
     back = dot(grad_pre, down_ref[...], 1, 1)
@@ -326,12 +354,12 @@
 
     for b in range(BD):
         gown_ref[b] = gext[b]
-    for out, items in zip(outs, all_items()):
+    for out, items in zip(outs, all_items(by)):
         for k, (a, b, c, s) in enumerate(items):
             out[k] = gext[BD + 2 * place(a, b, c) + s].astype(BF16)
 
 
-def last_kernel(me_ref, send_ref, vox_ref, center_ref, gown_ref, *rest):
+def last_kernel(me_ref, send_ref, mask_ref, center_ref, gown_ref, *rest):
     recv, out_ref, acc = rest[:10], rest[10], rest[11]
     for b in range(BD):
         acc[b] = gown_ref[b]
@@ -341,17 +369,13 @@
         at = choice(me_ref, send_ref, *item)
         acc[at] = acc[at] + data.astype(F32)
 
-    for (a, b), ref in zip(PLANE, recv):
-        for s in range(slots_of(a, b, 0)):
-            add(ref[s], -a, -b, 0, s)
-    for c, ref in zip((-1, 1), recv[8:]):
-        for s in range(2):
-            add(ref[s], 0, 0, -c, s)
-        for k, (a, b) in enumerate(PLANE):
-            add(ref[2 + k], -a, -b, -c, 0)
+    for ref, items in zip(recv, received_items(steps(me_ref[0]))):
+        for k, item in enumerate(items):
+            add(ref[k], *item)
     low8 = low_half((8, 128))
+    voxels = voxel_rows(mask_ref, False)
     for b in range(BD):
-        keep = spread_mask(vox_ref[b * ROWS : (b + 1) * ROWS, :], 64)
+        keep = spread_mask(voxels[b * ROWS : (b + 1) * ROWS], 64)
         lines = []
         for x in range(8):
             blocks = []
@@ -411,16 +435,25 @@
     )(*args)
 
 
-def exchange(parts, peers):
-    got = [lax.ppermute(v, "spatial", shift_pairs(peers, a, b, 0)) for (a, b), v in zip(PLANE, parts)]
+def exchange_plane(parts, peers):
+    return [lax.ppermute(v, "spatial", swap_pairs(peers, a, b)) for (a, b), v in zip(PLANE, parts)]
+
+
+def exchange_along(got, parts, peers):
+    swaps = [[(d, d ^ 1) for d in range(peers)]]
+    swaps += [[(d, d + 1 if d % SIDE == 1 else d - 1) for d in range(peers) if d % SIDE in (1, 2)]]
     along = []
-    for n, c in enumerate((-1, 1)):
+    for n in (1, 0):
         pieces = [parts[8 + n]]
         for v in got:
             at = v.shape[0] - 2 + n
             pieces.append(v[at : at + 1])
-        along.append(lax.ppermute(jnp.concatenate(pieces, axis=0), "spatial", shift_pairs(peers, 0, 0, c)))
-    return got + along
+        along.append(lax.ppermute(jnp.concatenate(pieces, axis=0), "spatial", swaps[n]))
+    return [*got, along[1], along[0]]
+
+
+def exchange(parts, peers):
+    return exchange_along(exchange_plane(parts, peers), parts, peers)
 
 
 def pair_weights(taps, width):
@@ -431,11 +464,21 @@
     return both.transpose(1, 0, 2, 3).reshape(2 * GROUP, 2 * width)
 
 
-def reduce_sums(sums, me, x, peers):
+def after(values, earlier):
+    return lax.optimization_barrier((tuple(values), earlier))[0]
+
+
+def exchange_and_sum(parts, sums, me, x, peers):
     core = me % 2
-    halves = sums.reshape(2, 4, SHELL, 128)
-    near = lax.dynamic_index_in_dim(halves, core, 0, keepdims=False)
-    far = lax.dynamic_index_in_dim(halves, 1 - core, 0, keepdims=False)
+    got = {}
+
+    def plane(lo, hi, earlier=None):
+        keys = PLANE[lo:hi]
+        ins = [parts[PLANE.index(k)] for k in keys]
+        if earlier is not None:
+            ins = after(ins, earlier)
+        for k, v in zip(keys, ins):
+            got[k] = lax.ppermute(v, "spatial", swap_pairs(peers, *k))
 
     def swap(v, bit):
         return lax.ppermute(v, "spatial", [(d, d ^ bit) for d in range(peers)])
@@ -443,26 +486,31 @@
     def swap_x(v, bit):
         return lax.ppermute(v, "dp", [(d, d ^ bit) for d in range(4)])
 
-    mine = near + swap(far.astype(BF16), 1).astype(F32)
+    def one_of(v, at):
+        return lax.dynamic_index_in_dim(v, at, 0, keepdims=False)
+
+    def pairs(w, bits):
+        all_of = [w.astype(F32)] + [swap(w, bit).astype(F32) for bit in bits]
+        while len(all_of) > 1:
+            all_of = [all_of[i] + all_of[i + 1] for i in range(0, len(all_of), 2)]
+        return all_of[0].astype(BF16)
+
+    halves = sums.reshape(2, 4, SHELL, 128)
+    plane(0, 4)
+    mine = one_of(halves, core) + swap(one_of(halves, 1 - core).astype(BF16), 1).astype(F32)
     small = mine.astype(BF16)
-    v = lax.dynamic_index_in_dim(mine, x, 0, keepdims=False)
+    away = [one_of(small, jnp.bitwise_xor(x, k)) for k in (1, 2, 3)]
+    plane(4, 8, tuple(away))
+    v = one_of(mine, x)
     for k in (1, 2, 3):
-        part = lax.dynamic_index_in_dim(small, jnp.bitwise_xor(x, k), 0, keepdims=False)
-        v = v + swap_x(part, k).astype(F32)
-
-    def pairs(v, bits):
-        w = v.astype(BF16)
-        got = [w.astype(F32)] + [swap(w, bit).astype(F32) for bit in bits]
-        while len(got) > 1:
-            got = [got[i] + got[i + 1] for i in range(0, len(got), 2)]
-        return got[0]
-
-    v = pairs(v, (16, 32, 48))
-    v = pairs(v, (2,))
-    v = pairs(v, (4, 8, 12))
+        v = v + swap_x(away[k - 1], k).astype(F32)
     w = v.astype(BF16)
+    w = pairs(w, (16, 32, 48))
+    w = pairs(w, (2,))
+    w = pairs(w, (4, 8, 12))
     near = jnp.stack([w] + [swap_x(w, k) for k in (1, 2, 3)])
-    return near, swap(near, 1)
+    came = exchange_along([got[k] for k in PLANE], parts, peers)
+    return came, near, swap(near, 1)
 
 
 def shards(features, masks, rulebook, send_lists, conv_weight, down_weight, cotangent):
@@ -470,17 +518,16 @@
     me = lax.axis_index("spatial").astype(jnp.int32)
     x = lax.axis_index("dp").astype(jnp.int32)
     me_s = me.reshape(1)
-    sends = send_lists.reshape(peers * 2)
+    sends = send_lists[0, 0].T
     feat = features.reshape(BD, ROWS, LANES)
     cot = cotangent.reshape(BD * 16, LANES)
-    vox = masks.reshape(BD * ROWS, 8).astype(BF16)
-    voxp = vox.reshape(BD, 4, 2, 4, 2, 8).transpose(2, 4, 0, 1, 3, 5).reshape(BD * ROWS, 8)
+    mask = masks.reshape(BD, 1, ROWS * EDGE)
 
     brick = jax.ShapeDtypeStruct((BD, ROWS, LANES), BF16)
     parts = [jax.ShapeDtypeStruct((len(items), SHELL, 128), BF16) for items in all_items()]
     held = pltpu.VMEM((BD + 1, SHELL, 128), BF16)
     own_shape = jax.ShapeDtypeStruct((BD, SHELL, 128), BF16)
-    masked, own, *sent = call(pack_kernel, [brick, own_shape, *parts], [me_s, sends, feat, vox], 2, [held])
+    masked, own, *sent = call(pack_kernel, [brick, own_shape, *parts], [me_s, sends, feat, mask], 2, [held])
     recv = exchange(sent, peers)
 
     entry = rulebook.reshape(BD * 27)
@@ -499,7 +546,7 @@
     down = down_weight.reshape(512, 128)
     sel, selt = (jnp.asarray(v, BF16) for v in selections())
     outs = [
-        jax.ShapeDtypeStruct((BD * 16, LANES), BF16),
+        jax.ShapeDtypeStruct((BD * HALF, HALF, LANES), BF16),
         jax.ShapeDtypeStruct((BD, ROWS, LANES), F32),
         jax.ShapeDtypeStruct((BD, SHELL, 128), F32),
         jax.ShapeDtypeStruct((8 * SHELL, 128), F32),
@@ -517,14 +564,13 @@
         pltpu.VMEM((BD * PADR, PADL), F32),
     ]
     coarse, center, gown, sums, *back = call(
-        main_kernel, outs, [idx, own, masked, voxp, cot, sel, selt, wf, wb, down, *recv], 1, scratch, 10**10
+        main_kernel, outs, [idx, me_s, own, masked, mask, cot, sel, selt, wf, wb, down, *recv], 2, scratch, 10**10
     )
-    came = exchange(back, peers)
-    near, far = reduce_sums(sums, me, x, peers)
+    came, near, far = exchange_and_sum(back, sums, me, x, peers)
     [grad] = call(
         last_kernel,
         [brick],
-        [me_s, sends, vox, center, gown, *came],
+        [me_s, sends, mask, center, gown, *came],
         2,
         [pltpu.VMEM((BD + 1, SHELL, 128), F32)],
     )
@@ -533,7 +579,7 @@
     conv_sum, down_sum = call(
         lambda *refs: finish_kernel(scale, *refs),
         [jax.ShapeDtypeStruct((27, 64, 64), F32), jax.ShapeDtypeStruct((8, 64, 128), F32)],
-        [spot, near, far],
+        [spot, near, *after([far], grad)],
         1,
         [pltpu.VMEM((8, SHELL, 128), F32)],
     )

time: 172 us -> 149 us (0.87)
  starting transfers between devices: 103 us -> 84.6 us
  local copies, waits for them, and re-layouts: 21.8 us -> 18.3 us
    ppermute x20, starting transfers between devices: 77.3 us -> 56 us  [the longest x8 25.6 us: plane(): got[k] = lax.ppermute(v, 'spatial', swap_pairs(peers, *k))]
    ppermute x9, starting transfers between devices: 17.1 us -> 20.7 us  [swap(): return lax.ppermute(v, 'spatial', [(d, d ^ bit) for d in range(peers)])]
    ppermute x9, waiting for transfers between devices: 6.44 us -> 3.29 us  [swap(): return lax.ppermute(v, 'spatial', [(d, d ^ bit) for d in range(peers)])]
    ppermute x6, waiting for transfers between devices: 4.25 us -> 6.66 us  [swap_x(): return lax.ppermute(v, 'dp', [(d, d ^ bit) for d in range(4)])]
    unnamed x80 -> x81, local copies, waits for them, and re-layouts: 9.79 us -> 9.26 us
  transfers between devices with their start and end apart: 35 -> 35, of which waited for: 6 -> 6; matrix products, arithmetic and copies ran while one was open for 11% -> 12% of each run, Pallas kernels for 1% -> 2%
where the time goes in v2:
time: 149 us
  starting transfers between devices  84.6 us (57%)
  Pallas kernels  29.2 us (20%)
  local copies, waits for them, and re-layouts  18.3 us (12%)
  waiting for transfers between devices  12.2 us (8%)
  other arithmetic  2.97 us (2%)
    pallas_call x4, Pallas kernels, call(): pl.pallas_call(kernel, out_shape=outs, in_specs=[spec_s] * smem + [spec_v...  29.2 us
    ppermute x8, starting transfers between devices, plane(): got[k] = lax.ppermute(v, 'spatial', swap_pairs(peers, *k))  25.6 us
    ppermute x8, starting transfers between devices, exchange_plane(): lax.ppermute(v, 'spatial', swap_pairs(peers, a, b))  21.5 us
    ppermute x9, starting transfers between devices, swap(): return lax.ppermute(v, 'spatial', [(d, d ^ bit) for d in range(peers)])  20.7 us
    unnamed x81, local copies, waits for them, and re-layouts  9.26 us
    ppermute x4, starting transfers between devices, exchange_along(): lax.ppermute(jnp.concatenate(pieces, axis=0), 'spatial', swaps[n])  8.83 us
    ppermute x6, starting transfers between devices, swap_x(): return lax.ppermute(v, 'dp', [(d, d ^ bit) for d in range(4)])  7.88 us
    ppermute x6, waiting for transfers between devices, swap_x(): return lax.ppermute(v, 'dp', [(d, d ^ bit) for d in range(4)])  6.66 us
  transfers between devices with their start and end apart: 35, of which 6 were waited for; matrix products, arithmetic and copies ran while one was open for 12% of the time, Pallas kernels for 2%

profile of v2, /device:TPU:41, one launch (start us, length us, event | category | flops | bytes accessed | tf_op | source)
XLA Modules:
  0.0 148.6 jit_solution(2590538075596999061)
XLA Ops:
  0.6 3.6 %shard_map.120 = (bf16[6,64,512]{2,1,0:T(8,128)(2,1)}, bf16[6,176,128]{2,1,0:T(8,128)(2,1)}, bf16[3,176,128]{2,1,0:T(8,128)(2,1)}, bf16[4,176,128]{2,1,0:T(8,128...) custom-call(s32[1]{0:T(128)} %bitcast.me_ref, ...), custom_call_target="tpu_custom_call" | custom-call | bytes 2511364 | tf_op jit(solution)/shard_map/pallas_call | solution.py:427
  4.3 4.8 %collective-permute-start = (bf16[3,176,128]{2,1,0:T(8,128)(2,1)}, bf16[3,176,128]{2,1,0:T(8,128)(2,1)S(1)}, u32[]{:S(2)}, u32[]{:S(2)}) collective-permute-start(bf16[3,176,128]{2,1,0:T(8,128)(2,1)} %get-tuple-element.39), channel_id=1, source_target_pairs={{0,144},{4,148},{8,152},{12,156},{16,128},{20,132},{24,136},{28,14... | collective-permute-start | bytes 405512 | tf_op jit(solution)/shard_map/ppermute | solution.py:439
  9.0 1.0 collective-permute-start.1
  10.0 0.7 collective-permute-start.2
  10.6 7.6 %collective-permute-start.3 = (bf16[4,176,128]{2,1,0:T(8,128)(2,1)}, bf16[4,176,128]{2,1,0:T(8,128)(2,1)S(1)}, u32[]{:S(2)}, u32[]{:S(2)}) collective-permute-start(bf16[4,176,128]{2,1,0:T(8,128)(2,1)} %get-tuple-element.42), channel_id=1, source_target_pairs={{0,16},{4,20},{8,24},{12,28},{16,0},{20,4},{24,8},{28,12},{32,48},... | collective-permute-start | bytes 540680 | tf_op jit(solution)/shard_map/ppermute | solution.py:439
  18.2 0.7 collective-permute-start.4
  18.9 1.0 reverse_bitcast_fusion
  21.0 0.9 copy.22
  21.9 0.5 reshape.59
  22.5 0.9 copy.23
  23.4 0.7 constant_dynamic-update-slice_fusion.8
  24.1 2.5 %collective-permute-start.5 = (bf16[3,176,128]{2,1,0:T(8,128)(2,1)S(1)}, bf16[3,176,128]{2,1,0:T(8,128)(2,1)S(1)}, u32[]{:S(2)}, u32[]{:S(2)}) collective-permute-start(bf16[3,176,128]{2,1,0:T(8,128)(2,1)S(1)} %copy-done.29), channel_id=1, source_target_pairs={{64,144},{68,148},{72,152},{76,156},{80,128},{84,132},{88,136},{92... | collective-permute-start | bytes 405512 | tf_op jit(solution)/shard_map/ppermute | solution.py:439
  26.5 0.6 constant_dynamic-update-slice_fusion.16
  27.2 3.8 %collective-permute-start.6 = (bf16[4,176,128]{2,1,0:T(8,128)(2,1)S(1)}, bf16[4,176,128]{2,1,0:T(8,128)(2,1)S(1)}, u32[]{:S(2)}, u32[]{:S(2)}) collective-permute-start(bf16[4,176,128]{2,1,0:T(8,128)(2,1)S(1)} %copy-done.25), channel_id=1, source_target_pairs={{64,128},{68,132},{72,136},{76,140},{80,144},{84,148},{88,152},{92... | collective-permute-start | bytes 540680 | tf_op jit(solution)/shard_map/ppermute | solution.py:439
  31.0 0.6 constant_dynamic-update-slice_fusion.15
  31.6 0.7 collective-permute-start.7
  32.3 0.6 constant_dynamic-update-slice_fusion.14
  33.0 0.7 constant_dynamic-update-slice_fusion.13
  33.7 0.7 constant_dynamic-update-slice_fusion.12
  34.3 0.7 constant_dynamic-update-slice_fusion.11
  35.0 2.2 %collective-permute-done.6.rest_6_ = bf16[4,176,128]{2,1,0:T(8,128)(2,1)S(1)} collective-permute-done((bf16[4,176,128]{2,1,0:T(8,128)(2,1)S(1)}, bf16[4,176,128]{2,1,0:T(8,128)(2,1)S(1)}, u32[]{:S(2)}, u32[]{:S(2)}) %collective-permute-start.6) | collective-permute-done | bytes 180256 | tf_op jit(solution)/shard_map/ppermute | solution.py:439
  37.2 0.7 constant_dynamic-update-slice_fusion.10
  37.9 0.7 constant_dynamic-update-slice_fusion.9
  38.6 0.9 collective-permute-start.8
  39.4 1.4 collective-permute-start.9
  41.5 1.2 copy.18
  42.7 0.5 reshape.57
  43.3 0.9 copy.19
  44.2 0.7 reshape.55.cot_ref
  44.8 0.6 fusion.15.idx_ref
  45.4 19.9 %shard_map.121 = (bf16[24,4,512]{2,1,0:T(4,128)(2,1)}, f32[6,64,512]{2,1,0:T(8,128)}, f32[6,176,128]{2,1,0:T(8,128)}, f32[1408,128]{1,0:T(8,128)}, bf16[3,176,12...) custom-call(s32[162]{0:T(256)} %fusion.15.idx_ref, ...), custom_call_target="tpu_custom_call" | custom-call | flops 10000000000 | bytes 8094348 | tf_op jit(solution)/shard_map/pallas_call | solution.py:427
  65.3 1.1 fusion
  66.4 4.1 %collective-permute-start.14 = (bf16[4,176,128]{2,1,0:T(8,128)(2,1)S(1)}, bf16[4,176,128]{2,1,0:T(8,128)(2,1)S(1)}, u32[]{:S(2)}, u32[]{:S(2)}) collective-permute-start(bf16[4,176,128]{2,1,0:T(8,128)(2,1)S(1)} %fusion), channel_id=1, source_target_pairs={{0,4},{4,0},{8,12},{12,8},{16,20},{20,16},{24,28},{28,24},{32,36},... | collective-permute-start | bytes 540680 | tf_op jit(solution)/shard_map/ppermute | solution.py:484
  70.5 0.9 constant_dynamic-update-slice_fusion.26
  71.4 9.9 %collective-permute-start.11 = (bf16[4,176,128]{2,1,0:T(8,128)(2,1)}, bf16[4,176,128]{2,1,0:T(8,128)(2,1)S(1)}, u32[]{:S(2)}, u32[]{:S(2)}) collective-permute-start(bf16[4,176,128]{2,1,0:T(8,128)(2,1)} %get-tuple-element.53), channel_id=1, source_target_pairs={{0,128},{4,132},{8,136},{12,140},{16,144},{20,148},{24,152},{28,15... | collective-permute-start | bytes 540680 | tf_op jit(solution)/shard_map/ppermute | solution.py:481
  81.3 0.7 collective-permute-start.12
  81.9 3.5 %collective-permute-start.13 = (bf16[4,176,128]{2,1,0:T(8,128)(2,1)}, bf16[4,176,128]{2,1,0:T(8,128)(2,1)S(1)}, u32[]{:S(2)}, u32[]{:S(2)}) collective-permute-start(bf16[4,176,128]{2,1,0:T(8,128)(2,1)} %get-tuple-element.55), channel_id=1, source_target_pairs={{0,16},{4,20},{8,24},{12,28},{16,0},{20,4},{24,8},{28,12},{32,48},... | collective-permute-start | bytes 540680 | tf_op jit(solution)/shard_map/ppermute | solution.py:481
  85.4 0.9 constant_dynamic-update-slice_fusion.35
  86.4 1.1 fusion.16
  87.5 1.3 collective-permute-start.21
  88.8 2.5 %collective-permute-start.22 = (bf16[176,128]{1,0:T(8,128)(2,1)S(1)}, bf16[176,128]{1,0:T(8,128)(2,1)S(1)}, u32[]{:S(2)}, u32[]{:S(2)}) collective-permute-start(bf16[176,128]{1,0:T(8,128)(2,1)S(1)} %get-tuple-element.85), channel_id=1, source_target_pairs={{0,2},{1,3},{2,0},{3,1},{4,6},{5,7},{6,4},{7,5},{8,10},{9,11},{10,... | collective-permute-start | bytes 135176 | tf_op jit(solution)/shard_map/ppermute | solution.py:487
  91.5 0.7 collective-permute-start.15
  92.2 1.0 collective-permute-done.22
  93.2 2.2 %collective-permute-done.23 = bf16[176,128]{1,0:T(8,128)(2,1)S(1)} collective-permute-done((bf16[176,128]{1,0:T(8,128)(2,1)S(1)}, bf16[176,128]{1,0:T(8,128)(2,1)S(1)}, u32[]{:S(2)}, u32[]{:S(2)}) %collective-permute-start.23) | collective-permute-done | bytes 45088 | tf_op jit(solution)/shard_map/ppermute | solution.py:487
  95.8 4.2 %collective-permute-start.25 = (bf16[176,128]{1,0:T(8,128)(2,1)S(1)}, bf16[176,128]{1,0:T(8,128)(2,1)S(1)}, u32[]{:S(2)}, u32[]{:S(2)}) collective-permute-start(bf16[176,128]{1,0:T(8,128)(2,1)S(1)} %fusion.3), channel_id=1, source_target_pairs={{0,128},{4,132},{8,136},{12,140},{16,144},{20,148},{24,152},{28,15... | collective-permute-start | bytes 135176 | tf_op jit(solution)/shard_map/ppermute | solution.py:484
  100.3 6.7 %collective-permute-start.16 = (bf16[3,176,128]{2,1,0:T(8,128)(2,1)S(1)}, bf16[3,176,128]{2,1,0:T(8,128)(2,1)S(1)}, u32[]{:S(2)}, u32[]{:S(2)}) collective-permute-start(bf16[3,176,128]{2,1,0:T(8,128)(2,1)S(1)} %copy-done.31), channel_id=1, source_target_pairs={{64,144},{68,148},{72,152},{76,156},{80,128},{84,132},{88,136},{92... | collective-permute-start | bytes 405512 | tf_op jit(solution)/shard_map/ppermute | solution.py:481
  107.0 3.6 %collective-permute-start.17 = (bf16[4,176,128]{2,1,0:T(8,128)(2,1)S(1)}, bf16[4,176,128]{2,1,0:T(8,128)(2,1)S(1)}, u32[]{:S(2)}, u32[]{:S(2)}) collective-permute-start(bf16[4,176,128]{2,1,0:T(8,128)(2,1)S(1)} %copy-done.26), channel_id=1, source_target_pairs={{64,128},{68,132},{72,136},{76,140},{80,144},{84,148},{88,152},{92... | collective-permute-start | bytes 540680 | tf_op jit(solution)/shard_map/ppermute | solution.py:481
  110.5 0.7 collective-permute-start.18
  111.4 3.3 %collective-permute-done.27 = bf16[176,128]{1,0:T(8,128)(2,1)S(1)} collective-permute-done((bf16[176,128]{1,0:T(8,128)(2,1)S(1)}, bf16[176,128]{1,0:T(8,128)(2,1)S(1)}, u32[]{:S(2)}, u32[]{:S(2)}) %collective-permute-start.27) | collective-permute-done | bytes 45088 | tf_op jit(solution)/shard_map/ppermute | solution.py:484
  114.7 3.0 %collective-permute-start.28 = (bf16[176,128]{1,0:T(8,128)(2,1)S(1)}, bf16[176,128]{1,0:T(8,128)(2,1)S(1)}, u32[]{:S(2)}, u32[]{:S(2)}) collective-permute-start(bf16[176,128]{1,0:T(8,128)(2,1)S(1)} %add_convert_fusion.1), channel_id=1, source_target_pairs={{0,16},{4,20},{8,24},{12,28},{16,0},{20,4},{24,8},{28,12},{32,48},... | collective-permute-start | bytes 135176 | tf_op jit(solution)/shard_map/ppermute | solution.py:484
  117.7 1.8 %collective-permute-start.29 = (bf16[176,128]{1,0:T(8,128)(2,1)S(1)}, bf16[176,128]{1,0:T(8,128)(2,1)S(1)}, u32[]{:S(2)}, u32[]{:S(2)}) collective-permute-start(bf16[176,128]{1,0:T(8,128)(2,1)S(1)} %add_convert_fusion.1), channel_id=1, source_target_pairs={{0,32},{4,36},{8,40},{12,44},{16,48},{20,52},{24,56},{28,60},{32,0... | collective-permute-start | bytes 135176 | tf_op jit(solution)/shard_map/ppermute | solution.py:484
  119.6 1.7 %collective-permute-start.30 = (bf16[176,128]{1,0:T(8,128)(2,1)S(1)}, bf16[176,128]{1,0:T(8,128)(2,1)S(1)}, u32[]{:S(2)}, u32[]{:S(2)}) collective-permute-start(bf16[176,128]{1,0:T(8,128)(2,1)S(1)} %add_convert_fusion.1), channel_id=1, source_target_pairs={{0,48},{4,52},{8,56},{12,60},{16,32},{20,36},{24,40},{28,44},{32,1... | collective-permute-start | bytes 135176 | tf_op jit(solution)/shard_map/ppermute | solution.py:484
  121.4 5.8 %collective-permute-start.19 = (bf16[10,176,128]{2,1,0:T(8,128)(2,1)S(1)}, bf16[10,176,128]{2,1,0:T(8,128)(2,1)S(1)}, u32[]{:S(2)}, u32[]{:S(2)}) collective-permute-start(bf16[10,176,128]{2,1,0:T(8,128)(2,1)S(1)} %get-tuple-element.96), channel_id=1, source_target_pairs={{0,4},{4,0},{8,12},{12,8},{16,20},{20,16},{24,28},{28,24},{32,36},... | collective-permute-start | bytes 1351688 | tf_op jit(solution)/shard_map/ppermute | solution.py:451
  127.2 0.7 collective-permute-start.20
  128.1 3.2 %collective-permute-start.32 = (bf16[176,128]{1,0:T(8,128)(2,1)S(1)}, bf16[176,128]{1,0:T(8,128)(2,1)S(1)}, u32[]{:S(2)}, u32[]{:S(2)}) collective-permute-start(bf16[176,128]{1,0:T(8,128)(2,1)S(1)} %add_convert_fusion), channel_id=1, source_target_pairs={{0,2},{1,3},{2,0},{3,1},{4,6},{5,7},{6,4},{7,5},{8,10},{9,11},{10,... | collective-permute-start | bytes 135176 | tf_op jit(solution)/shard_map/ppermute | solution.py:487
  131.3 0.6 collective-permute-start.33
  131.9 1.3 collective-permute-done.32
  133.2 2.2 %collective-permute-done.33 = bf16[176,128]{1,0:T(8,128)(2,1)S(1)} collective-permute-done((bf16[176,128]{1,0:T(8,128)(2,1)S(1)}, bf16[176,128]{1,0:T(8,128)(2,1)S(1)}, u32[]{:S(2)}, u32[]{:S(2)}) %collective-permute-start.33) | collective-permute-done | bytes 45088 | tf_op jit(solution)/shard_map/ppermute | solution.py:487
  135.4 5.2 %collective-permute-start.34 = (bf16[4,176,128]{2,1,0:T(8,128)(2,1)S(1)}, bf16[4,176,128]{2,1,0:T(8,128)(2,1)S(1)}, u32[]{:S(2)}, u32[]{:S(2)}) collective-permute-start(bf16[4,176,128]{2,1,0:T(8,128)(2,1)S(1)} %pad_maximum_fusion.2.refs_1_), channel_id=1, source_target_pairs={{0,4},{4,0},{8,12},{12,8},{16,20},{20,16},{24,28},{28,24},{32,36},... | collective-permute-start | bytes 540680 | tf_op jit(solution)/shard_map/ppermute | solution.py:484
  140.6 0.7 pad_add_fusion.refs_0_
  141.3 0.7 copy-done.2
  142.2 3.4 %shard_map.122 = bf16[6,64,512]{2,1,0:T(8,128)(2,1)} custom-call(s32[1]{0:T(128)} %bitcast.me_ref, s32[2,64]{1,0:T(2,128)} %bitcast.68, s32[6,1,512]{2,1,0:T(1,128)} %bitcast.63, f32[6,64,512]{2,1,0:T(8,128)} %get-tuple-element.50.center_ref, f32[6,176,128]{2,1,0:T(8,128)} %get-tuple-element.51.gown_ref, bf16[3,176,128]{2,1,0:T(8,128)(2,1)} %copy-done.8, ...), custom_call_target="tpu_custom_call" | custom-call | bytes 3895812 | tf_op jit(solution)/shard_map/pallas_call | solution.py:427
  145.6 0.7 copy-done.12
  146.3 2.4 %shard_map.123 = (f32[27,64,64]{2,1,0:T(8,128)}, f32[8,64,128]{2,1,0:T(8,128)}) custom-call(s32[2]{0:T(128)} %pad_add_fusion.refs_0_, bf16[4,176,128]{2,1,0:T(8,128)(2,1)} %copy-done.1, bf16[4,176,128]{2,1,0:T(8,128)(2,1)} %copy-done.12), custom_call_target="tpu_custom_call" | custom-call | bytes 1064968 | tf_op jit(solution)/shard_map/pallas_call | solution.py:427
  (117 shorter events, 3.1 us)
Async XLA Ops:
  4.3 19.8 %collective-permute-start = (bf16[3,176,128]{2,1,0:T(8,128)(2,1)}, bf16[3,176,128]{2,1,0:T(8,128)(2,1)S(1)}, u32[]{:S(2)}, u32[]{:S(2)}) collective-permute-start(bf16[3,176,128]{2,1,0:T(8,128)(2,1)} %get-tuple-element.39), channel_id=1, source_target_pairs={{0,144},{4,148},{8,152},{12,156},{16,128},{20,132},{24,136},{28,14... | collective-permute-start | bytes 405512 | tf_op jit(solution)/shard_map/ppermute | solution.py:439
  9.0 18.1 %collective-permute-start.1 = (bf16[4,176,128]{2,1,0:T(8,128)(2,1)}, bf16[4,176,128]{2,1,0:T(8,128)(2,1)S(1)}, u32[]{:S(2)}, u32[]{:S(2)}) collective-permute-start(bf16[4,176,128]{2,1,0:T(8,128)(2,1)} %get-tuple-element.40), channel_id=1, source_target_pairs={{0,128},{4,132},{8,136},{12,140},{16,144},{20,148},{24,152},{28,15... | collective-permute-start | bytes 540680 | tf_op jit(solution)/shard_map/ppermute | solution.py:439
  10.0 21.7 %collective-permute-start.2 = (bf16[3,176,128]{2,1,0:T(8,128)(2,1)}, bf16[3,176,128]{2,1,0:T(8,128)(2,1)S(1)}, u32[]{:S(2)}, u32[]{:S(2)}) collective-permute-start(bf16[3,176,128]{2,1,0:T(8,128)(2,1)} %get-tuple-element.41), channel_id=1, source_target_pairs={{16,160},{20,164},{24,168},{28,172},{32,144},{36,148},{40,152},{44... | collective-permute-start | bytes 405512 | tf_op jit(solution)/shard_map/ppermute | solution.py:439
  10.6 22.3 %collective-permute-start.3 = (bf16[4,176,128]{2,1,0:T(8,128)(2,1)}, bf16[4,176,128]{2,1,0:T(8,128)(2,1)S(1)}, u32[]{:S(2)}, u32[]{:S(2)}) collective-permute-start(bf16[4,176,128]{2,1,0:T(8,128)(2,1)} %get-tuple-element.42), channel_id=1, source_target_pairs={{0,16},{4,20},{8,24},{12,28},{16,0},{20,4},{24,8},{28,12},{32,48},... | collective-permute-start | bytes 540680 | tf_op jit(solution)/shard_map/ppermute | solution.py:439
  18.2 15.5 %collective-permute-start.4 = (bf16[4,176,128]{2,1,0:T(8,128)(2,1)}, bf16[4,176,128]{2,1,0:T(8,128)(2,1)S(1)}, u32[]{:S(2)}, u32[]{:S(2)}) collective-permute-start(bf16[4,176,128]{2,1,0:T(8,128)(2,1)} %get-tuple-element.43), channel_id=1, source_target_pairs={{16,32},{20,36},{24,40},{28,44},{32,16},{36,20},{40,24},{44,28},{8... | collective-permute-start | bytes 540680 | tf_op jit(solution)/shard_map/ppermute | solution.py:439
  21.9 1.5 %copy-start.14 = (bf16[2,176,128]{2,1,0:T(8,128)(2,1)S(1)}, bf16[2,176,128]{2,1,0:T(8,128)(2,1)}, u32[]{:S(2)}) copy-start(bf16[2,176,128]{2,1,0:T(8,128)(2,1)} %get-tuple-element.47) | copy-start | bytes 270340
  21.9 1.5 copy-start.15
  22.4 1.6 %copy-start.29 = (bf16[3,176,128]{2,1,0:T(8,128)(2,1)S(1)}, bf16[3,176,128]{2,1,0:T(8,128)(2,1)}, u32[]{:S(2)}) copy-start(bf16[3,176,128]{2,1,0:T(8,128)(2,1)} %get-tuple-element.44) | copy-start | bytes 405508
  22.5 4.7 %copy-start.25 = (bf16[4,176,128]{2,1,0:T(8,128)(2,1)S(1)}, bf16[4,176,128]{2,1,0:T(8,128)(2,1)}, u32[]{:S(2)}) copy-start(bf16[4,176,128]{2,1,0:T(8,128)(2,1)} %get-tuple-element.45) | copy-start | bytes 540676
  22.5 9.2 %copy-start.28 = (bf16[3,176,128]{2,1,0:T(8,128)(2,1)S(1)}, bf16[3,176,128]{2,1,0:T(8,128)(2,1)}, u32[]{:S(2)}) copy-start(bf16[3,176,128]{2,1,0:T(8,128)(2,1)} %get-tuple-element.46) | copy-start | bytes 405508
  23.4 17.5 %copy-start = (bf16[27,64,64]{2,1,0:T(8,128)(2,1)S(1)}, bf16[27,64,64]{2,1,0:T(8,128)(2,1)}, u32[]{:S(2)}) copy-start(bf16[27,64,64]{2,1,0:T(8,128)(2,1)} %param.13) | copy-start | bytes 663556
  24.0 17.1 %copy-start.16 = (bf16[3,176,128]{2,1,0:T(8,128)(2,1)}, bf16[3,176,128]{2,1,0:T(8,128)(2,1)S(1)}, u32[]{:S(2)}) copy-start(bf16[3,176,128]{2,1,0:T(8,128)(2,1)S(1)} %collective-permute-done.rest_0_) | copy-start | bytes 405508
  24.1 10.3 %collective-permute-start.5 = (bf16[3,176,128]{2,1,0:T(8,128)(2,1)S(1)}, bf16[3,176,128]{2,1,0:T(8,128)(2,1)S(1)}, u32[]{:S(2)}, u32[]{:S(2)}) collective-permute-start(bf16[3,176,128]{2,1,0:T(8,128)(2,1)S(1)} %copy-done.29), channel_id=1, source_target_pairs={{64,144},{68,148},{72,152},{76,156},{80,128},{84,132},{88,136},{92... | collective-permute-start | bytes 405512 | tf_op jit(solution)/shard_map/ppermute | solution.py:439
  27.2 14.0 %copy-start.20 = (bf16[4,176,128]{2,1,0:T(8,128)(2,1)}, bf16[4,176,128]{2,1,0:T(8,128)(2,1)S(1)}, u32[]{:S(2)}) copy-start(bf16[4,176,128]{2,1,0:T(8,128)(2,1)S(1)} %collective-permute-done.1.rest_1_) | copy-start | bytes 540676
  27.2 10.0 %collective-permute-start.6 = (bf16[4,176,128]{2,1,0:T(8,128)(2,1)S(1)}, bf16[4,176,128]{2,1,0:T(8,128)(2,1)S(1)}, u32[]{:S(2)}, u32[]{:S(2)}) collective-permute-start(bf16[4,176,128]{2,1,0:T(8,128)(2,1)S(1)} %copy-done.25), channel_id=1, source_target_pairs={{64,128},{68,132},{72,136},{76,140},{80,144},{84,148},{88,152},{92... | collective-permute-start | bytes 540680 | tf_op jit(solution)/shard_map/ppermute | solution.py:439
  31.6 9.5 %copy-start.17 = (bf16[3,176,128]{2,1,0:T(8,128)(2,1)}, bf16[3,176,128]{2,1,0:T(8,128)(2,1)S(1)}, u32[]{:S(2)}) copy-start(bf16[3,176,128]{2,1,0:T(8,128)(2,1)S(1)} %collective-permute-done.2.rest_2_) | copy-start | bytes 405508
  31.6 6.2 %collective-permute-start.7 = (bf16[3,176,128]{2,1,0:T(8,128)(2,1)S(1)}, bf16[3,176,128]{2,1,0:T(8,128)(2,1)S(1)}, u32[]{:S(2)}, u32[]{:S(2)}) collective-permute-start(bf16[3,176,128]{2,1,0:T(8,128)(2,1)S(1)} %copy-done.28), channel_id=1, source_target_pairs={{80,160},{84,164},{88,168},{92,172},{96,144},{100,148},{104,152},{... | collective-permute-start | bytes 405512 | tf_op jit(solution)/shard_map/ppermute | solution.py:439
  33.0 8.2 %copy-start.21 = (bf16[4,176,128]{2,1,0:T(8,128)(2,1)}, bf16[4,176,128]{2,1,0:T(8,128)(2,1)S(1)}, u32[]{:S(2)}) copy-start(bf16[4,176,128]{2,1,0:T(8,128)(2,1)S(1)} %collective-permute-done.3.rest_3_) | copy-start | bytes 540676
  33.6 7.5 %copy-start.22 = (bf16[4,176,128]{2,1,0:T(8,128)(2,1)}, bf16[4,176,128]{2,1,0:T(8,128)(2,1)S(1)}, u32[]{:S(2)}) copy-start(bf16[4,176,128]{2,1,0:T(8,128)(2,1)S(1)} %collective-permute-done.4.rest_4_) | copy-start | bytes 540676
  34.3 7.2 %copy-start.18 = (bf16[3,176,128]{2,1,0:T(8,128)(2,1)}, bf16[3,176,128]{2,1,0:T(8,128)(2,1)S(1)}, u32[]{:S(2)}) copy-start(bf16[3,176,128]{2,1,0:T(8,128)(2,1)S(1)} %collective-permute-done.5.rest_5_) | copy-start | bytes 405508
  37.2 4.3 %copy-start.23 = (bf16[4,176,128]{2,1,0:T(8,128)(2,1)}, bf16[4,176,128]{2,1,0:T(8,128)(2,1)S(1)}, u32[]{:S(2)}) copy-start(bf16[4,176,128]{2,1,0:T(8,128)(2,1)S(1)} %collective-permute-done.6.rest_6_) | copy-start | bytes 540676
  37.9 3.6 %copy-start.19 = (bf16[3,176,128]{2,1,0:T(8,128)(2,1)}, bf16[3,176,128]{2,1,0:T(8,128)(2,1)S(1)}, u32[]{:S(2)}) copy-start(bf16[3,176,128]{2,1,0:T(8,128)(2,1)S(1)} %collective-permute-done.7.rest_7_) | copy-start | bytes 405508
  38.6 6.9 %collective-permute-start.8 = (bf16[10,176,128]{2,1,0:T(8,128)(2,1)}, bf16[10,176,128]{2,1,0:T(8,128)(2,1)}, u32[]{:S(2)}, u32[]{:S(2)}) collective-permute-start(bf16[10,176,128]{2,1,0:T(8,128)(2,1)} %get-tuple-element.104), channel_id=1, source_target_pairs={{0,4},{4,0},{8,12},{12,8},{16,20},{20,16},{24,28},{28,24},{32,36},... | collective-permute-start | bytes 1351688 | tf_op jit(solution)/shard_map/ppermute | solution.py:451
  39.4 6.0 %collective-permute-start.9 = (bf16[10,176,128]{2,1,0:T(8,128)(2,1)}, bf16[10,176,128]{2,1,0:T(8,128)(2,1)}, u32[]{:S(2)}, u32[]{:S(2)}) collective-permute-start(bf16[10,176,128]{2,1,0:T(8,128)(2,1)} %get-tuple-element.103), channel_id=1, source_target_pairs={{4,8},{8,4},{20,24},{24,20},{36,40},{40,36},{52,56},{56,52},{68,72... | collective-permute-start | bytes 1351688 | tf_op jit(solution)/shard_map/ppermute | solution.py:451
  42.7 1.4 copy-start.13
  65.3 26.2 %copy-start.27 = (bf16[4,176,128]{2,1,0:T(8,128)(2,1)S(1)}, bf16[4,176,128]{2,1,0:T(8,128)(2,1)}, u32[]{:S(2)}) copy-start(bf16[4,176,128]{2,1,0:T(8,128)(2,1)} %get-tuple-element.61) | copy-start | bytes 540676
  66.4 20.1 %collective-permute-start.14 = (bf16[4,176,128]{2,1,0:T(8,128)(2,1)S(1)}, bf16[4,176,128]{2,1,0:T(8,128)(2,1)S(1)}, u32[]{:S(2)}, u32[]{:S(2)}) collective-permute-start(bf16[4,176,128]{2,1,0:T(8,128)(2,1)S(1)} %fusion), channel_id=1, source_target_pairs={{0,4},{4,0},{8,12},{12,8},{16,20},{20,16},{24,28},{28,24},{32,36},... | collective-permute-start | bytes 540680 | tf_op jit(solution)/shard_map/ppermute | solution.py:484
  70.5 15.9 %collective-permute-start.10 = (bf16[3,176,128]{2,1,0:T(8,128)(2,1)}, bf16[3,176,128]{2,1,0:T(8,128)(2,1)S(1)}, u32[]{:S(2)}, u32[]{:S(2)}) collective-permute-start(bf16[3,176,128]{2,1,0:T(8,128)(2,1)} %get-tuple-element.52), channel_id=1, source_target_pairs={{0,144},{4,148},{8,152},{12,156},{16,128},{20,132},{24,136},{28,14... | collective-permute-start | bytes 405512 | tf_op jit(solution)/shard_map/ppermute | solution.py:481
  71.4 19.9 %collective-permute-start.11 = (bf16[4,176,128]{2,1,0:T(8,128)(2,1)}, bf16[4,176,128]{2,1,0:T(8,128)(2,1)S(1)}, u32[]{:S(2)}, u32[]{:S(2)}) collective-permute-start(bf16[4,176,128]{2,1,0:T(8,128)(2,1)} %get-tuple-element.53), channel_id=1, source_target_pairs={{0,128},{4,132},{8,136},{12,140},{16,144},{20,148},{24,152},{28,15... | collective-permute-start | bytes 540680 | tf_op jit(solution)/shard_map/ppermute | solution.py:481
  81.3 18.7 %collective-permute-start.12 = (bf16[3,176,128]{2,1,0:T(8,128)(2,1)}, bf16[3,176,128]{2,1,0:T(8,128)(2,1)S(1)}, u32[]{:S(2)}, u32[]{:S(2)}) collective-permute-start(bf16[3,176,128]{2,1,0:T(8,128)(2,1)} %get-tuple-element.54), channel_id=1, source_target_pairs={{16,160},{20,164},{24,168},{28,172},{32,144},{36,148},{40,152},{44... | collective-permute-start | bytes 405512 | tf_op jit(solution)/shard_map/ppermute | solution.py:481
  81.9 29.3 %collective-permute-start.13 = (bf16[4,176,128]{2,1,0:T(8,128)(2,1)}, bf16[4,176,128]{2,1,0:T(8,128)(2,1)S(1)}, u32[]{:S(2)}, u32[]{:S(2)}) collective-permute-start(bf16[4,176,128]{2,1,0:T(8,128)(2,1)} %get-tuple-element.55), channel_id=1, source_target_pairs={{0,16},{4,20},{8,24},{12,28},{16,0},{20,4},{24,8},{28,12},{32,48},... | collective-permute-start | bytes 540680 | tf_op jit(solution)/shard_map/ppermute | solution.py:481
  85.4 14.8 %copy-start.31 = (bf16[3,176,128]{2,1,0:T(8,128)(2,1)S(1)}, bf16[3,176,128]{2,1,0:T(8,128)(2,1)}, u32[]{:S(2)}) copy-start(bf16[3,176,128]{2,1,0:T(8,128)(2,1)} %get-tuple-element.62) | copy-start | bytes 405508
  85.4 21.5 %copy-start.26 = (bf16[4,176,128]{2,1,0:T(8,128)(2,1)S(1)}, bf16[4,176,128]{2,1,0:T(8,128)(2,1)}, u32[]{:S(2)}) copy-start(bf16[4,176,128]{2,1,0:T(8,128)(2,1)} %get-tuple-element.63) | copy-start | bytes 540676
  85.4 25.1 %copy-start.30 = (bf16[3,176,128]{2,1,0:T(8,128)(2,1)S(1)}, bf16[3,176,128]{2,1,0:T(8,128)(2,1)}, u32[]{:S(2)}) copy-start(bf16[3,176,128]{2,1,0:T(8,128)(2,1)} %get-tuple-element.64) | copy-start | bytes 405508
  86.4 24.9 %copy-start.8 = (bf16[3,176,128]{2,1,0:T(8,128)(2,1)}, bf16[3,176,128]{2,1,0:T(8,128)(2,1)S(1)}, u32[]{:S(2)}) copy-start(bf16[3,176,128]{2,1,0:T(8,128)(2,1)S(1)} %collective-permute-done.10.rest_0_) | copy-start | bytes 405508
  87.5 4.0 %collective-permute-start.21 = (bf16[176,128]{1,0:T(8,128)(2,1)S(1)}, bf16[176,128]{1,0:T(8,128)(2,1)S(1)}, u32[]{:S(2)}, u32[]{:S(2)}) collective-permute-start(bf16[176,128]{1,0:T(8,128)(2,1)S(1)} %get-tuple-element.86), channel_id=1, source_target_pairs={{0,1},{1,0},{2,3},{3,2},{4,5},{5,4},{6,7},{7,6},{8,9},{9,8},{10,11... | collective-permute-start | bytes 135176 | tf_op jit(solution)/shard_map/ppermute | solution.py:487
  88.8 4.4 %collective-permute-start.22 = (bf16[176,128]{1,0:T(8,128)(2,1)S(1)}, bf16[176,128]{1,0:T(8,128)(2,1)S(1)}, u32[]{:S(2)}, u32[]{:S(2)}) collective-permute-start(bf16[176,128]{1,0:T(8,128)(2,1)S(1)} %get-tuple-element.85), channel_id=1, source_target_pairs={{0,2},{1,3},{2,0},{3,1},{4,6},{5,7},{6,4},{7,5},{8,10},{9,11},{10,... | collective-permute-start | bytes 135176 | tf_op jit(solution)/shard_map/ppermute | solution.py:487
  91.3 44.1 %copy-start.4 = (bf16[4,176,128]{2,1,0:T(8,128)(2,1)}, bf16[4,176,128]{2,1,0:T(8,128)(2,1)S(1)}, u32[]{:S(2)}) copy-start(bf16[4,176,128]{2,1,0:T(8,128)(2,1)S(1)} %collective-permute-done.11.rest_1_) | copy-start | bytes 540676
  91.3 4.1 %collective-permute-start.23 = (bf16[176,128]{1,0:T(8,128)(2,1)S(1)}, bf16[176,128]{1,0:T(8,128)(2,1)S(1)}, u32[]{:S(2)}, u32[]{:S(2)}) collective-permute-start(bf16[176,128]{1,0:T(8,128)(2,1)S(1)} %get-tuple-element.84), channel_id=1, source_target_pairs={{0,3},{1,2},{2,1},{3,0},{4,7},{5,6},{6,5},{7,4},{8,11},{9,10},{10,... | collective-permute-start | bytes 135176 | tf_op jit(solution)/shard_map/ppermute | solution.py:487
  91.5 26.2 %collective-permute-start.15 = (bf16[4,176,128]{2,1,0:T(8,128)(2,1)S(1)}, bf16[4,176,128]{2,1,0:T(8,128)(2,1)S(1)}, u32[]{:S(2)}, u32[]{:S(2)}) collective-permute-start(bf16[4,176,128]{2,1,0:T(8,128)(2,1)S(1)} %copy-done.27), channel_id=1, source_target_pairs={{16,32},{20,36},{24,40},{28,44},{32,16},{36,20},{40,24},{44,28},{8... | collective-permute-start | bytes 540680 | tf_op jit(solution)/shard_map/ppermute | solution.py:481
  95.4 4.8 %collective-permute-start.24 = (bf16[176,128]{1,0:T(8,128)(2,1)S(1)}, bf16[176,128]{1,0:T(8,128)(2,1)S(1)}, u32[]{:S(2)}, u32[]{:S(2)}) collective-permute-start(bf16[176,128]{1,0:T(8,128)(2,1)S(1)} %fusion.3), channel_id=1, source_target_pairs={{0,64},{4,68},{8,72},{12,76},{16,80},{20,84},{24,88},{28,92},{32,9... | collective-permute-start | bytes 135176 | tf_op jit(solution)/shard_map/ppermute | solution.py:484
  95.8 11.2 %collective-permute-start.25 = (bf16[176,128]{1,0:T(8,128)(2,1)S(1)}, bf16[176,128]{1,0:T(8,128)(2,1)S(1)}, u32[]{:S(2)}, u32[]{:S(2)}) collective-permute-start(bf16[176,128]{1,0:T(8,128)(2,1)S(1)} %fusion.3), channel_id=1, source_target_pairs={{0,128},{4,132},{8,136},{12,140},{16,144},{20,148},{24,152},{28,15... | collective-permute-start | bytes 135176 | tf_op jit(solution)/shard_map/ppermute | solution.py:484
  100.0 41.3 %copy-start.9 = (bf16[3,176,128]{2,1,0:T(8,128)(2,1)}, bf16[3,176,128]{2,1,0:T(8,128)(2,1)S(1)}, u32[]{:S(2)}) copy-start(bf16[3,176,128]{2,1,0:T(8,128)(2,1)S(1)} %collective-permute-done.12.rest_2_) | copy-start | bytes 405508
  100.0 10.6 %collective-permute-start.26 = (bf16[176,128]{1,0:T(8,128)(2,1)S(1)}, bf16[176,128]{1,0:T(8,128)(2,1)S(1)}, u32[]{:S(2)}, u32[]{:S(2)}) collective-permute-start(bf16[176,128]{1,0:T(8,128)(2,1)S(1)} %fusion.3), channel_id=1, source_target_pairs={{0,192},{4,196},{8,200},{12,204},{16,208},{20,212},{24,216},{28,22... | collective-permute-start | bytes 135176 | tf_op jit(solution)/shard_map/ppermute | solution.py:484
  100.3 19.3 %collective-permute-start.16 = (bf16[3,176,128]{2,1,0:T(8,128)(2,1)S(1)}, bf16[3,176,128]{2,1,0:T(8,128)(2,1)S(1)}, u32[]{:S(2)}, u32[]{:S(2)}) collective-permute-start(bf16[3,176,128]{2,1,0:T(8,128)(2,1)S(1)} %copy-done.31), channel_id=1, source_target_pairs={{64,144},{68,148},{72,152},{76,156},{80,128},{84,132},{88,136},{92... | collective-permute-start | bytes 405512 | tf_op jit(solution)/shard_map/ppermute | solution.py:481
  107.0 14.3 %collective-permute-start.17 = (bf16[4,176,128]{2,1,0:T(8,128)(2,1)S(1)}, bf16[4,176,128]{2,1,0:T(8,128)(2,1)S(1)}, u32[]{:S(2)}, u32[]{:S(2)}) collective-permute-start(bf16[4,176,128]{2,1,0:T(8,128)(2,1)S(1)} %copy-done.26), channel_id=1, source_target_pairs={{64,128},{68,132},{72,136},{76,140},{80,144},{84,148},{88,152},{92... | collective-permute-start | bytes 540680 | tf_op jit(solution)/shard_map/ppermute | solution.py:481
  110.5 10.8 %collective-permute-start.18 = (bf16[3,176,128]{2,1,0:T(8,128)(2,1)S(1)}, bf16[3,176,128]{2,1,0:T(8,128)(2,1)S(1)}, u32[]{:S(2)}, u32[]{:S(2)}) collective-permute-start(bf16[3,176,128]{2,1,0:T(8,128)(2,1)S(1)} %copy-done.30), channel_id=1, source_target_pairs={{80,160},{84,164},{88,168},{92,172},{96,144},{100,148},{104,152},{... | collective-permute-start | bytes 405512 | tf_op jit(solution)/shard_map/ppermute | solution.py:481
  111.3 30.0 %copy-start.5 = (bf16[4,176,128]{2,1,0:T(8,128)(2,1)}, bf16[4,176,128]{2,1,0:T(8,128)(2,1)S(1)}, u32[]{:S(2)}) copy-start(bf16[4,176,128]{2,1,0:T(8,128)(2,1)S(1)} %collective-permute-done.13.rest_3_) | copy-start | bytes 540676
  111.3 3.4 %collective-permute-start.27 = (bf16[176,128]{1,0:T(8,128)(2,1)S(1)}, bf16[176,128]{1,0:T(8,128)(2,1)S(1)}, u32[]{:S(2)}, u32[]{:S(2)}) collective-permute-start(bf16[176,128]{1,0:T(8,128)(2,1)S(1)} %add_convert_fusion.2), channel_id=1, source_target_pairs={{0,8},{4,12},{8,0},{12,4},{16,24},{20,28},{24,16},{28,20},{32,40},... | collective-permute-start | bytes 135176 | tf_op jit(solution)/shard_map/ppermute | solution.py:484
  114.7 13.2 %collective-permute-start.28 = (bf16[176,128]{1,0:T(8,128)(2,1)S(1)}, bf16[176,128]{1,0:T(8,128)(2,1)S(1)}, u32[]{:S(2)}, u32[]{:S(2)}) collective-permute-start(bf16[176,128]{1,0:T(8,128)(2,1)S(1)} %add_convert_fusion.1), channel_id=1, source_target_pairs={{0,16},{4,20},{8,24},{12,28},{16,0},{20,4},{24,8},{28,12},{32,48},... | collective-permute-start | bytes 135176 | tf_op jit(solution)/shard_map/ppermute | solution.py:484
  117.7 23.6 %copy-start.6 = (bf16[4,176,128]{2,1,0:T(8,128)(2,1)}, bf16[4,176,128]{2,1,0:T(8,128)(2,1)S(1)}, u32[]{:S(2)}) copy-start(bf16[4,176,128]{2,1,0:T(8,128)(2,1)S(1)} %collective-permute-done.15.rest_4_) | copy-start | bytes 540676
  117.7 10.2 %collective-permute-start.29 = (bf16[176,128]{1,0:T(8,128)(2,1)S(1)}, bf16[176,128]{1,0:T(8,128)(2,1)S(1)}, u32[]{:S(2)}, u32[]{:S(2)}) collective-permute-start(bf16[176,128]{1,0:T(8,128)(2,1)S(1)} %add_convert_fusion.1), channel_id=1, source_target_pairs={{0,32},{4,36},{8,40},{12,44},{16,48},{20,52},{24,56},{28,60},{32,0... | collective-permute-start | bytes 135176 | tf_op jit(solution)/shard_map/ppermute | solution.py:484
  119.6 21.7 %copy-start.10 = (bf16[3,176,128]{2,1,0:T(8,128)(2,1)}, bf16[3,176,128]{2,1,0:T(8,128)(2,1)S(1)}, u32[]{:S(2)}) copy-start(bf16[3,176,128]{2,1,0:T(8,128)(2,1)S(1)} %collective-permute-done.16.rest_5_) | copy-start | bytes 405508
  119.6 8.3 %collective-permute-start.30 = (bf16[176,128]{1,0:T(8,128)(2,1)S(1)}, bf16[176,128]{1,0:T(8,128)(2,1)S(1)}, u32[]{:S(2)}, u32[]{:S(2)}) collective-permute-start(bf16[176,128]{1,0:T(8,128)(2,1)S(1)} %add_convert_fusion.1), channel_id=1, source_target_pairs={{0,48},{4,52},{8,56},{12,60},{16,32},{20,36},{24,40},{28,44},{32,1... | collective-permute-start | bytes 135176 | tf_op jit(solution)/shard_map/ppermute | solution.py:484
  121.3 20.0 %copy-start.7 = (bf16[4,176,128]{2,1,0:T(8,128)(2,1)}, bf16[4,176,128]{2,1,0:T(8,128)(2,1)S(1)}, u32[]{:S(2)}) copy-start(bf16[4,176,128]{2,1,0:T(8,128)(2,1)S(1)} %collective-permute-done.17.rest_6_) | copy-start | bytes 540676
  121.3 20.0 %copy-start.11 = (bf16[3,176,128]{2,1,0:T(8,128)(2,1)}, bf16[3,176,128]{2,1,0:T(8,128)(2,1)S(1)}, u32[]{:S(2)}) copy-start(bf16[3,176,128]{2,1,0:T(8,128)(2,1)S(1)} %collective-permute-done.18.rest_7_) | copy-start | bytes 405508
  121.4 19.9 %collective-permute-start.19 = (bf16[10,176,128]{2,1,0:T(8,128)(2,1)S(1)}, bf16[10,176,128]{2,1,0:T(8,128)(2,1)S(1)}, u32[]{:S(2)}, u32[]{:S(2)}) collective-permute-start(bf16[10,176,128]{2,1,0:T(8,128)(2,1)S(1)} %get-tuple-element.96), channel_id=1, source_target_pairs={{0,4},{4,0},{8,12},{12,8},{16,20},{20,16},{24,28},{28,24},{32,36},... | collective-permute-start | bytes 1351688 | tf_op jit(solution)/shard_map/ppermute | solution.py:451
  127.2 14.1 %collective-permute-start.20 = (bf16[10,176,128]{2,1,0:T(8,128)(2,1)S(1)}, bf16[10,176,128]{2,1,0:T(8,128)(2,1)S(1)}, u32[]{:S(2)}, u32[]{:S(2)}) collective-permute-start(bf16[10,176,128]{2,1,0:T(8,128)(2,1)S(1)} %get-tuple-element.95), channel_id=1, source_target_pairs={{4,8},{8,4},{20,24},{24,20},{36,40},{40,36},{52,56},{56,52},{68,72... | collective-permute-start | bytes 1351688 | tf_op jit(solution)/shard_map/ppermute | solution.py:451
  128.0 3.9 %collective-permute-start.31 = (bf16[176,128]{1,0:T(8,128)(2,1)S(1)}, bf16[176,128]{1,0:T(8,128)(2,1)S(1)}, u32[]{:S(2)}, u32[]{:S(2)}) collective-permute-start(bf16[176,128]{1,0:T(8,128)(2,1)S(1)} %add_convert_fusion), channel_id=1, source_target_pairs={{0,1},{1,0},{2,3},{3,2},{4,5},{5,4},{6,7},{7,6},{8,9},{9,8},{10,11... | collective-permute-start | bytes 135176 | tf_op jit(solution)/shard_map/ppermute | solution.py:487
  128.1 5.1 %collective-permute-start.32 = (bf16[176,128]{1,0:T(8,128)(2,1)S(1)}, bf16[176,128]{1,0:T(8,128)(2,1)S(1)}, u32[]{:S(2)}, u32[]{:S(2)}) collective-permute-start(bf16[176,128]{1,0:T(8,128)(2,1)S(1)} %add_convert_fusion), channel_id=1, source_target_pairs={{0,2},{1,3},{2,0},{3,1},{4,6},{5,7},{6,4},{7,5},{8,10},{9,11},{10,... | collective-permute-start | bytes 135176 | tf_op jit(solution)/shard_map/ppermute | solution.py:487
  131.3 4.1 %collective-permute-start.33 = (bf16[176,128]{1,0:T(8,128)(2,1)S(1)}, bf16[176,128]{1,0:T(8,128)(2,1)S(1)}, u32[]{:S(2)}, u32[]{:S(2)}) collective-permute-start(bf16[176,128]{1,0:T(8,128)(2,1)S(1)} %add_convert_fusion), channel_id=1, source_target_pairs={{0,3},{1,2},{2,1},{3,0},{4,7},{5,6},{6,5},{7,4},{8,11},{9,10},{10,... | collective-permute-start | bytes 135176 | tf_op jit(solution)/shard_map/ppermute | solution.py:487
  135.4 10.2 %copy-start.1 = (bf16[4,176,128]{2,1,0:T(8,128)(2,1)}, bf16[4,176,128]{2,1,0:T(8,128)(2,1)S(1)}, u32[]{:S(2)}) copy-start(bf16[4,176,128]{2,1,0:T(8,128)(2,1)S(1)} %pad_maximum_fusion.2.refs_1_) | copy-start | bytes 540676
  135.4 10.2 %collective-permute-start.34 = (bf16[4,176,128]{2,1,0:T(8,128)(2,1)S(1)}, bf16[4,176,128]{2,1,0:T(8,128)(2,1)S(1)}, u32[]{:S(2)}, u32[]{:S(2)}) collective-permute-start(bf16[4,176,128]{2,1,0:T(8,128)(2,1)S(1)} %pad_maximum_fusion.2.refs_1_), channel_id=1, source_target_pairs={{0,4},{4,0},{8,12},{12,8},{16,20},{20,16},{24,28},{28,24},{32,36},... | collective-permute-start | bytes 540680 | tf_op jit(solution)/shard_map/ppermute | solution.py:484
  141.3 0.9 copy-start.3
  (3 other events, 2.2 us)

commit v3 on v2

--- a/solution.py
+++ b/solution.py
@@ -23,7 +23,7 @@
 
 X_LO, X_HI, Y_LO, Y_HI, Z_AT = 0, 32, 64, 96, 128
 
-PLANE = [(1, 1), (1, 0), (1, -1), (0, 1), (0, -1), (-1, 1), (-1, 0), (-1, -1)]
+PLANE = [(0, 1), (0, -1), (1, 1), (1, 0), (1, -1), (-1, 1), (-1, 0), (-1, -1)]
 
 
 def slots_of(a, b, c):
@@ -500,11 +500,12 @@
     mine = one_of(halves, core) + swap(one_of(halves, 1 - core).astype(BF16), 1).astype(F32)
     small = mine.astype(BF16)
     away = [one_of(small, jnp.bitwise_xor(x, k)) for k in (1, 2, 3)]
-    plane(4, 8, tuple(away))
+    plane(4, 6, tuple(away))
     v = one_of(mine, x)
     for k in (1, 2, 3):
         v = v + swap_x(away[k - 1], k).astype(F32)
     w = v.astype(BF16)
+    plane(6, 8, w)
     w = pairs(w, (16, 32, 48))
     w = pairs(w, (2,))
     w = pairs(w, (4, 8, 12))

time: 149 us -> 145 us (0.973)
  waiting for transfers between devices: 12.2 us -> 4.93 us
  starting transfers between devices: 84.6 us -> 87.5 us
    ppermute x9, starting transfers between devices: 20.7 us -> 24.6 us  [swap(): return lax.ppermute(v, 'spatial', [(d, d ^ bit) for d in range(peers)])]
    ppermute x9, waiting for transfers between devices: 3.29 us -> 0.25 us  [swap(): return lax.ppermute(v, 'spatial', [(d, d ^ bit) for d in range(peers)])]
    ppermute x8, waiting for transfers between devices: 2.17 us -> 0.02 us  [exchange_plane(): lax.ppermute(v, 'spatial', swap_pairs(peers, a, b))]
    ppermute x8, starting transfers between devices: 25.6 us -> 23.6 us  [plane(): got[k] = lax.ppermute(v, 'spatial', swap_pairs(peers, *k))]
    ppermute x6, waiting for transfers between devices: 6.66 us -> 4.63 us  [swap_x(): return lax.ppermute(v, 'dp', [(d, d ^ bit) for d in range(4)])]
  transfers between devices with their start and end apart: 35 -> 35, of which waited for: 6 -> 5; matrix products, arithmetic and copies ran while one was open for 12% -> 12% of each run, Pallas kernels for 2% -> 2%
where the time goes in v3:
time: 145 us; the launch traced here: 144 us
  starting transfers between devices  87.5 us (60%)
  Pallas kernels  29.3 us (20%)
  local copies, waits for them, and re-layouts  18.3 us (13%)
  waiting for transfers between devices  4.93 us (3%)
  other arithmetic  3 us (2%)
    pallas_call x4, Pallas kernels, call(): pl.pallas_call(kernel, out_shape=outs, in_specs=[spec_s] * smem + [spec_v...  29.3 us
    ppermute x9, starting transfers between devices, swap(): return lax.ppermute(v, 'spatial', [(d, d ^ bit) for d in range(peers)])  24.6 us
    ppermute x8, starting transfers between devices, plane(): got[k] = lax.ppermute(v, 'spatial', swap_pairs(peers, *k))  23.6 us
    ppermute x8, starting transfers between devices, exchange_plane(): lax.ppermute(v, 'spatial', swap_pairs(peers, a, b))  21.4 us
    ppermute x4, starting transfers between devices, exchange_along(): lax.ppermute(jnp.concatenate(pieces, axis=0), 'spatial', swaps[n])  9.94 us
    unnamed x81, local copies, waits for them, and re-layouts  9.25 us
    ppermute x6, starting transfers between devices, swap_x(): return lax.ppermute(v, 'dp', [(d, d ^ bit) for d in range(4)])  7.97 us
    ppermute x6, waiting for transfers between devices, swap_x(): return lax.ppermute(v, 'dp', [(d, d ^ bit) for d in range(4)])  4.63 us
  transfers between devices with their start and end apart: 35, of which 5 were waited for; matrix products, arithmetic and copies ran while one was open for 12% of the time, Pallas kernels for 2%

profile of v3, /device:TPU:41, one launch (start us, length us, event | category | flops | bytes accessed | tf_op | source)
XLA Modules:
  0.0 144.3 jit_solution(168469753244291316)
XLA Ops:
  0.6 3.6 %shard_map.120 = (bf16[6,64,512]{2,1,0:T(8,128)(2,1)}, bf16[6,176,128]{2,1,0:T(8,128)(2,1)}, bf16[4,176,128]{2,1,0:T(8,128)(2,1)}, bf16[4,176,128]{2,1,0:T(8,128...) custom-call(s32[1]{0:T(128)} %bitcast.me_ref, ...), custom_call_target="tpu_custom_call" | custom-call | bytes 2511364 | tf_op jit(solution)/shard_map/pallas_call | solution.py:427
  4.3 3.0 %collective-permute-start = (bf16[4,176,128]{2,1,0:T(8,128)(2,1)}, bf16[4,176,128]{2,1,0:T(8,128)(2,1)S(1)}, u32[]{:S(2)}, u32[]{:S(2)}) collective-permute-start(bf16[4,176,128]{2,1,0:T(8,128)(2,1)} %get-tuple-element.39), channel_id=1, source_target_pairs={{0,16},{4,20},{8,24},{12,28},{16,0},{20,4},{24,8},{28,12},{32,48},... | collective-permute-start | bytes 540680 | tf_op jit(solution)/shard_map/ppermute | solution.py:439
  7.3 0.7 collective-permute-start.1
  8.0 7.5 %collective-permute-start.2 = (bf16[3,176,128]{2,1,0:T(8,128)(2,1)}, bf16[3,176,128]{2,1,0:T(8,128)(2,1)S(1)}, u32[]{:S(2)}, u32[]{:S(2)}) collective-permute-start(bf16[3,176,128]{2,1,0:T(8,128)(2,1)} %get-tuple-element.41), channel_id=1, source_target_pairs={{0,144},{4,148},{8,152},{12,156},{16,128},{20,132},{24,136},{28,14... | collective-permute-start | bytes 405512 | tf_op jit(solution)/shard_map/ppermute | solution.py:439
  15.5 1.0 collective-permute-start.3
  16.5 0.7 collective-permute-start.4
  17.1 1.0 reverse_bitcast_fusion
  19.2 0.9 copy.22
  20.2 0.5 reshape.59
  20.7 0.9 copy.23
  21.6 0.7 constant_dynamic-update-slice_fusion.8
  22.3 4.3 %collective-permute-start.5 = (bf16[3,176,128]{2,1,0:T(8,128)(2,1)S(1)}, bf16[3,176,128]{2,1,0:T(8,128)(2,1)S(1)}, u32[]{:S(2)}, u32[]{:S(2)}) collective-permute-start(bf16[3,176,128]{2,1,0:T(8,128)(2,1)S(1)} %copy-done.28), channel_id=1, source_target_pairs={{64,144},{68,148},{72,152},{76,156},{80,128},{84,132},{88,136},{92... | collective-permute-start | bytes 405512 | tf_op jit(solution)/shard_map/ppermute | solution.py:439
  26.6 0.6 constant_dynamic-update-slice_fusion.16
  27.3 3.6 %collective-permute-start.6 = (bf16[4,176,128]{2,1,0:T(8,128)(2,1)S(1)}, bf16[4,176,128]{2,1,0:T(8,128)(2,1)S(1)}, u32[]{:S(2)}, u32[]{:S(2)}) collective-permute-start(bf16[4,176,128]{2,1,0:T(8,128)(2,1)S(1)} %copy-done.25), channel_id=1, source_target_pairs={{64,128},{68,132},{72,136},{76,140},{80,144},{84,148},{88,152},{92... | collective-permute-start | bytes 540680 | tf_op jit(solution)/shard_map/ppermute | solution.py:439
  30.9 0.6 constant_dynamic-update-slice_fusion.15
  31.6 0.7 collective-permute-start.7
  32.2 0.6 constant_dynamic-update-slice_fusion.14
  32.9 0.7 constant_dynamic-update-slice_fusion.13
  33.6 0.7 constant_dynamic-update-slice_fusion.12
  34.2 0.7 constant_dynamic-update-slice_fusion.11
  34.9 0.7 constant_dynamic-update-slice_fusion.10
  35.6 0.7 constant_dynamic-update-slice_fusion.9
  36.3 2.4 %collective-permute-start.8 = (bf16[10,176,128]{2,1,0:T(8,128)(2,1)}, bf16[10,176,128]{2,1,0:T(8,128)(2,1)}, u32[]{:S(2)}, u32[]{:S(2)}) collective-permute-start(bf16[10,176,128]{2,1,0:T(8,128)(2,1)} %get-tuple-element.104), channel_id=1, source_target_pairs={{0,4},{4,0},{8,12},{12,8},{16,20},{20,16},{24,28},{28,24},{32,36},... | collective-permute-start | bytes 1351688 | tf_op jit(solution)/shard_map/ppermute | solution.py:451
  38.7 1.4 %collective-permute-start.9 = (bf16[10,176,128]{2,1,0:T(8,128)(2,1)}, bf16[10,176,128]{2,1,0:T(8,128)(2,1)}, u32[]{:S(2)}, u32[]{:S(2)}) collective-permute-start(bf16[10,176,128]{2,1,0:T(8,128)(2,1)} %get-tuple-element.103), channel_id=1, source_target_pairs={{4,8},{8,4},{20,24},{24,20},{36,40},{40,36},{52,56},{56,52},{68,72... | collective-permute-start | bytes 1351688 | tf_op jit(solution)/shard_map/ppermute | solution.py:451
  40.7 1.2 copy.18
  42.0 0.5 reshape.57
  42.5 0.9 copy.19
  43.4 0.7 reshape.55.cot_ref
  44.1 0.6 fusion.15.idx_ref
  44.7 19.9 %shard_map.121 = (bf16[24,4,512]{2,1,0:T(4,128)(2,1)}, f32[6,64,512]{2,1,0:T(8,128)}, f32[6,176,128]{2,1,0:T(8,128)}, f32[1408,128]{1,0:T(8,128)}, bf16[4,176,12...) custom-call(s32[162]{0:T(256)} %fusion.15.idx_ref, ...), custom_call_target="tpu_custom_call" | custom-call | flops 10000000000 | bytes 8094348 | tf_op jit(solution)/shard_map/pallas_call | solution.py:427
  64.6 1.1 fusion
  65.6 4.1 %collective-permute-start.14 = (bf16[4,176,128]{2,1,0:T(8,128)(2,1)S(1)}, bf16[4,176,128]{2,1,0:T(8,128)(2,1)S(1)}, u32[]{:S(2)}, u32[]{:S(2)}) collective-permute-start(bf16[4,176,128]{2,1,0:T(8,128)(2,1)S(1)} %fusion), channel_id=1, source_target_pairs={{0,4},{4,0},{8,12},{12,8},{16,20},{20,16},{24,28},{28,24},{32,36},... | collective-permute-start | bytes 540680 | tf_op jit(solution)/shard_map/ppermute | solution.py:484
  69.7 6.2 %collective-permute-start.10 = (bf16[4,176,128]{2,1,0:T(8,128)(2,1)}, bf16[4,176,128]{2,1,0:T(8,128)(2,1)S(1)}, u32[]{:S(2)}, u32[]{:S(2)}) collective-permute-start(bf16[4,176,128]{2,1,0:T(8,128)(2,1)} %get-tuple-element.52), channel_id=1, source_target_pairs={{0,16},{4,20},{8,24},{12,28},{16,0},{20,4},{24,8},{28,12},{32,48},... | collective-permute-start | bytes 540680 | tf_op jit(solution)/shard_map/ppermute | solution.py:481
  76.0 0.7 collective-permute-start.11
  76.7 7.2 %collective-permute-start.13 = (bf16[4,176,128]{2,1,0:T(8,128)(2,1)}, bf16[4,176,128]{2,1,0:T(8,128)(2,1)S(1)}, u32[]{:S(2)}, u32[]{:S(2)}) collective-permute-start(bf16[4,176,128]{2,1,0:T(8,128)(2,1)} %get-tuple-element.55), channel_id=1, source_target_pairs={{0,128},{4,132},{8,136},{12,140},{16,144},{20,148},{24,152},{28,15... | collective-permute-start | bytes 540680 | tf_op jit(solution)/shard_map/ppermute | solution.py:481
  83.9 0.9 constant_dynamic-update-slice_fusion.26
  84.8 0.9 constant_dynamic-update-slice_fusion.35
  85.8 1.1 fusion.16
  86.9 1.3 collective-permute-start.17
  88.2 2.4 %collective-permute-start.18 = (bf16[176,128]{1,0:T(8,128)(2,1)S(1)}, bf16[176,128]{1,0:T(8,128)(2,1)S(1)}, u32[]{:S(2)}, u32[]{:S(2)}) collective-permute-start(bf16[176,128]{1,0:T(8,128)(2,1)S(1)} %get-tuple-element.85), channel_id=1, source_target_pairs={{0,2},{1,3},{2,0},{3,1},{4,6},{5,7},{6,4},{7,5},{8,10},{9,11},{10,... | collective-permute-start | bytes 135176 | tf_op jit(solution)/shard_map/ppermute | solution.py:487
  91.0 0.7 collective-permute-start.15
  91.7 0.9 collective-permute-done.18
  92.6 2.3 %collective-permute-done.19 = bf16[176,128]{1,0:T(8,128)(2,1)S(1)} collective-permute-done((bf16[176,128]{1,0:T(8,128)(2,1)S(1)}, bf16[176,128]{1,0:T(8,128)(2,1)S(1)}, u32[]{:S(2)}, u32[]{:S(2)}) %collective-permute-start.19) | collective-permute-done | bytes 45088 | tf_op jit(solution)/shard_map/ppermute | solution.py:487
  95.0 1.5 %collective-permute-start.25 = (bf16[176,128]{1,0:T(8,128)(2,1)S(1)}, bf16[176,128]{1,0:T(8,128)(2,1)S(1)}, u32[]{:S(2)}, u32[]{:S(2)}) collective-permute-start(bf16[176,128]{1,0:T(8,128)(2,1)S(1)} %fusion.3), channel_id=1, source_target_pairs={{0,128},{4,132},{8,136},{12,140},{16,144},{20,148},{24,152},{28,15... | collective-permute-start | bytes 135176 | tf_op jit(solution)/shard_map/ppermute | solution.py:484
  96.5 1.1 collective-permute-start.26
  97.9 6.0 %collective-permute-start.16 = (bf16[3,176,128]{2,1,0:T(8,128)(2,1)S(1)}, bf16[3,176,128]{2,1,0:T(8,128)(2,1)S(1)}, u32[]{:S(2)}, u32[]{:S(2)}) collective-permute-start(bf16[3,176,128]{2,1,0:T(8,128)(2,1)S(1)} %copy-done.30), channel_id=1, source_target_pairs={{64,144},{68,148},{72,152},{76,156},{80,128},{84,132},{88,136},{92... | collective-permute-start | bytes 405512 | tf_op jit(solution)/shard_map/ppermute | solution.py:481
  103.9 0.6 collective-permute-start.27
  104.6 2.1 %collective-permute-start.20 = (bf16[4,176,128]{2,1,0:T(8,128)(2,1)S(1)}, bf16[4,176,128]{2,1,0:T(8,128)(2,1)S(1)}, u32[]{:S(2)}, u32[]{:S(2)}) collective-permute-start(bf16[4,176,128]{2,1,0:T(8,128)(2,1)S(1)} %copy-done.26), channel_id=1, source_target_pairs={{64,128},{68,132},{72,136},{76,140},{80,144},{84,148},{88,152},{92... | collective-permute-start | bytes 540680 | tf_op jit(solution)/shard_map/ppermute | solution.py:481
  106.7 0.7 collective-permute-start.21
  107.4 6.4 %collective-permute-start.28 = (bf16[176,128]{1,0:T(8,128)(2,1)S(1)}, bf16[176,128]{1,0:T(8,128)(2,1)S(1)}, u32[]{:S(2)}, u32[]{:S(2)}) collective-permute-start(bf16[176,128]{1,0:T(8,128)(2,1)S(1)} %add_convert_fusion.1), channel_id=1, source_target_pairs={{0,16},{4,20},{8,24},{12,28},{16,0},{20,4},{24,8},{28,12},{32,48},... | collective-permute-start | bytes 135176 | tf_op jit(solution)/shard_map/ppermute | solution.py:484
  113.8 1.5 %collective-permute-start.29 = (bf16[176,128]{1,0:T(8,128)(2,1)S(1)}, bf16[176,128]{1,0:T(8,128)(2,1)S(1)}, u32[]{:S(2)}, u32[]{:S(2)}) collective-permute-start(bf16[176,128]{1,0:T(8,128)(2,1)S(1)} %add_convert_fusion.1), channel_id=1, source_target_pairs={{0,32},{4,36},{8,40},{12,44},{16,48},{20,52},{24,56},{28,60},{32,0... | collective-permute-start | bytes 135176 | tf_op jit(solution)/shard_map/ppermute | solution.py:484
  115.4 1.9 %collective-permute-start.30 = (bf16[176,128]{1,0:T(8,128)(2,1)S(1)}, bf16[176,128]{1,0:T(8,128)(2,1)S(1)}, u32[]{:S(2)}, u32[]{:S(2)}) collective-permute-start(bf16[176,128]{1,0:T(8,128)(2,1)S(1)} %add_convert_fusion.1), channel_id=1, source_target_pairs={{0,48},{4,52},{8,56},{12,60},{16,32},{20,36},{24,40},{28,44},{32,1... | collective-permute-start | bytes 135176 | tf_op jit(solution)/shard_map/ppermute | solution.py:484
  117.5 5.5 %collective-permute-start.22 = (bf16[10,176,128]{2,1,0:T(8,128)(2,1)S(1)}, bf16[10,176,128]{2,1,0:T(8,128)(2,1)S(1)}, u32[]{:S(2)}, u32[]{:S(2)}) collective-permute-start(bf16[10,176,128]{2,1,0:T(8,128)(2,1)S(1)} %get-tuple-element.96), channel_id=1, source_target_pairs={{0,4},{4,0},{8,12},{12,8},{16,20},{20,16},{24,28},{28,24},{32,36},... | collective-permute-start | bytes 1351688 | tf_op jit(solution)/shard_map/ppermute | solution.py:451
  122.9 0.7 collective-permute-start.23
  123.8 1.1 collective-permute-start.32
  124.9 2.7 %collective-permute-start.33 = (bf16[176,128]{1,0:T(8,128)(2,1)S(1)}, bf16[176,128]{1,0:T(8,128)(2,1)S(1)}, u32[]{:S(2)}, u32[]{:S(2)}) collective-permute-start(bf16[176,128]{1,0:T(8,128)(2,1)S(1)} %add_convert_fusion), channel_id=1, source_target_pairs={{0,3},{1,2},{2,1},{3,0},{4,7},{5,6},{6,5},{7,4},{8,11},{9,10},{10,... | collective-permute-start | bytes 135176 | tf_op jit(solution)/shard_map/ppermute | solution.py:487
  127.6 0.6 collective-permute-done.32
  128.3 0.8 collective-permute-done.33
  129.1 7.2 %collective-permute-start.34 = (bf16[4,176,128]{2,1,0:T(8,128)(2,1)S(1)}, bf16[4,176,128]{2,1,0:T(8,128)(2,1)S(1)}, u32[]{:S(2)}, u32[]{:S(2)}) collective-permute-start(bf16[4,176,128]{2,1,0:T(8,128)(2,1)S(1)} %pad_maximum_fusion.2.refs_1_), channel_id=1, source_target_pairs={{0,4},{4,0},{8,12},{12,8},{16,20},{20,16},{24,28},{28,24},{32,36},... | collective-permute-start | bytes 540680 | tf_op jit(solution)/shard_map/ppermute | solution.py:484
  136.3 0.7 pad_add_fusion.refs_0_
  137.0 0.7 copy-done.2
  137.9 3.4 %shard_map.122 = bf16[6,64,512]{2,1,0:T(8,128)(2,1)} custom-call(s32[1]{0:T(128)} %bitcast.me_ref, s32[2,64]{1,0:T(2,128)} %bitcast.68, s32[6,1,512]{2,1,0:T(1,128)} %bitcast.63, f32[6,64,512]{2,1,0:T(8,128)} %get-tuple-element.50.center_ref, f32[6,176,128]{2,1,0:T(8,128)} %get-tuple-element.51.gown_ref, bf16[4,176,128]{2,1,0:T(8,128)(2,1)} %copy-done.4, ...), custom_call_target="tpu_custom_call" | custom-call | bytes 3895812 | tf_op jit(solution)/shard_map/pallas_call | solution.py:427
  141.3 0.7 copy-done.12
  142.0 2.4 %shard_map.123 = (f32[27,64,64]{2,1,0:T(8,128)}, f32[8,64,128]{2,1,0:T(8,128)}) custom-call(s32[2]{0:T(128)} %pad_add_fusion.refs_0_, bf16[4,176,128]{2,1,0:T(8,128)(2,1)} %copy-done.1, bf16[4,176,128]{2,1,0:T(8,128)(2,1)} %copy-done.12), custom_call_target="tpu_custom_call" | custom-call | bytes 1064968 | tf_op jit(solution)/shard_map/pallas_call | solution.py:427
  (117 shorter events, 2.9 us)
Async XLA Ops:
  4.3 18.0 %collective-permute-start = (bf16[4,176,128]{2,1,0:T(8,128)(2,1)}, bf16[4,176,128]{2,1,0:T(8,128)(2,1)S(1)}, u32[]{:S(2)}, u32[]{:S(2)}) collective-permute-start(bf16[4,176,128]{2,1,0:T(8,128)(2,1)} %get-tuple-element.39), channel_id=1, source_target_pairs={{0,16},{4,20},{8,24},{12,28},{16,0},{20,4},{24,8},{28,12},{32,48},... | collective-permute-start | bytes 540680 | tf_op jit(solution)/shard_map/ppermute | solution.py:439
  7.3 20.0 %collective-permute-start.1 = (bf16[4,176,128]{2,1,0:T(8,128)(2,1)}, bf16[4,176,128]{2,1,0:T(8,128)(2,1)S(1)}, u32[]{:S(2)}, u32[]{:S(2)}) collective-permute-start(bf16[4,176,128]{2,1,0:T(8,128)(2,1)} %get-tuple-element.40), channel_id=1, source_target_pairs={{16,32},{20,36},{24,40},{28,44},{32,16},{36,20},{40,24},{44,28},{8... | collective-permute-start | bytes 540680 | tf_op jit(solution)/shard_map/ppermute | solution.py:439
  8.0 23.6 %collective-permute-start.2 = (bf16[3,176,128]{2,1,0:T(8,128)(2,1)}, bf16[3,176,128]{2,1,0:T(8,128)(2,1)S(1)}, u32[]{:S(2)}, u32[]{:S(2)}) collective-permute-start(bf16[3,176,128]{2,1,0:T(8,128)(2,1)} %get-tuple-element.41), channel_id=1, source_target_pairs={{0,144},{4,148},{8,152},{12,156},{16,128},{20,132},{24,136},{28,14... | collective-permute-start | bytes 405512 | tf_op jit(solution)/shard_map/ppermute | solution.py:439
  15.5 17.4 %collective-permute-start.3 = (bf16[4,176,128]{2,1,0:T(8,128)(2,1)}, bf16[4,176,128]{2,1,0:T(8,128)(2,1)S(1)}, u32[]{:S(2)}, u32[]{:S(2)}) collective-permute-start(bf16[4,176,128]{2,1,0:T(8,128)(2,1)} %get-tuple-element.42), channel_id=1, source_target_pairs={{0,128},{4,132},{8,136},{12,140},{16,144},{20,148},{24,152},{28,15... | collective-permute-start | bytes 540680 | tf_op jit(solution)/shard_map/ppermute | solution.py:439
  16.5 17.1 %collective-permute-start.4 = (bf16[3,176,128]{2,1,0:T(8,128)(2,1)}, bf16[3,176,128]{2,1,0:T(8,128)(2,1)S(1)}, u32[]{:S(2)}, u32[]{:S(2)}) collective-permute-start(bf16[3,176,128]{2,1,0:T(8,128)(2,1)} %get-tuple-element.43), channel_id=1, source_target_pairs={{16,160},{20,164},{24,168},{28,172},{32,144},{36,148},{40,152},{44... | collective-permute-start | bytes 405512 | tf_op jit(solution)/shard_map/ppermute | solution.py:439
  20.1 1.5 %copy-start.14 = (bf16[2,176,128]{2,1,0:T(8,128)(2,1)S(1)}, bf16[2,176,128]{2,1,0:T(8,128)(2,1)}, u32[]{:S(2)}) copy-start(bf16[2,176,128]{2,1,0:T(8,128)(2,1)} %get-tuple-element.47) | copy-start | bytes 270340
  20.1 1.5 %copy-start.15 = (bf16[2,176,128]{2,1,0:T(8,128)(2,1)S(1)}, bf16[2,176,128]{2,1,0:T(8,128)(2,1)}, u32[]{:S(2)}) copy-start(bf16[2,176,128]{2,1,0:T(8,128)(2,1)} %get-tuple-element.48) | copy-start | bytes 270340
  20.7 1.6 %copy-start.28 = (bf16[3,176,128]{2,1,0:T(8,128)(2,1)S(1)}, bf16[3,176,128]{2,1,0:T(8,128)(2,1)}, u32[]{:S(2)}) copy-start(bf16[3,176,128]{2,1,0:T(8,128)(2,1)} %get-tuple-element.44) | copy-start | bytes 405508
  20.7 6.5 %copy-start.25 = (bf16[4,176,128]{2,1,0:T(8,128)(2,1)S(1)}, bf16[4,176,128]{2,1,0:T(8,128)(2,1)}, u32[]{:S(2)}) copy-start(bf16[4,176,128]{2,1,0:T(8,128)(2,1)} %get-tuple-element.45) | copy-start | bytes 540676
  20.7 10.8 %copy-start.27 = (bf16[3,176,128]{2,1,0:T(8,128)(2,1)S(1)}, bf16[3,176,128]{2,1,0:T(8,128)(2,1)}, u32[]{:S(2)}) copy-start(bf16[3,176,128]{2,1,0:T(8,128)(2,1)} %get-tuple-element.46) | copy-start | bytes 405508
  21.6 18.5 %copy-start = (bf16[27,64,64]{2,1,0:T(8,128)(2,1)S(1)}, bf16[27,64,64]{2,1,0:T(8,128)(2,1)}, u32[]{:S(2)}) copy-start(bf16[27,64,64]{2,1,0:T(8,128)(2,1)} %param.13) | copy-start | bytes 663556
  22.3 18.1 %copy-start.20 = (bf16[4,176,128]{2,1,0:T(8,128)(2,1)}, bf16[4,176,128]{2,1,0:T(8,128)(2,1)S(1)}, u32[]{:S(2)}) copy-start(bf16[4,176,128]{2,1,0:T(8,128)(2,1)S(1)} %collective-permute-done.rest_0_) | copy-start | bytes 540676
  22.3 11.9 %collective-permute-start.5 = (bf16[3,176,128]{2,1,0:T(8,128)(2,1)S(1)}, bf16[3,176,128]{2,1,0:T(8,128)(2,1)S(1)}, u32[]{:S(2)}, u32[]{:S(2)}) collective-permute-start(bf16[3,176,128]{2,1,0:T(8,128)(2,1)S(1)} %copy-done.28), channel_id=1, source_target_pairs={{64,144},{68,148},{72,152},{76,156},{80,128},{84,132},{88,136},{92... | collective-permute-start | bytes 405512 | tf_op jit(solution)/shard_map/ppermute | solution.py:439
  27.2 13.2 %copy-start.21 = (bf16[4,176,128]{2,1,0:T(8,128)(2,1)}, bf16[4,176,128]{2,1,0:T(8,128)(2,1)S(1)}, u32[]{:S(2)}) copy-start(bf16[4,176,128]{2,1,0:T(8,128)(2,1)S(1)} %collective-permute-done.1.rest_1_) | copy-start | bytes 540676
  27.3 7.7 %collective-permute-start.6 = (bf16[4,176,128]{2,1,0:T(8,128)(2,1)S(1)}, bf16[4,176,128]{2,1,0:T(8,128)(2,1)S(1)}, u32[]{:S(2)}, u32[]{:S(2)}) collective-permute-start(bf16[4,176,128]{2,1,0:T(8,128)(2,1)S(1)} %copy-done.25), channel_id=1, source_target_pairs={{64,128},{68,132},{72,136},{76,140},{80,144},{84,148},{88,152},{92... | collective-permute-start | bytes 540680 | tf_op jit(solution)/shard_map/ppermute | solution.py:439
  31.5 8.9 %copy-start.16 = (bf16[3,176,128]{2,1,0:T(8,128)(2,1)}, bf16[3,176,128]{2,1,0:T(8,128)(2,1)S(1)}, u32[]{:S(2)}) copy-start(bf16[3,176,128]{2,1,0:T(8,128)(2,1)S(1)} %collective-permute-done.2.rest_2_) | copy-start | bytes 405508
  31.6 4.1 %collective-permute-start.7 = (bf16[3,176,128]{2,1,0:T(8,128)(2,1)S(1)}, bf16[3,176,128]{2,1,0:T(8,128)(2,1)S(1)}, u32[]{:S(2)}, u32[]{:S(2)}) collective-permute-start(bf16[3,176,128]{2,1,0:T(8,128)(2,1)S(1)} %copy-done.27), channel_id=1, source_target_pairs={{80,160},{84,164},{88,168},{92,172},{96,144},{100,148},{104,152},{... | collective-permute-start | bytes 405512 | tf_op jit(solution)/shard_map/ppermute | solution.py:439
  32.9 7.5 %copy-start.22 = (bf16[4,176,128]{2,1,0:T(8,128)(2,1)}, bf16[4,176,128]{2,1,0:T(8,128)(2,1)S(1)}, u32[]{:S(2)}) copy-start(bf16[4,176,128]{2,1,0:T(8,128)(2,1)S(1)} %collective-permute-done.3.rest_3_) | copy-start | bytes 540676
  33.6 6.9 %copy-start.17 = (bf16[3,176,128]{2,1,0:T(8,128)(2,1)}, bf16[3,176,128]{2,1,0:T(8,128)(2,1)S(1)}, u32[]{:S(2)}) copy-start(bf16[3,176,128]{2,1,0:T(8,128)(2,1)S(1)} %collective-permute-done.4.rest_4_) | copy-start | bytes 405508
  34.2 6.5 %copy-start.18 = (bf16[3,176,128]{2,1,0:T(8,128)(2,1)}, bf16[3,176,128]{2,1,0:T(8,128)(2,1)S(1)}, u32[]{:S(2)}) copy-start(bf16[3,176,128]{2,1,0:T(8,128)(2,1)S(1)} %collective-permute-done.5.rest_5_) | copy-start | bytes 405508
  34.9 5.8 %copy-start.23 = (bf16[4,176,128]{2,1,0:T(8,128)(2,1)}, bf16[4,176,128]{2,1,0:T(8,128)(2,1)S(1)}, u32[]{:S(2)}) copy-start(bf16[4,176,128]{2,1,0:T(8,128)(2,1)S(1)} %collective-permute-done.6.rest_6_) | copy-start | bytes 540676
  35.6 5.1 %copy-start.19 = (bf16[3,176,128]{2,1,0:T(8,128)(2,1)}, bf16[3,176,128]{2,1,0:T(8,128)(2,1)S(1)}, u32[]{:S(2)}) copy-start(bf16[3,176,128]{2,1,0:T(8,128)(2,1)S(1)} %collective-permute-done.7.rest_7_) | copy-start | bytes 405508
  36.3 8.3 %collective-permute-start.8 = (bf16[10,176,128]{2,1,0:T(8,128)(2,1)}, bf16[10,176,128]{2,1,0:T(8,128)(2,1)}, u32[]{:S(2)}, u32[]{:S(2)}) collective-permute-start(bf16[10,176,128]{2,1,0:T(8,128)(2,1)} %get-tuple-element.104), channel_id=1, source_target_pairs={{0,4},{4,0},{8,12},{12,8},{16,20},{20,16},{24,28},{28,24},{32,36},... | collective-permute-start | bytes 1351688 | tf_op jit(solution)/shard_map/ppermute | solution.py:451
  38.7 6.0 %collective-permute-start.9 = (bf16[10,176,128]{2,1,0:T(8,128)(2,1)}, bf16[10,176,128]{2,1,0:T(8,128)(2,1)}, u32[]{:S(2)}, u32[]{:S(2)}) collective-permute-start(bf16[10,176,128]{2,1,0:T(8,128)(2,1)} %get-tuple-element.103), channel_id=1, source_target_pairs={{4,8},{8,4},{20,24},{24,20},{36,40},{40,36},{52,56},{56,52},{68,72... | collective-permute-start | bytes 1351688 | tf_op jit(solution)/shard_map/ppermute | solution.py:451
  42.0 1.4 copy-start.13
  64.5 26.4 %copy-start.31 = (bf16[3,176,128]{2,1,0:T(8,128)(2,1)S(1)}, bf16[3,176,128]{2,1,0:T(8,128)(2,1)}, u32[]{:S(2)}) copy-start(bf16[3,176,128]{2,1,0:T(8,128)(2,1)} %get-tuple-element.59) | copy-start | bytes 405508
  65.6 20.1 %collective-permute-start.14 = (bf16[4,176,128]{2,1,0:T(8,128)(2,1)S(1)}, bf16[4,176,128]{2,1,0:T(8,128)(2,1)S(1)}, u32[]{:S(2)}, u32[]{:S(2)}) collective-permute-start(bf16[4,176,128]{2,1,0:T(8,128)(2,1)S(1)} %fusion), channel_id=1, source_target_pairs={{0,4},{4,0},{8,12},{12,8},{16,20},{20,16},{24,28},{28,24},{32,36},... | collective-permute-start | bytes 540680 | tf_op jit(solution)/shard_map/ppermute | solution.py:484
  69.7 18.5 %collective-permute-start.10 = (bf16[4,176,128]{2,1,0:T(8,128)(2,1)}, bf16[4,176,128]{2,1,0:T(8,128)(2,1)S(1)}, u32[]{:S(2)}, u32[]{:S(2)}) collective-permute-start(bf16[4,176,128]{2,1,0:T(8,128)(2,1)} %get-tuple-element.52), channel_id=1, source_target_pairs={{0,16},{4,20},{8,24},{12,28},{16,0},{20,4},{24,8},{28,12},{32,48},... | collective-permute-start | bytes 540680 | tf_op jit(solution)/shard_map/ppermute | solution.py:481
  76.0 14.7 %collective-permute-start.11 = (bf16[4,176,128]{2,1,0:T(8,128)(2,1)}, bf16[4,176,128]{2,1,0:T(8,128)(2,1)S(1)}, u32[]{:S(2)}, u32[]{:S(2)}) collective-permute-start(bf16[4,176,128]{2,1,0:T(8,128)(2,1)} %get-tuple-element.53), channel_id=1, source_target_pairs={{16,32},{20,36},{24,40},{28,44},{32,16},{36,20},{40,24},{44,28},{8... | collective-permute-start | bytes 540680 | tf_op jit(solution)/shard_map/ppermute | solution.py:481
  76.6 19.9 %collective-permute-start.12 = (bf16[3,176,128]{2,1,0:T(8,128)(2,1)}, bf16[3,176,128]{2,1,0:T(8,128)(2,1)S(1)}, u32[]{:S(2)}, u32[]{:S(2)}) collective-permute-start(bf16[3,176,128]{2,1,0:T(8,128)(2,1)} %get-tuple-element.54), channel_id=1, source_target_pairs={{0,144},{4,148},{8,152},{12,156},{16,128},{20,132},{24,136},{28,14... | collective-permute-start | bytes 405512 | tf_op jit(solution)/shard_map/ppermute | solution.py:481
  76.7 27.8 %collective-permute-start.13 = (bf16[4,176,128]{2,1,0:T(8,128)(2,1)}, bf16[4,176,128]{2,1,0:T(8,128)(2,1)S(1)}, u32[]{:S(2)}, u32[]{:S(2)}) collective-permute-start(bf16[4,176,128]{2,1,0:T(8,128)(2,1)} %get-tuple-element.55), channel_id=1, source_target_pairs={{0,128},{4,132},{8,136},{12,140},{16,144},{20,148},{24,152},{28,15... | collective-permute-start | bytes 540680 | tf_op jit(solution)/shard_map/ppermute | solution.py:481
  84.8 13.1 %copy-start.30 = (bf16[3,176,128]{2,1,0:T(8,128)(2,1)S(1)}, bf16[3,176,128]{2,1,0:T(8,128)(2,1)}, u32[]{:S(2)}) copy-start(bf16[3,176,128]{2,1,0:T(8,128)(2,1)} %get-tuple-element.60) | copy-start | bytes 405508
  85.7 18.8 %copy-start.26 = (bf16[4,176,128]{2,1,0:T(8,128)(2,1)S(1)}, bf16[4,176,128]{2,1,0:T(8,128)(2,1)}, u32[]{:S(2)}) copy-start(bf16[4,176,128]{2,1,0:T(8,128)(2,1)} %get-tuple-element.63) | copy-start | bytes 540676
  85.8 20.9 %copy-start.29 = (bf16[3,176,128]{2,1,0:T(8,128)(2,1)S(1)}, bf16[3,176,128]{2,1,0:T(8,128)(2,1)}, u32[]{:S(2)}) copy-start(bf16[3,176,128]{2,1,0:T(8,128)(2,1)} %get-tuple-element.64) | copy-start | bytes 405508
  86.9 4.1 %collective-permute-start.17 = (bf16[176,128]{1,0:T(8,128)(2,1)S(1)}, bf16[176,128]{1,0:T(8,128)(2,1)S(1)}, u32[]{:S(2)}, u32[]{:S(2)}) collective-permute-start(bf16[176,128]{1,0:T(8,128)(2,1)S(1)} %get-tuple-element.86), channel_id=1, source_target_pairs={{0,1},{1,0},{2,3},{3,2},{4,5},{5,4},{6,7},{7,6},{8,9},{9,8},{10,11... | collective-permute-start | bytes 135176 | tf_op jit(solution)/shard_map/ppermute | solution.py:487
  88.2 40.9 %copy-start.4 = (bf16[4,176,128]{2,1,0:T(8,128)(2,1)}, bf16[4,176,128]{2,1,0:T(8,128)(2,1)S(1)}, u32[]{:S(2)}) copy-start(bf16[4,176,128]{2,1,0:T(8,128)(2,1)S(1)} %collective-permute-done.10.rest_0_) | copy-start | bytes 540676
  88.2 4.4 %collective-permute-start.18 = (bf16[176,128]{1,0:T(8,128)(2,1)S(1)}, bf16[176,128]{1,0:T(8,128)(2,1)S(1)}, u32[]{:S(2)}, u32[]{:S(2)}) collective-permute-start(bf16[176,128]{1,0:T(8,128)(2,1)S(1)} %get-tuple-element.85), channel_id=1, source_target_pairs={{0,2},{1,3},{2,0},{3,1},{4,6},{5,7},{6,4},{7,5},{8,10},{9,11},{10,... | collective-permute-start | bytes 135176 | tf_op jit(solution)/shard_map/ppermute | solution.py:487
  90.7 38.4 %copy-start.5 = (bf16[4,176,128]{2,1,0:T(8,128)(2,1)}, bf16[4,176,128]{2,1,0:T(8,128)(2,1)S(1)}, u32[]{:S(2)}) copy-start(bf16[4,176,128]{2,1,0:T(8,128)(2,1)S(1)} %collective-permute-done.11.rest_1_) | copy-start | bytes 540676
  90.7 4.2 %collective-permute-start.19 = (bf16[176,128]{1,0:T(8,128)(2,1)S(1)}, bf16[176,128]{1,0:T(8,128)(2,1)S(1)}, u32[]{:S(2)}, u32[]{:S(2)}) collective-permute-start(bf16[176,128]{1,0:T(8,128)(2,1)S(1)} %get-tuple-element.84), channel_id=1, source_target_pairs={{0,3},{1,2},{2,1},{3,0},{4,7},{5,6},{6,5},{7,4},{8,11},{9,10},{10,... | collective-permute-start | bytes 135176 | tf_op jit(solution)/shard_map/ppermute | solution.py:487
  91.0 22.8 %collective-permute-start.15 = (bf16[3,176,128]{2,1,0:T(8,128)(2,1)S(1)}, bf16[3,176,128]{2,1,0:T(8,128)(2,1)S(1)}, u32[]{:S(2)}, u32[]{:S(2)}) collective-permute-start(bf16[3,176,128]{2,1,0:T(8,128)(2,1)S(1)} %copy-done.31), channel_id=1, source_target_pairs={{16,160},{20,164},{24,168},{28,172},{32,144},{36,148},{40,152},{44... | collective-permute-start | bytes 405512 | tf_op jit(solution)/shard_map/ppermute | solution.py:481
  94.9 3.0 %collective-permute-start.24 = (bf16[176,128]{1,0:T(8,128)(2,1)S(1)}, bf16[176,128]{1,0:T(8,128)(2,1)S(1)}, u32[]{:S(2)}, u32[]{:S(2)}) collective-permute-start(bf16[176,128]{1,0:T(8,128)(2,1)S(1)} %fusion.3), channel_id=1, source_target_pairs={{0,64},{4,68},{8,72},{12,76},{16,80},{20,84},{24,88},{28,92},{32,9... | collective-permute-start | bytes 135176 | tf_op jit(solution)/shard_map/ppermute | solution.py:484
  95.0 8.9 %collective-permute-start.25 = (bf16[176,128]{1,0:T(8,128)(2,1)S(1)}, bf16[176,128]{1,0:T(8,128)(2,1)S(1)}, u32[]{:S(2)}, u32[]{:S(2)}) collective-permute-start(bf16[176,128]{1,0:T(8,128)(2,1)S(1)} %fusion.3), channel_id=1, source_target_pairs={{0,128},{4,132},{8,136},{12,140},{16,144},{20,148},{24,152},{28,15... | collective-permute-start | bytes 135176 | tf_op jit(solution)/shard_map/ppermute | solution.py:484
  96.5 40.5 %copy-start.8 = (bf16[3,176,128]{2,1,0:T(8,128)(2,1)}, bf16[3,176,128]{2,1,0:T(8,128)(2,1)S(1)}, u32[]{:S(2)}) copy-start(bf16[3,176,128]{2,1,0:T(8,128)(2,1)S(1)} %collective-permute-done.12.rest_2_) | copy-start | bytes 405508
  96.5 7.4 %collective-permute-start.26 = (bf16[176,128]{1,0:T(8,128)(2,1)S(1)}, bf16[176,128]{1,0:T(8,128)(2,1)S(1)}, u32[]{:S(2)}, u32[]{:S(2)}) collective-permute-start(bf16[176,128]{1,0:T(8,128)(2,1)S(1)} %fusion.3), channel_id=1, source_target_pairs={{0,192},{4,196},{8,200},{12,204},{16,208},{20,212},{24,216},{28,22... | collective-permute-start | bytes 135176 | tf_op jit(solution)/shard_map/ppermute | solution.py:484
  97.9 17.5 %collective-permute-start.16 = (bf16[3,176,128]{2,1,0:T(8,128)(2,1)S(1)}, bf16[3,176,128]{2,1,0:T(8,128)(2,1)S(1)}, u32[]{:S(2)}, u32[]{:S(2)}) collective-permute-start(bf16[3,176,128]{2,1,0:T(8,128)(2,1)S(1)} %copy-done.30), channel_id=1, source_target_pairs={{64,144},{68,148},{72,152},{76,156},{80,128},{84,132},{88,136},{92... | collective-permute-start | bytes 405512 | tf_op jit(solution)/shard_map/ppermute | solution.py:481
  103.9 3.4 %collective-permute-start.27 = (bf16[176,128]{1,0:T(8,128)(2,1)S(1)}, bf16[176,128]{1,0:T(8,128)(2,1)S(1)}, u32[]{:S(2)}, u32[]{:S(2)}) collective-permute-start(bf16[176,128]{1,0:T(8,128)(2,1)S(1)} %add_convert_fusion.2), channel_id=1, source_target_pairs={{0,8},{4,12},{8,0},{12,4},{16,24},{20,28},{24,16},{28,20},{32,40},... | collective-permute-start | bytes 135176 | tf_op jit(solution)/shard_map/ppermute | solution.py:484
  104.6 32.4 %copy-start.6 = (bf16[4,176,128]{2,1,0:T(8,128)(2,1)}, bf16[4,176,128]{2,1,0:T(8,128)(2,1)S(1)}, u32[]{:S(2)}) copy-start(bf16[4,176,128]{2,1,0:T(8,128)(2,1)S(1)} %collective-permute-done.13.rest_3_) | copy-start | bytes 540676
  104.6 12.8 %collective-permute-start.20 = (bf16[4,176,128]{2,1,0:T(8,128)(2,1)S(1)}, bf16[4,176,128]{2,1,0:T(8,128)(2,1)S(1)}, u32[]{:S(2)}, u32[]{:S(2)}) collective-permute-start(bf16[4,176,128]{2,1,0:T(8,128)(2,1)S(1)} %copy-done.26), channel_id=1, source_target_pairs={{64,128},{68,132},{72,136},{76,140},{80,144},{84,148},{88,152},{92... | collective-permute-start | bytes 540680 | tf_op jit(solution)/shard_map/ppermute | solution.py:481
  106.7 10.7 %collective-permute-start.21 = (bf16[3,176,128]{2,1,0:T(8,128)(2,1)S(1)}, bf16[3,176,128]{2,1,0:T(8,128)(2,1)S(1)}, u32[]{:S(2)}, u32[]{:S(2)}) collective-permute-start(bf16[3,176,128]{2,1,0:T(8,128)(2,1)S(1)} %copy-done.29), channel_id=1, source_target_pairs={{80,160},{84,164},{88,168},{92,172},{96,144},{100,148},{104,152},{... | collective-permute-start | bytes 405512 | tf_op jit(solution)/shard_map/ppermute | solution.py:481
  107.4 16.2 %collective-permute-start.28 = (bf16[176,128]{1,0:T(8,128)(2,1)S(1)}, bf16[176,128]{1,0:T(8,128)(2,1)S(1)}, u32[]{:S(2)}, u32[]{:S(2)}) collective-permute-start(bf16[176,128]{1,0:T(8,128)(2,1)S(1)} %add_convert_fusion.1), channel_id=1, source_target_pairs={{0,16},{4,20},{8,24},{12,28},{16,0},{20,4},{24,8},{28,12},{32,48},... | collective-permute-start | bytes 135176 | tf_op jit(solution)/shard_map/ppermute | solution.py:484
  113.8 23.2 %copy-start.9 = (bf16[3,176,128]{2,1,0:T(8,128)(2,1)}, bf16[3,176,128]{2,1,0:T(8,128)(2,1)S(1)}, u32[]{:S(2)}) copy-start(bf16[3,176,128]{2,1,0:T(8,128)(2,1)S(1)} %collective-permute-done.15.rest_4_) | copy-start | bytes 405508
  113.8 9.8 %collective-permute-start.29 = (bf16[176,128]{1,0:T(8,128)(2,1)S(1)}, bf16[176,128]{1,0:T(8,128)(2,1)S(1)}, u32[]{:S(2)}, u32[]{:S(2)}) collective-permute-start(bf16[176,128]{1,0:T(8,128)(2,1)S(1)} %add_convert_fusion.1), channel_id=1, source_target_pairs={{0,32},{4,36},{8,40},{12,44},{16,48},{20,52},{24,56},{28,60},{32,0... | collective-permute-start | bytes 135176 | tf_op jit(solution)/shard_map/ppermute | solution.py:484
  115.4 21.6 %copy-start.10 = (bf16[3,176,128]{2,1,0:T(8,128)(2,1)}, bf16[3,176,128]{2,1,0:T(8,128)(2,1)S(1)}, u32[]{:S(2)}) copy-start(bf16[3,176,128]{2,1,0:T(8,128)(2,1)S(1)} %collective-permute-done.16.rest_5_) | copy-start | bytes 405508
  115.4 8.2 %collective-permute-start.30 = (bf16[176,128]{1,0:T(8,128)(2,1)S(1)}, bf16[176,128]{1,0:T(8,128)(2,1)S(1)}, u32[]{:S(2)}, u32[]{:S(2)}) collective-permute-start(bf16[176,128]{1,0:T(8,128)(2,1)S(1)} %add_convert_fusion.1), channel_id=1, source_target_pairs={{0,48},{4,52},{8,56},{12,60},{16,32},{20,36},{24,40},{28,44},{32,1... | collective-permute-start | bytes 135176 | tf_op jit(solution)/shard_map/ppermute | solution.py:484
  117.4 19.6 %copy-start.7 = (bf16[4,176,128]{2,1,0:T(8,128)(2,1)}, bf16[4,176,128]{2,1,0:T(8,128)(2,1)S(1)}, u32[]{:S(2)}) copy-start(bf16[4,176,128]{2,1,0:T(8,128)(2,1)S(1)} %collective-permute-done.20.rest_6_) | copy-start | bytes 540676
  117.4 19.6 %copy-start.11 = (bf16[3,176,128]{2,1,0:T(8,128)(2,1)}, bf16[3,176,128]{2,1,0:T(8,128)(2,1)S(1)}, u32[]{:S(2)}) copy-start(bf16[3,176,128]{2,1,0:T(8,128)(2,1)S(1)} %collective-permute-done.21.rest_7_) | copy-start | bytes 405508
  117.5 19.5 %collective-permute-start.22 = (bf16[10,176,128]{2,1,0:T(8,128)(2,1)S(1)}, bf16[10,176,128]{2,1,0:T(8,128)(2,1)S(1)}, u32[]{:S(2)}, u32[]{:S(2)}) collective-permute-start(bf16[10,176,128]{2,1,0:T(8,128)(2,1)S(1)} %get-tuple-element.96), channel_id=1, source_target_pairs={{0,4},{4,0},{8,12},{12,8},{16,20},{20,16},{24,28},{28,24},{32,36},... | collective-permute-start | bytes 1351688 | tf_op jit(solution)/shard_map/ppermute | solution.py:451
  122.9 14.0 %collective-permute-start.23 = (bf16[10,176,128]{2,1,0:T(8,128)(2,1)S(1)}, bf16[10,176,128]{2,1,0:T(8,128)(2,1)S(1)}, u32[]{:S(2)}, u32[]{:S(2)}) collective-permute-start(bf16[10,176,128]{2,1,0:T(8,128)(2,1)S(1)} %get-tuple-element.95), channel_id=1, source_target_pairs={{4,8},{8,4},{20,24},{24,20},{36,40},{40,36},{52,56},{56,52},{68,72... | collective-permute-start | bytes 1351688 | tf_op jit(solution)/shard_map/ppermute | solution.py:451
  123.7 3.9 %collective-permute-start.31 = (bf16[176,128]{1,0:T(8,128)(2,1)S(1)}, bf16[176,128]{1,0:T(8,128)(2,1)S(1)}, u32[]{:S(2)}, u32[]{:S(2)}) collective-permute-start(bf16[176,128]{1,0:T(8,128)(2,1)S(1)} %add_convert_fusion), channel_id=1, source_target_pairs={{0,1},{1,0},{2,3},{3,2},{4,5},{5,4},{6,7},{7,6},{8,9},{9,8},{10,11... | collective-permute-start | bytes 135176 | tf_op jit(solution)/shard_map/ppermute | solution.py:487
  123.8 4.5 %collective-permute-start.32 = (bf16[176,128]{1,0:T(8,128)(2,1)S(1)}, bf16[176,128]{1,0:T(8,128)(2,1)S(1)}, u32[]{:S(2)}, u32[]{:S(2)}) collective-permute-start(bf16[176,128]{1,0:T(8,128)(2,1)S(1)} %add_convert_fusion), channel_id=1, source_target_pairs={{0,2},{1,3},{2,0},{3,1},{4,6},{5,7},{6,4},{7,5},{8,10},{9,11},{10,... | collective-permute-start | bytes 135176 | tf_op jit(solution)/shard_map/ppermute | solution.py:487
  124.9 4.2 %collective-permute-start.33 = (bf16[176,128]{1,0:T(8,128)(2,1)S(1)}, bf16[176,128]{1,0:T(8,128)(2,1)S(1)}, u32[]{:S(2)}, u32[]{:S(2)}) collective-permute-start(bf16[176,128]{1,0:T(8,128)(2,1)S(1)} %add_convert_fusion), channel_id=1, source_target_pairs={{0,3},{1,2},{2,1},{3,0},{4,7},{5,6},{6,5},{7,4},{8,11},{9,10},{10,... | collective-permute-start | bytes 135176 | tf_op jit(solution)/shard_map/ppermute | solution.py:487
  129.1 12.1 %copy-start.1 = (bf16[4,176,128]{2,1,0:T(8,128)(2,1)}, bf16[4,176,128]{2,1,0:T(8,128)(2,1)S(1)}, u32[]{:S(2)}) copy-start(bf16[4,176,128]{2,1,0:T(8,128)(2,1)S(1)} %pad_maximum_fusion.2.refs_1_) | copy-start | bytes 540676
  129.1 12.1 %collective-permute-start.34 = (bf16[4,176,128]{2,1,0:T(8,128)(2,1)S(1)}, bf16[4,176,128]{2,1,0:T(8,128)(2,1)S(1)}, u32[]{:S(2)}, u32[]{:S(2)}) collective-permute-start(bf16[4,176,128]{2,1,0:T(8,128)(2,1)S(1)} %pad_maximum_fusion.2.refs_1_), channel_id=1, source_target_pairs={{0,4},{4,0},{8,12},{12,8},{16,20},{20,16},{24,28},{28,24},{32,36},... | collective-permute-start | bytes 540680 | tf_op jit(solution)/shard_map/ppermute | solution.py:484
  137.0 0.9 copy-start.3
  (3 other events, 2.2 us)

commit v4 on v3

--- a/solution.py
+++ b/solution.py
@@ -187,9 +187,9 @@
     idx_ref, me_ref, own_ref, masked_ref, mask_ref, cot_ref, sel_ref, selt_ref, wf_ref, wb_ref, down_ref, *rest
 ):
     recv = rest[:10]
-    coarse_ref, center_ref, gown_ref, sums_ref = rest[10:14]
-    outs = rest[14:24]
-    ext, gext, pad, cols, slope, kids, grads, gcols, gpad = rest[24:]
+    coarse_ref, center_ref, gown_ref, kept_ref, away_ref = rest[10:15]
+    outs = rest[15:25]
+    ext, gext, pad, cols, slope, kids, grads, gcols, gpad, sums_ref = rest[25:]
     low8 = low_half((8, 128))
 
     for b in range(BD):
@@ -297,6 +297,10 @@
             low64, third[2 * m], pltpu.roll(third[2 * m + 1], 64, 1)
         )
 
+    half, core = 4 * SHELL, me_ref[0] % 2
+    kept_ref[...] = sums_ref[pl.ds(pl.multiple_of(core * half, 8), half), :]
+    away_ref[...] = sums_ref[pl.ds(pl.multiple_of((1 - core) * half, 8), half), :].astype(BF16)
+
     @pl.loop(0, BD)
     def _(b):
         mine = jnp.concatenate(
@@ -468,8 +472,7 @@
     return lax.optimization_barrier((tuple(values), earlier))[0]
 
 
-def exchange_and_sum(parts, sums, me, x, peers):
-    core = me % 2
+def exchange_and_sum(parts, kept, sent, x, peers):
     got = {}
 
     def plane(lo, hi, earlier=None):
@@ -495,9 +498,9 @@
             all_of = [all_of[i] + all_of[i + 1] for i in range(0, len(all_of), 2)]
         return all_of[0].astype(BF16)
 
-    halves = sums.reshape(2, 4, SHELL, 128)
+    shape = (4, SHELL, 128)
     plane(0, 4)
-    mine = one_of(halves, core) + swap(one_of(halves, 1 - core).astype(BF16), 1).astype(F32)
+    mine = kept.reshape(shape) + swap(sent.reshape(shape), 1).astype(F32)
     small = mine.astype(BF16)
     away = [one_of(small, jnp.bitwise_xor(x, k)) for k in (1, 2, 3)]
     plane(4, 6, tuple(away))
@@ -550,7 +553,8 @@
         jax.ShapeDtypeStruct((BD * HALF, HALF, LANES), BF16),
         jax.ShapeDtypeStruct((BD, ROWS, LANES), F32),
         jax.ShapeDtypeStruct((BD, SHELL, 128), F32),
-        jax.ShapeDtypeStruct((8 * SHELL, 128), F32),
+        jax.ShapeDtypeStruct((4 * SHELL, 128), F32),
+        jax.ShapeDtypeStruct((4 * SHELL, 128), BF16),
         *parts,
     ]
     scratch = [
@@ -563,11 +567,12 @@
         pltpu.VMEM((BD * ROWS, LANES), BF16),
         pltpu.VMEM((BD * PADR, 4 * GROUP), BF16),
         pltpu.VMEM((BD * PADR, PADL), F32),
+        pltpu.VMEM((8 * SHELL, 128), F32),
     ]
-    coarse, center, gown, sums, *back = call(
+    coarse, center, gown, kept, away, *back = call(
         main_kernel, outs, [idx, me_s, own, masked, mask, cot, sel, selt, wf, wb, down, *recv], 2, scratch, 10**10
     )
-    came, near, far = exchange_and_sum(back, sums, me, x, peers)
+    came, near, far = exchange_and_sum(back, kept, away, x, peers)
     [grad] = call(
         last_kernel,
         [brick],

time: 145 us -> 144 us (level)
  no operation moved by 1% of the time
where the time goes in v4:
time: 144 us; the launch traced here: 143 us
  starting transfers between devices  87.4 us (61%)
  Pallas kernels  29.2 us (20%)
  local copies, waits for them, and re-layouts  17.3 us (12%)
  waiting for transfers between devices  4.93 us (3%)
  other arithmetic  2.96 us (2%)
    pallas_call x4, Pallas kernels, call(): pl.pallas_call(kernel, out_shape=outs, in_specs=[spec_s] * smem + [spec_v...  29.2 us
    ppermute x9, starting transfers between devices, swap(): return lax.ppermute(v, 'spatial', [(d, d ^ bit) for d in range(peers)])  24.5 us
    ppermute x8, starting transfers between devices, plane(): got[k] = lax.ppermute(v, 'spatial', swap_pairs(peers, *k))  23.5 us
    ppermute x8, starting transfers between devices, exchange_plane(): lax.ppermute(v, 'spatial', swap_pairs(peers, a, b))  21.4 us
    ppermute x4, starting transfers between devices, exchange_along(): lax.ppermute(jnp.concatenate(pieces, axis=0), 'spatial', swaps[n])  9.92 us
    unnamed x81, local copies, waits for them, and re-layouts  9.28 us
    ppermute x6, starting transfers between devices, swap_x(): return lax.ppermute(v, 'dp', [(d, d ^ bit) for d in range(4)])  7.97 us
    ppermute x6, waiting for transfers between devices, swap_x(): return lax.ppermute(v, 'dp', [(d, d ^ bit) for d in range(4)])  4.63 us
  transfers between devices with their start and end apart: 35, of which 5 were waited for; matrix products, arithmetic and copies ran while one was open for 12% of the time, Pallas kernels for 2%

profile of v4, /device:TPU:41, one launch (start us, length us, event | category | flops | bytes accessed | tf_op | source)
XLA Modules:
  0.0 143.1 jit_solution(16558825044873578855)
XLA Ops:
  0.6 3.6 %shard_map.120 = (bf16[6,64,512]{2,1,0:T(8,128)(2,1)}, bf16[6,176,128]{2,1,0:T(8,128)(2,1)}, bf16[4,176,128]{2,1,0:T(8,128)(2,1)}, bf16[4,176,128]{2,1,0:T(8,128...) custom-call(s32[1]{0:T(128)} %bitcast.me_ref, ...), custom_call_target="tpu_custom_call" | custom-call | bytes 2511364 | tf_op jit(solution)/shard_map/pallas_call | solution.py:431
  4.3 3.0 %collective-permute-start = (bf16[4,176,128]{2,1,0:T(8,128)(2,1)}, bf16[4,176,128]{2,1,0:T(8,128)(2,1)S(1)}, u32[]{:S(2)}, u32[]{:S(2)}) collective-permute-start(bf16[4,176,128]{2,1,0:T(8,128)(2,1)} %get-tuple-element.40), channel_id=1, source_target_pairs={{0,16},{4,20},{8,24},{12,28},{16,0},{20,4},{24,8},{28,12},{32,48},... | collective-permute-start | bytes 540680 | tf_op jit(solution)/shard_map/ppermute | solution.py:443
  7.3 0.7 collective-permute-start.1
  8.0 7.5 %collective-permute-start.2 = (bf16[3,176,128]{2,1,0:T(8,128)(2,1)}, bf16[3,176,128]{2,1,0:T(8,128)(2,1)S(1)}, u32[]{:S(2)}, u32[]{:S(2)}) collective-permute-start(bf16[3,176,128]{2,1,0:T(8,128)(2,1)} %get-tuple-element.42), channel_id=1, source_target_pairs={{0,144},{4,148},{8,152},{12,156},{16,128},{20,132},{24,136},{28,14... | collective-permute-start | bytes 405512 | tf_op jit(solution)/shard_map/ppermute | solution.py:443
  15.5 1.0 collective-permute-start.3
  16.5 0.7 collective-permute-start.4
  17.1 1.0 reverse_bitcast_fusion
  18.8 0.3 copy-done.24
  19.2 0.9 copy.22
  20.2 0.5 reshape.61
  20.7 0.9 copy.23
  21.6 0.7 constant_dynamic-update-slice_fusion.8
  22.3 4.3 %collective-permute-start.5 = (bf16[3,176,128]{2,1,0:T(8,128)(2,1)S(1)}, bf16[3,176,128]{2,1,0:T(8,128)(2,1)S(1)}, u32[]{:S(2)}, u32[]{:S(2)}) collective-permute-start(bf16[3,176,128]{2,1,0:T(8,128)(2,1)S(1)} %copy-done.28), channel_id=1, source_target_pairs={{64,144},{68,148},{72,152},{76,156},{80,128},{84,132},{88,136},{92... | collective-permute-start | bytes 405512 | tf_op jit(solution)/shard_map/ppermute | solution.py:443
  26.6 0.6 constant_dynamic-update-slice_fusion.16
  27.2 3.6 %collective-permute-start.6 = (bf16[4,176,128]{2,1,0:T(8,128)(2,1)S(1)}, bf16[4,176,128]{2,1,0:T(8,128)(2,1)S(1)}, u32[]{:S(2)}, u32[]{:S(2)}) collective-permute-start(bf16[4,176,128]{2,1,0:T(8,128)(2,1)S(1)} %copy-done.25), channel_id=1, source_target_pairs={{64,128},{68,132},{72,136},{76,140},{80,144},{84,148},{88,152},{92... | collective-permute-start | bytes 540680 | tf_op jit(solution)/shard_map/ppermute | solution.py:443
  30.9 0.6 constant_dynamic-update-slice_fusion.15
  31.5 0.7 collective-permute-start.7
  32.2 0.6 constant_dynamic-update-slice_fusion.14
  32.9 0.7 constant_dynamic-update-slice_fusion.13
  33.6 0.7 constant_dynamic-update-slice_fusion.12
  34.2 0.7 constant_dynamic-update-slice_fusion.11
  34.9 0.7 constant_dynamic-update-slice_fusion.10
  35.6 0.7 constant_dynamic-update-slice_fusion.9
  36.3 2.4 %collective-permute-start.8 = (bf16[10,176,128]{2,1,0:T(8,128)(2,1)}, bf16[10,176,128]{2,1,0:T(8,128)(2,1)}, u32[]{:S(2)}, u32[]{:S(2)}) collective-permute-start(bf16[10,176,128]{2,1,0:T(8,128)(2,1)} %get-tuple-element.106), channel_id=1, source_target_pairs={{0,4},{4,0},{8,12},{12,8},{16,20},{20,16},{24,28},{28,24},{32,36},... | collective-permute-start | bytes 1351688 | tf_op jit(solution)/shard_map/ppermute | solution.py:455
  38.7 1.4 collective-permute-start.9
  40.7 1.2 copy.18
  42.0 0.5 reshape.59
  42.5 0.9 copy.19
  43.4 0.7 reshape.57.cot_ref
  44.1 0.6 fusion.14.idx_ref
  44.6 19.8 %shard_map.121 = (bf16[24,4,512]{2,1,0:T(4,128)(2,1)}, f32[6,64,512]{2,1,0:T(8,128)}, f32[6,176,128]{2,1,0:T(8,128)}, f32[704,128]{1,0:T(8,128)}, bf16[704,128]{...) custom-call(s32[162]{0:T(256)} %fusion.14.idx_ref, ...), custom_call_target="tpu_custom_call" | custom-call | flops 10000000000 | bytes 7914124 | tf_op jit(solution)/shard_map/pallas_call | solution.py:431
  64.4 4.1 %collective-permute-start.14 = (bf16[4,176,128]{2,1,0:T(8,128)(2,1)}, bf16[4,176,128]{2,1,0:T(8,128)(2,1)S(1)}, u32[]{:S(2)}, u32[]{:S(2)}) collective-permute-start(bf16[4,176,128]{2,1,0:T(8,128)(2,1)} %bitcast.64), channel_id=1, source_target_pairs={{0,4},{4,0},{8,12},{12,8},{16,20},{20,16},{24,28},{28,24},{32,36},... | collective-permute-start | bytes 540680 | tf_op jit(solution)/shard_map/ppermute | solution.py:487
  68.6 6.2 %collective-permute-start.10 = (bf16[4,176,128]{2,1,0:T(8,128)(2,1)}, bf16[4,176,128]{2,1,0:T(8,128)(2,1)S(1)}, u32[]{:S(2)}, u32[]{:S(2)}) collective-permute-start(bf16[4,176,128]{2,1,0:T(8,128)(2,1)} %get-tuple-element.53), channel_id=1, source_target_pairs={{0,16},{4,20},{8,24},{12,28},{16,0},{20,4},{24,8},{28,12},{32,48},... | collective-permute-start | bytes 540680 | tf_op jit(solution)/shard_map/ppermute | solution.py:484
  74.8 0.7 collective-permute-start.11
  75.6 7.2 %collective-permute-start.13 = (bf16[4,176,128]{2,1,0:T(8,128)(2,1)}, bf16[4,176,128]{2,1,0:T(8,128)(2,1)S(1)}, u32[]{:S(2)}, u32[]{:S(2)}) collective-permute-start(bf16[4,176,128]{2,1,0:T(8,128)(2,1)} %get-tuple-element.56), channel_id=1, source_target_pairs={{0,128},{4,132},{8,136},{12,140},{16,144},{20,148},{24,152},{28,15... | collective-permute-start | bytes 540680 | tf_op jit(solution)/shard_map/ppermute | solution.py:484
  82.7 0.9 constant_dynamic-update-slice_fusion.26
  83.6 0.9 constant_dynamic-update-slice_fusion.35
  84.6 1.1 fusion.15
  85.7 1.3 collective-permute-start.17
  87.0 2.4 %collective-permute-start.18 = (bf16[176,128]{1,0:T(8,128)(2,1)S(1)}, bf16[176,128]{1,0:T(8,128)(2,1)S(1)}, u32[]{:S(2)}, u32[]{:S(2)}) collective-permute-start(bf16[176,128]{1,0:T(8,128)(2,1)S(1)} %get-tuple-element.87), channel_id=1, source_target_pairs={{0,2},{1,3},{2,0},{3,1},{4,6},{5,7},{6,4},{7,5},{8,10},{9,11},{10,... | collective-permute-start | bytes 135176 | tf_op jit(solution)/shard_map/ppermute | solution.py:490
  89.8 0.7 collective-permute-start.15
  90.5 0.9 collective-permute-done.18
  91.4 2.3 %collective-permute-done.19 = bf16[176,128]{1,0:T(8,128)(2,1)S(1)} collective-permute-done((bf16[176,128]{1,0:T(8,128)(2,1)S(1)}, bf16[176,128]{1,0:T(8,128)(2,1)S(1)}, u32[]{:S(2)}, u32[]{:S(2)}) %collective-permute-start.19) | collective-permute-done | bytes 45088 | tf_op jit(solution)/shard_map/ppermute | solution.py:490
  93.8 1.5 %collective-permute-start.25 = (bf16[176,128]{1,0:T(8,128)(2,1)S(1)}, bf16[176,128]{1,0:T(8,128)(2,1)S(1)}, u32[]{:S(2)}, u32[]{:S(2)}) collective-permute-start(bf16[176,128]{1,0:T(8,128)(2,1)S(1)} %fusion.2), channel_id=1, source_target_pairs={{0,128},{4,132},{8,136},{12,140},{16,144},{20,148},{24,152},{28,15... | collective-permute-start | bytes 135176 | tf_op jit(solution)/shard_map/ppermute | solution.py:487
  95.3 1.1 collective-permute-start.26
  96.7 6.0 %collective-permute-start.16 = (bf16[3,176,128]{2,1,0:T(8,128)(2,1)S(1)}, bf16[3,176,128]{2,1,0:T(8,128)(2,1)S(1)}, u32[]{:S(2)}, u32[]{:S(2)}) collective-permute-start(bf16[3,176,128]{2,1,0:T(8,128)(2,1)S(1)} %copy-done.30), channel_id=1, source_target_pairs={{64,144},{68,148},{72,152},{76,156},{80,128},{84,132},{88,136},{92... | collective-permute-start | bytes 405512 | tf_op jit(solution)/shard_map/ppermute | solution.py:484
  102.8 0.6 collective-permute-start.27
  103.4 2.1 %collective-permute-start.20 = (bf16[4,176,128]{2,1,0:T(8,128)(2,1)S(1)}, bf16[4,176,128]{2,1,0:T(8,128)(2,1)S(1)}, u32[]{:S(2)}, u32[]{:S(2)}) collective-permute-start(bf16[4,176,128]{2,1,0:T(8,128)(2,1)S(1)} %copy-done.26), channel_id=1, source_target_pairs={{64,128},{68,132},{72,136},{76,140},{80,144},{84,148},{88,152},{92... | collective-permute-start | bytes 540680 | tf_op jit(solution)/shard_map/ppermute | solution.py:484
  105.5 0.7 collective-permute-start.21
  106.2 6.4 %collective-permute-start.28 = (bf16[176,128]{1,0:T(8,128)(2,1)S(1)}, bf16[176,128]{1,0:T(8,128)(2,1)S(1)}, u32[]{:S(2)}, u32[]{:S(2)}) collective-permute-start(bf16[176,128]{1,0:T(8,128)(2,1)S(1)} %add_convert_fusion.1), channel_id=1, source_target_pairs={{0,16},{4,20},{8,24},{12,28},{16,0},{20,4},{24,8},{28,12},{32,48},... | collective-permute-start | bytes 135176 | tf_op jit(solution)/shard_map/ppermute | solution.py:487
  112.6 1.6 %collective-permute-start.29 = (bf16[176,128]{1,0:T(8,128)(2,1)S(1)}, bf16[176,128]{1,0:T(8,128)(2,1)S(1)}, u32[]{:S(2)}, u32[]{:S(2)}) collective-permute-start(bf16[176,128]{1,0:T(8,128)(2,1)S(1)} %add_convert_fusion.1), channel_id=1, source_target_pairs={{0,32},{4,36},{8,40},{12,44},{16,48},{20,52},{24,56},{28,60},{32,0... | collective-permute-start | bytes 135176 | tf_op jit(solution)/shard_map/ppermute | solution.py:487
  114.2 1.9 %collective-permute-start.30 = (bf16[176,128]{1,0:T(8,128)(2,1)S(1)}, bf16[176,128]{1,0:T(8,128)(2,1)S(1)}, u32[]{:S(2)}, u32[]{:S(2)}) collective-permute-start(bf16[176,128]{1,0:T(8,128)(2,1)S(1)} %add_convert_fusion.1), channel_id=1, source_target_pairs={{0,48},{4,52},{8,56},{12,60},{16,32},{20,36},{24,40},{28,44},{32,1... | collective-permute-start | bytes 135176 | tf_op jit(solution)/shard_map/ppermute | solution.py:487
  116.3 5.5 %collective-permute-start.22 = (bf16[10,176,128]{2,1,0:T(8,128)(2,1)S(1)}, bf16[10,176,128]{2,1,0:T(8,128)(2,1)S(1)}, u32[]{:S(2)}, u32[]{:S(2)}) collective-permute-start(bf16[10,176,128]{2,1,0:T(8,128)(2,1)S(1)} %get-tuple-element.98), channel_id=1, source_target_pairs={{0,4},{4,0},{8,12},{12,8},{16,20},{20,16},{24,28},{28,24},{32,36},... | collective-permute-start | bytes 1351688 | tf_op jit(solution)/shard_map/ppermute | solution.py:455
  121.7 0.7 collective-permute-start.23
  122.6 1.1 collective-permute-start.32
  123.7 2.7 %collective-permute-start.33 = (bf16[176,128]{1,0:T(8,128)(2,1)S(1)}, bf16[176,128]{1,0:T(8,128)(2,1)S(1)}, u32[]{:S(2)}, u32[]{:S(2)}) collective-permute-start(bf16[176,128]{1,0:T(8,128)(2,1)S(1)} %add_convert_fusion), channel_id=1, source_target_pairs={{0,3},{1,2},{2,1},{3,0},{4,7},{5,6},{6,5},{7,4},{8,11},{9,10},{10,... | collective-permute-start | bytes 135176 | tf_op jit(solution)/shard_map/ppermute | solution.py:490
  126.4 0.6 collective-permute-done.32
  127.1 0.8 collective-permute-done.33
  127.9 7.1 %collective-permute-start.34 = (bf16[4,176,128]{2,1,0:T(8,128)(2,1)S(1)}, bf16[4,176,128]{2,1,0:T(8,128)(2,1)S(1)}, u32[]{:S(2)}, u32[]{:S(2)}) collective-permute-start(bf16[4,176,128]{2,1,0:T(8,128)(2,1)S(1)} %pad_maximum_fusion.2.refs_1_), channel_id=1, source_target_pairs={{0,4},{4,0},{8,12},{12,8},{16,20},{20,16},{24,28},{28,24},{32,36},... | collective-permute-start | bytes 540680 | tf_op jit(solution)/shard_map/ppermute | solution.py:487
  135.1 0.6 pad_add_fusion.refs_0_
  135.8 0.7 copy-done.2
  136.6 3.4 %shard_map.122 = bf16[6,64,512]{2,1,0:T(8,128)(2,1)} custom-call(s32[1]{0:T(128)} %bitcast.me_ref, s32[2,64]{1,0:T(2,128)} %bitcast.63, s32[6,1,512]{2,1,0:T(1,128)} %bitcast.58, f32[6,64,512]{2,1,0:T(8,128)} %get-tuple-element.51.center_ref, f32[6,176,128]{2,1,0:T(8,128)} %get-tuple-element.52.gown_ref, bf16[4,176,128]{2,1,0:T(8,128)(2,1)} %copy-done.4, ...), custom_call_target="tpu_custom_call" | custom-call | bytes 3895812 | tf_op jit(solution)/shard_map/pallas_call | solution.py:431
  140.0 0.7 copy-done.12
  140.7 2.4 %shard_map.123 = (f32[27,64,64]{2,1,0:T(8,128)}, f32[8,64,128]{2,1,0:T(8,128)}) custom-call(s32[2]{0:T(128)} %pad_add_fusion.refs_0_, bf16[4,176,128]{2,1,0:T(8,128)(2,1)} %copy-done.1, bf16[4,176,128]{2,1,0:T(8,128)(2,1)} %copy-done.12), custom_call_target="tpu_custom_call" | custom-call | bytes 1064968 | tf_op jit(solution)/shard_map/pallas_call | solution.py:431
  (116 shorter events, 2.6 us)
Async XLA Ops:
  4.3 18.0 %collective-permute-start = (bf16[4,176,128]{2,1,0:T(8,128)(2,1)}, bf16[4,176,128]{2,1,0:T(8,128)(2,1)S(1)}, u32[]{:S(2)}, u32[]{:S(2)}) collective-permute-start(bf16[4,176,128]{2,1,0:T(8,128)(2,1)} %get-tuple-element.40), channel_id=1, source_target_pairs={{0,16},{4,20},{8,24},{12,28},{16,0},{20,4},{24,8},{28,12},{32,48},... | collective-permute-start | bytes 540680 | tf_op jit(solution)/shard_map/ppermute | solution.py:443
  7.3 19.9 %collective-permute-start.1 = (bf16[4,176,128]{2,1,0:T(8,128)(2,1)}, bf16[4,176,128]{2,1,0:T(8,128)(2,1)S(1)}, u32[]{:S(2)}, u32[]{:S(2)}) collective-permute-start(bf16[4,176,128]{2,1,0:T(8,128)(2,1)} %get-tuple-element.41), channel_id=1, source_target_pairs={{16,32},{20,36},{24,40},{28,44},{32,16},{36,20},{40,24},{44,28},{8... | collective-permute-start | bytes 540680 | tf_op jit(solution)/shard_map/ppermute | solution.py:443
  8.0 23.6 %collective-permute-start.2 = (bf16[3,176,128]{2,1,0:T(8,128)(2,1)}, bf16[3,176,128]{2,1,0:T(8,128)(2,1)S(1)}, u32[]{:S(2)}, u32[]{:S(2)}) collective-permute-start(bf16[3,176,128]{2,1,0:T(8,128)(2,1)} %get-tuple-element.42), channel_id=1, source_target_pairs={{0,144},{4,148},{8,152},{12,156},{16,128},{20,132},{24,136},{28,14... | collective-permute-start | bytes 405512 | tf_op jit(solution)/shard_map/ppermute | solution.py:443
  15.5 17.4 %collective-permute-start.3 = (bf16[4,176,128]{2,1,0:T(8,128)(2,1)}, bf16[4,176,128]{2,1,0:T(8,128)(2,1)S(1)}, u32[]{:S(2)}, u32[]{:S(2)}) collective-permute-start(bf16[4,176,128]{2,1,0:T(8,128)(2,1)} %get-tuple-element.43), channel_id=1, source_target_pairs={{0,128},{4,132},{8,136},{12,140},{16,144},{20,148},{24,152},{28,15... | collective-permute-start | bytes 540680 | tf_op jit(solution)/shard_map/ppermute | solution.py:443
  16.5 17.1 %collective-permute-start.4 = (bf16[3,176,128]{2,1,0:T(8,128)(2,1)}, bf16[3,176,128]{2,1,0:T(8,128)(2,1)S(1)}, u32[]{:S(2)}, u32[]{:S(2)}) collective-permute-start(bf16[3,176,128]{2,1,0:T(8,128)(2,1)} %get-tuple-element.44), channel_id=1, source_target_pairs={{16,160},{20,164},{24,168},{28,172},{32,144},{36,148},{40,152},{44... | collective-permute-start | bytes 405512 | tf_op jit(solution)/shard_map/ppermute | solution.py:443
  20.1 1.5 %copy-start.14 = (bf16[2,176,128]{2,1,0:T(8,128)(2,1)S(1)}, bf16[2,176,128]{2,1,0:T(8,128)(2,1)}, u32[]{:S(2)}) copy-start(bf16[2,176,128]{2,1,0:T(8,128)(2,1)} %get-tuple-element.48) | copy-start | bytes 270340
  20.1 1.5 %copy-start.15 = (bf16[2,176,128]{2,1,0:T(8,128)(2,1)S(1)}, bf16[2,176,128]{2,1,0:T(8,128)(2,1)}, u32[]{:S(2)}) copy-start(bf16[2,176,128]{2,1,0:T(8,128)(2,1)} %get-tuple-element.49) | copy-start | bytes 270340
  20.7 1.6 %copy-start.28 = (bf16[3,176,128]{2,1,0:T(8,128)(2,1)S(1)}, bf16[3,176,128]{2,1,0:T(8,128)(2,1)}, u32[]{:S(2)}) copy-start(bf16[3,176,128]{2,1,0:T(8,128)(2,1)} %get-tuple-element.45) | copy-start | bytes 405508
  20.7 6.5 %copy-start.25 = (bf16[4,176,128]{2,1,0:T(8,128)(2,1)S(1)}, bf16[4,176,128]{2,1,0:T(8,128)(2,1)}, u32[]{:S(2)}) copy-start(bf16[4,176,128]{2,1,0:T(8,128)(2,1)} %get-tuple-element.46) | copy-start | bytes 540676
  20.7 10.8 %copy-start.27 = (bf16[3,176,128]{2,1,0:T(8,128)(2,1)S(1)}, bf16[3,176,128]{2,1,0:T(8,128)(2,1)}, u32[]{:S(2)}) copy-start(bf16[3,176,128]{2,1,0:T(8,128)(2,1)} %get-tuple-element.47) | copy-start | bytes 405508
  21.6 18.5 %copy-start = (bf16[27,64,64]{2,1,0:T(8,128)(2,1)S(1)}, bf16[27,64,64]{2,1,0:T(8,128)(2,1)}, u32[]{:S(2)}) copy-start(bf16[27,64,64]{2,1,0:T(8,128)(2,1)} %param.13) | copy-start | bytes 663556
  22.3 18.1 %copy-start.20 = (bf16[4,176,128]{2,1,0:T(8,128)(2,1)}, bf16[4,176,128]{2,1,0:T(8,128)(2,1)S(1)}, u32[]{:S(2)}) copy-start(bf16[4,176,128]{2,1,0:T(8,128)(2,1)S(1)} %collective-permute-done.rest_0_) | copy-start | bytes 540676
  22.3 11.9 %collective-permute-start.5 = (bf16[3,176,128]{2,1,0:T(8,128)(2,1)S(1)}, bf16[3,176,128]{2,1,0:T(8,128)(2,1)S(1)}, u32[]{:S(2)}, u32[]{:S(2)}) collective-permute-start(bf16[3,176,128]{2,1,0:T(8,128)(2,1)S(1)} %copy-done.28), channel_id=1, source_target_pairs={{64,144},{68,148},{72,152},{76,156},{80,128},{84,132},{88,136},{92... | collective-permute-start | bytes 405512 | tf_op jit(solution)/shard_map/ppermute | solution.py:443
  27.2 13.1 %copy-start.21 = (bf16[4,176,128]{2,1,0:T(8,128)(2,1)}, bf16[4,176,128]{2,1,0:T(8,128)(2,1)S(1)}, u32[]{:S(2)}) copy-start(bf16[4,176,128]{2,1,0:T(8,128)(2,1)S(1)} %collective-permute-done.1.rest_1_) | copy-start | bytes 540676
  27.2 7.7 %collective-permute-start.6 = (bf16[4,176,128]{2,1,0:T(8,128)(2,1)S(1)}, bf16[4,176,128]{2,1,0:T(8,128)(2,1)S(1)}, u32[]{:S(2)}, u32[]{:S(2)}) collective-permute-start(bf16[4,176,128]{2,1,0:T(8,128)(2,1)S(1)} %copy-done.25), channel_id=1, source_target_pairs={{64,128},{68,132},{72,136},{76,140},{80,144},{84,148},{88,152},{92... | collective-permute-start | bytes 540680 | tf_op jit(solution)/shard_map/ppermute | solution.py:443
  31.5 8.9 %copy-start.16 = (bf16[3,176,128]{2,1,0:T(8,128)(2,1)}, bf16[3,176,128]{2,1,0:T(8,128)(2,1)S(1)}, u32[]{:S(2)}) copy-start(bf16[3,176,128]{2,1,0:T(8,128)(2,1)S(1)} %collective-permute-done.2.rest_2_) | copy-start | bytes 405508
  31.5 4.1 %collective-permute-start.7 = (bf16[3,176,128]{2,1,0:T(8,128)(2,1)S(1)}, bf16[3,176,128]{2,1,0:T(8,128)(2,1)S(1)}, u32[]{:S(2)}, u32[]{:S(2)}) collective-permute-start(bf16[3,176,128]{2,1,0:T(8,128)(2,1)S(1)} %copy-done.27), channel_id=1, source_target_pairs={{80,160},{84,164},{88,168},{92,172},{96,144},{100,148},{104,152},{... | collective-permute-start | bytes 405512 | tf_op jit(solution)/shard_map/ppermute | solution.py:443
  32.9 7.5 %copy-start.22 = (bf16[4,176,128]{2,1,0:T(8,128)(2,1)}, bf16[4,176,128]{2,1,0:T(8,128)(2,1)S(1)}, u32[]{:S(2)}) copy-start(bf16[4,176,128]{2,1,0:T(8,128)(2,1)S(1)} %collective-permute-done.3.rest_3_) | copy-start | bytes 540676
  33.6 6.9 %copy-start.17 = (bf16[3,176,128]{2,1,0:T(8,128)(2,1)}, bf16[3,176,128]{2,1,0:T(8,128)(2,1)S(1)}, u32[]{:S(2)}) copy-start(bf16[3,176,128]{2,1,0:T(8,128)(2,1)S(1)} %collective-permute-done.4.rest_4_) | copy-start | bytes 405508
  34.2 6.5 %copy-start.18 = (bf16[3,176,128]{2,1,0:T(8,128)(2,1)}, bf16[3,176,128]{2,1,0:T(8,128)(2,1)S(1)}, u32[]{:S(2)}) copy-start(bf16[3,176,128]{2,1,0:T(8,128)(2,1)S(1)} %collective-permute-done.5.rest_5_) | copy-start | bytes 405508
  34.9 5.8 %copy-start.23 = (bf16[4,176,128]{2,1,0:T(8,128)(2,1)}, bf16[4,176,128]{2,1,0:T(8,128)(2,1)S(1)}, u32[]{:S(2)}) copy-start(bf16[4,176,128]{2,1,0:T(8,128)(2,1)S(1)} %collective-permute-done.6.rest_6_) | copy-start | bytes 540676
  35.6 5.1 %copy-start.19 = (bf16[3,176,128]{2,1,0:T(8,128)(2,1)}, bf16[3,176,128]{2,1,0:T(8,128)(2,1)S(1)}, u32[]{:S(2)}) copy-start(bf16[3,176,128]{2,1,0:T(8,128)(2,1)S(1)} %collective-permute-done.7.rest_7_) | copy-start | bytes 405508
  36.3 8.3 %collective-permute-start.8 = (bf16[10,176,128]{2,1,0:T(8,128)(2,1)}, bf16[10,176,128]{2,1,0:T(8,128)(2,1)}, u32[]{:S(2)}, u32[]{:S(2)}) collective-permute-start(bf16[10,176,128]{2,1,0:T(8,128)(2,1)} %get-tuple-element.106), channel_id=1, source_target_pairs={{0,4},{4,0},{8,12},{12,8},{16,20},{20,16},{24,28},{28,24},{32,36},... | collective-permute-start | bytes 1351688 | tf_op jit(solution)/shard_map/ppermute | solution.py:455
  38.7 6.0 %collective-permute-start.9 = (bf16[10,176,128]{2,1,0:T(8,128)(2,1)}, bf16[10,176,128]{2,1,0:T(8,128)(2,1)}, u32[]{:S(2)}, u32[]{:S(2)}) collective-permute-start(bf16[10,176,128]{2,1,0:T(8,128)(2,1)} %get-tuple-element.105), channel_id=1, source_target_pairs={{4,8},{8,4},{20,24},{24,20},{36,40},{40,36},{52,56},{56,52},{68,72... | collective-permute-start | bytes 1351688 | tf_op jit(solution)/shard_map/ppermute | solution.py:455
  42.0 1.4 %copy-start.13 = (bf16[1,6,4,4,512]{4,3,2,1,0:T(4,128)(2,1)S(1)}, bf16[1,6,4,4,512]{4,3,2,1,0:T(4,128)(2,1)}, u32[]{:S(2)}) copy-start(bf16[1,6,4,4,512]{4,3,2,1,0:T(4,128)(2,1)} %param.15) | copy-start | bytes 294916
  64.4 25.4 %copy-start.31 = (bf16[3,176,128]{2,1,0:T(8,128)(2,1)S(1)}, bf16[3,176,128]{2,1,0:T(8,128)(2,1)}, u32[]{:S(2)}) copy-start(bf16[3,176,128]{2,1,0:T(8,128)(2,1)} %get-tuple-element.61) | copy-start | bytes 405508
  64.4 20.1 %collective-permute-start.14 = (bf16[4,176,128]{2,1,0:T(8,128)(2,1)}, bf16[4,176,128]{2,1,0:T(8,128)(2,1)S(1)}, u32[]{:S(2)}, u32[]{:S(2)}) collective-permute-start(bf16[4,176,128]{2,1,0:T(8,128)(2,1)} %bitcast.64), channel_id=1, source_target_pairs={{0,4},{4,0},{8,12},{12,8},{16,20},{20,16},{24,28},{28,24},{32,36},... | collective-permute-start | bytes 540680 | tf_op jit(solution)/shard_map/ppermute | solution.py:487
  68.6 18.4 %collective-permute-start.10 = (bf16[4,176,128]{2,1,0:T(8,128)(2,1)}, bf16[4,176,128]{2,1,0:T(8,128)(2,1)S(1)}, u32[]{:S(2)}, u32[]{:S(2)}) collective-permute-start(bf16[4,176,128]{2,1,0:T(8,128)(2,1)} %get-tuple-element.53), channel_id=1, source_target_pairs={{0,16},{4,20},{8,24},{12,28},{16,0},{20,4},{24,8},{28,12},{32,48},... | collective-permute-start | bytes 540680 | tf_op jit(solution)/shard_map/ppermute | solution.py:484
  74.8 14.7 %collective-permute-start.11 = (bf16[4,176,128]{2,1,0:T(8,128)(2,1)}, bf16[4,176,128]{2,1,0:T(8,128)(2,1)S(1)}, u32[]{:S(2)}, u32[]{:S(2)}) collective-permute-start(bf16[4,176,128]{2,1,0:T(8,128)(2,1)} %get-tuple-element.54), channel_id=1, source_target_pairs={{16,32},{20,36},{24,40},{28,44},{32,16},{36,20},{40,24},{44,28},{8... | collective-permute-start | bytes 540680 | tf_op jit(solution)/shard_map/ppermute | solution.py:484
  75.5 19.9 %collective-permute-start.12 = (bf16[3,176,128]{2,1,0:T(8,128)(2,1)}, bf16[3,176,128]{2,1,0:T(8,128)(2,1)S(1)}, u32[]{:S(2)}, u32[]{:S(2)}) collective-permute-start(bf16[3,176,128]{2,1,0:T(8,128)(2,1)} %get-tuple-element.55), channel_id=1, source_target_pairs={{0,144},{4,148},{8,152},{12,156},{16,128},{20,132},{24,136},{28,14... | collective-permute-start | bytes 405512 | tf_op jit(solution)/shard_map/ppermute | solution.py:484
  75.6 27.8 %collective-permute-start.13 = (bf16[4,176,128]{2,1,0:T(8,128)(2,1)}, bf16[4,176,128]{2,1,0:T(8,128)(2,1)S(1)}, u32[]{:S(2)}, u32[]{:S(2)}) collective-permute-start(bf16[4,176,128]{2,1,0:T(8,128)(2,1)} %get-tuple-element.56), channel_id=1, source_target_pairs={{0,128},{4,132},{8,136},{12,140},{16,144},{20,148},{24,152},{28,15... | collective-permute-start | bytes 540680 | tf_op jit(solution)/shard_map/ppermute | solution.py:484
  83.6 13.1 %copy-start.30 = (bf16[3,176,128]{2,1,0:T(8,128)(2,1)S(1)}, bf16[3,176,128]{2,1,0:T(8,128)(2,1)}, u32[]{:S(2)}) copy-start(bf16[3,176,128]{2,1,0:T(8,128)(2,1)} %get-tuple-element.62) | copy-start | bytes 405508
  84.6 18.8 %copy-start.26 = (bf16[4,176,128]{2,1,0:T(8,128)(2,1)S(1)}, bf16[4,176,128]{2,1,0:T(8,128)(2,1)}, u32[]{:S(2)}) copy-start(bf16[4,176,128]{2,1,0:T(8,128)(2,1)} %get-tuple-element.65) | copy-start | bytes 540676
  84.6 20.9 %copy-start.29 = (bf16[3,176,128]{2,1,0:T(8,128)(2,1)S(1)}, bf16[3,176,128]{2,1,0:T(8,128)(2,1)}, u32[]{:S(2)}) copy-start(bf16[3,176,128]{2,1,0:T(8,128)(2,1)} %get-tuple-element.66) | copy-start | bytes 405508
  85.7 4.1 %collective-permute-start.17 = (bf16[176,128]{1,0:T(8,128)(2,1)S(1)}, bf16[176,128]{1,0:T(8,128)(2,1)S(1)}, u32[]{:S(2)}, u32[]{:S(2)}) collective-permute-start(bf16[176,128]{1,0:T(8,128)(2,1)S(1)} %get-tuple-element.88), channel_id=1, source_target_pairs={{0,1},{1,0},{2,3},{3,2},{4,5},{5,4},{6,7},{7,6},{8,9},{9,8},{10,11... | collective-permute-start | bytes 135176 | tf_op jit(solution)/shard_map/ppermute | solution.py:490
  87.0 40.9 %copy-start.4 = (bf16[4,176,128]{2,1,0:T(8,128)(2,1)}, bf16[4,176,128]{2,1,0:T(8,128)(2,1)S(1)}, u32[]{:S(2)}) copy-start(bf16[4,176,128]{2,1,0:T(8,128)(2,1)S(1)} %collective-permute-done.10.rest_0_) | copy-start | bytes 540676
  87.0 4.4 %collective-permute-start.18 = (bf16[176,128]{1,0:T(8,128)(2,1)S(1)}, bf16[176,128]{1,0:T(8,128)(2,1)S(1)}, u32[]{:S(2)}, u32[]{:S(2)}) collective-permute-start(bf16[176,128]{1,0:T(8,128)(2,1)S(1)} %get-tuple-element.87), channel_id=1, source_target_pairs={{0,2},{1,3},{2,0},{3,1},{4,6},{5,7},{6,4},{7,5},{8,10},{9,11},{10,... | collective-permute-start | bytes 135176 | tf_op jit(solution)/shard_map/ppermute | solution.py:490
  89.5 38.4 %copy-start.5 = (bf16[4,176,128]{2,1,0:T(8,128)(2,1)}, bf16[4,176,128]{2,1,0:T(8,128)(2,1)S(1)}, u32[]{:S(2)}) copy-start(bf16[4,176,128]{2,1,0:T(8,128)(2,1)S(1)} %collective-permute-done.11.rest_1_) | copy-start | bytes 540676
  89.5 4.2 %collective-permute-start.19 = (bf16[176,128]{1,0:T(8,128)(2,1)S(1)}, bf16[176,128]{1,0:T(8,128)(2,1)S(1)}, u32[]{:S(2)}, u32[]{:S(2)}) collective-permute-start(bf16[176,128]{1,0:T(8,128)(2,1)S(1)} %get-tuple-element.86), channel_id=1, source_target_pairs={{0,3},{1,2},{2,1},{3,0},{4,7},{5,6},{6,5},{7,4},{8,11},{9,10},{10,... | collective-permute-start | bytes 135176 | tf_op jit(solution)/shard_map/ppermute | solution.py:490
  89.8 22.8 %collective-permute-start.15 = (bf16[3,176,128]{2,1,0:T(8,128)(2,1)S(1)}, bf16[3,176,128]{2,1,0:T(8,128)(2,1)S(1)}, u32[]{:S(2)}, u32[]{:S(2)}) collective-permute-start(bf16[3,176,128]{2,1,0:T(8,128)(2,1)S(1)} %copy-done.31), channel_id=1, source_target_pairs={{16,160},{20,164},{24,168},{28,172},{32,144},{36,148},{40,152},{44... | collective-permute-start | bytes 405512 | tf_op jit(solution)/shard_map/ppermute | solution.py:484
  93.7 3.0 %collective-permute-start.24 = (bf16[176,128]{1,0:T(8,128)(2,1)S(1)}, bf16[176,128]{1,0:T(8,128)(2,1)S(1)}, u32[]{:S(2)}, u32[]{:S(2)}) collective-permute-start(bf16[176,128]{1,0:T(8,128)(2,1)S(1)} %fusion.2), channel_id=1, source_target_pairs={{0,64},{4,68},{8,72},{12,76},{16,80},{20,84},{24,88},{28,92},{32,9... | collective-permute-start | bytes 135176 | tf_op jit(solution)/shard_map/ppermute | solution.py:487
  93.8 8.9 %collective-permute-start.25 = (bf16[176,128]{1,0:T(8,128)(2,1)S(1)}, bf16[176,128]{1,0:T(8,128)(2,1)S(1)}, u32[]{:S(2)}, u32[]{:S(2)}) collective-permute-start(bf16[176,128]{1,0:T(8,128)(2,1)S(1)} %fusion.2), channel_id=1, source_target_pairs={{0,128},{4,132},{8,136},{12,140},{16,144},{20,148},{24,152},{28,15... | collective-permute-start | bytes 135176 | tf_op jit(solution)/shard_map/ppermute | solution.py:487
  95.3 40.4 %copy-start.8 = (bf16[3,176,128]{2,1,0:T(8,128)(2,1)}, bf16[3,176,128]{2,1,0:T(8,128)(2,1)S(1)}, u32[]{:S(2)}) copy-start(bf16[3,176,128]{2,1,0:T(8,128)(2,1)S(1)} %collective-permute-done.12.rest_2_) | copy-start | bytes 405508
  95.3 7.4 %collective-permute-start.26 = (bf16[176,128]{1,0:T(8,128)(2,1)S(1)}, bf16[176,128]{1,0:T(8,128)(2,1)S(1)}, u32[]{:S(2)}, u32[]{:S(2)}) collective-permute-start(bf16[176,128]{1,0:T(8,128)(2,1)S(1)} %fusion.2), channel_id=1, source_target_pairs={{0,192},{4,196},{8,200},{12,204},{16,208},{20,212},{24,216},{28,22... | collective-permute-start | bytes 135176 | tf_op jit(solution)/shard_map/ppermute | solution.py:487
  96.7 17.5 %collective-permute-start.16 = (bf16[3,176,128]{2,1,0:T(8,128)(2,1)S(1)}, bf16[3,176,128]{2,1,0:T(8,128)(2,1)S(1)}, u32[]{:S(2)}, u32[]{:S(2)}) collective-permute-start(bf16[3,176,128]{2,1,0:T(8,128)(2,1)S(1)} %copy-done.30), channel_id=1, source_target_pairs={{64,144},{68,148},{72,152},{76,156},{80,128},{84,132},{88,136},{92... | collective-permute-start | bytes 405512 | tf_op jit(solution)/shard_map/ppermute | solution.py:484
  102.8 3.4 %collective-permute-start.27 = (bf16[176,128]{1,0:T(8,128)(2,1)S(1)}, bf16[176,128]{1,0:T(8,128)(2,1)S(1)}, u32[]{:S(2)}, u32[]{:S(2)}) collective-permute-start(bf16[176,128]{1,0:T(8,128)(2,1)S(1)} %add_convert_fusion.2), channel_id=1, source_target_pairs={{0,8},{4,12},{8,0},{12,4},{16,24},{20,28},{24,16},{28,20},{32,40},... | collective-permute-start | bytes 135176 | tf_op jit(solution)/shard_map/ppermute | solution.py:487
  103.4 32.4 %copy-start.6 = (bf16[4,176,128]{2,1,0:T(8,128)(2,1)}, bf16[4,176,128]{2,1,0:T(8,128)(2,1)S(1)}, u32[]{:S(2)}) copy-start(bf16[4,176,128]{2,1,0:T(8,128)(2,1)S(1)} %collective-permute-done.13.rest_3_) | copy-start | bytes 540676
  103.4 12.8 %collective-permute-start.20 = (bf16[4,176,128]{2,1,0:T(8,128)(2,1)S(1)}, bf16[4,176,128]{2,1,0:T(8,128)(2,1)S(1)}, u32[]{:S(2)}, u32[]{:S(2)}) collective-permute-start(bf16[4,176,128]{2,1,0:T(8,128)(2,1)S(1)} %copy-done.26), channel_id=1, source_target_pairs={{64,128},{68,132},{72,136},{76,140},{80,144},{84,148},{88,152},{92... | collective-permute-start | bytes 540680 | tf_op jit(solution)/shard_map/ppermute | solution.py:484
  105.5 10.7 %collective-permute-start.21 = (bf16[3,176,128]{2,1,0:T(8,128)(2,1)S(1)}, bf16[3,176,128]{2,1,0:T(8,128)(2,1)S(1)}, u32[]{:S(2)}, u32[]{:S(2)}) collective-permute-start(bf16[3,176,128]{2,1,0:T(8,128)(2,1)S(1)} %copy-done.29), channel_id=1, source_target_pairs={{80,160},{84,164},{88,168},{92,172},{96,144},{100,148},{104,152},{... | collective-permute-start | bytes 405512 | tf_op jit(solution)/shard_map/ppermute | solution.py:484
  106.2 16.2 %collective-permute-start.28 = (bf16[176,128]{1,0:T(8,128)(2,1)S(1)}, bf16[176,128]{1,0:T(8,128)(2,1)S(1)}, u32[]{:S(2)}, u32[]{:S(2)}) collective-permute-start(bf16[176,128]{1,0:T(8,128)(2,1)S(1)} %add_convert_fusion.1), channel_id=1, source_target_pairs={{0,16},{4,20},{8,24},{12,28},{16,0},{20,4},{24,8},{28,12},{32,48},... | collective-permute-start | bytes 135176 | tf_op jit(solution)/shard_map/ppermute | solution.py:487
  112.6 23.1 %copy-start.9 = (bf16[3,176,128]{2,1,0:T(8,128)(2,1)}, bf16[3,176,128]{2,1,0:T(8,128)(2,1)S(1)}, u32[]{:S(2)}) copy-start(bf16[3,176,128]{2,1,0:T(8,128)(2,1)S(1)} %collective-permute-done.15.rest_4_) | copy-start | bytes 405508
  112.6 9.8 %collective-permute-start.29 = (bf16[176,128]{1,0:T(8,128)(2,1)S(1)}, bf16[176,128]{1,0:T(8,128)(2,1)S(1)}, u32[]{:S(2)}, u32[]{:S(2)}) collective-permute-start(bf16[176,128]{1,0:T(8,128)(2,1)S(1)} %add_convert_fusion.1), channel_id=1, source_target_pairs={{0,32},{4,36},{8,40},{12,44},{16,48},{20,52},{24,56},{28,60},{32,0... | collective-permute-start | bytes 135176 | tf_op jit(solution)/shard_map/ppermute | solution.py:487
  114.2 21.5 %copy-start.10 = (bf16[3,176,128]{2,1,0:T(8,128)(2,1)}, bf16[3,176,128]{2,1,0:T(8,128)(2,1)S(1)}, u32[]{:S(2)}) copy-start(bf16[3,176,128]{2,1,0:T(8,128)(2,1)S(1)} %collective-permute-done.16.rest_5_) | copy-start | bytes 405508
  114.2 8.2 %collective-permute-start.30 = (bf16[176,128]{1,0:T(8,128)(2,1)S(1)}, bf16[176,128]{1,0:T(8,128)(2,1)S(1)}, u32[]{:S(2)}, u32[]{:S(2)}) collective-permute-start(bf16[176,128]{1,0:T(8,128)(2,1)S(1)} %add_convert_fusion.1), channel_id=1, source_target_pairs={{0,48},{4,52},{8,56},{12,60},{16,32},{20,36},{24,40},{28,44},{32,1... | collective-permute-start | bytes 135176 | tf_op jit(solution)/shard_map/ppermute | solution.py:487
  116.2 19.6 %copy-start.7 = (bf16[4,176,128]{2,1,0:T(8,128)(2,1)}, bf16[4,176,128]{2,1,0:T(8,128)(2,1)S(1)}, u32[]{:S(2)}) copy-start(bf16[4,176,128]{2,1,0:T(8,128)(2,1)S(1)} %collective-permute-done.20.rest_6_) | copy-start | bytes 540676
  116.2 19.5 %copy-start.11 = (bf16[3,176,128]{2,1,0:T(8,128)(2,1)}, bf16[3,176,128]{2,1,0:T(8,128)(2,1)S(1)}, u32[]{:S(2)}) copy-start(bf16[3,176,128]{2,1,0:T(8,128)(2,1)S(1)} %collective-permute-done.21.rest_7_) | copy-start | bytes 405508
  116.3 19.4 %collective-permute-start.22 = (bf16[10,176,128]{2,1,0:T(8,128)(2,1)S(1)}, bf16[10,176,128]{2,1,0:T(8,128)(2,1)S(1)}, u32[]{:S(2)}, u32[]{:S(2)}) collective-permute-start(bf16[10,176,128]{2,1,0:T(8,128)(2,1)S(1)} %get-tuple-element.98), channel_id=1, source_target_pairs={{0,4},{4,0},{8,12},{12,8},{16,20},{20,16},{24,28},{28,24},{32,36},... | collective-permute-start | bytes 1351688 | tf_op jit(solution)/shard_map/ppermute | solution.py:455
  121.7 14.0 %collective-permute-start.23 = (bf16[10,176,128]{2,1,0:T(8,128)(2,1)S(1)}, bf16[10,176,128]{2,1,0:T(8,128)(2,1)S(1)}, u32[]{:S(2)}, u32[]{:S(2)}) collective-permute-start(bf16[10,176,128]{2,1,0:T(8,128)(2,1)S(1)} %get-tuple-element.97), channel_id=1, source_target_pairs={{4,8},{8,4},{20,24},{24,20},{36,40},{40,36},{52,56},{56,52},{68,72... | collective-permute-start | bytes 1351688 | tf_op jit(solution)/shard_map/ppermute | solution.py:455
  122.5 3.9 %collective-permute-start.31 = (bf16[176,128]{1,0:T(8,128)(2,1)S(1)}, bf16[176,128]{1,0:T(8,128)(2,1)S(1)}, u32[]{:S(2)}, u32[]{:S(2)}) collective-permute-start(bf16[176,128]{1,0:T(8,128)(2,1)S(1)} %add_convert_fusion), channel_id=1, source_target_pairs={{0,1},{1,0},{2,3},{3,2},{4,5},{5,4},{6,7},{7,6},{8,9},{9,8},{10,11... | collective-permute-start | bytes 135176 | tf_op jit(solution)/shard_map/ppermute | solution.py:490
  122.6 4.5 %collective-permute-start.32 = (bf16[176,128]{1,0:T(8,128)(2,1)S(1)}, bf16[176,128]{1,0:T(8,128)(2,1)S(1)}, u32[]{:S(2)}, u32[]{:S(2)}) collective-permute-start(bf16[176,128]{1,0:T(8,128)(2,1)S(1)} %add_convert_fusion), channel_id=1, source_target_pairs={{0,2},{1,3},{2,0},{3,1},{4,6},{5,7},{6,4},{7,5},{8,10},{9,11},{10,... | collective-permute-start | bytes 135176 | tf_op jit(solution)/shard_map/ppermute | solution.py:490
  123.7 4.2 %collective-permute-start.33 = (bf16[176,128]{1,0:T(8,128)(2,1)S(1)}, bf16[176,128]{1,0:T(8,128)(2,1)S(1)}, u32[]{:S(2)}, u32[]{:S(2)}) collective-permute-start(bf16[176,128]{1,0:T(8,128)(2,1)S(1)} %add_convert_fusion), channel_id=1, source_target_pairs={{0,3},{1,2},{2,1},{3,0},{4,7},{5,6},{6,5},{7,4},{8,11},{9,10},{10,... | collective-permute-start | bytes 135176 | tf_op jit(solution)/shard_map/ppermute | solution.py:490
  127.9 12.1 %copy-start.1 = (bf16[4,176,128]{2,1,0:T(8,128)(2,1)}, bf16[4,176,128]{2,1,0:T(8,128)(2,1)S(1)}, u32[]{:S(2)}) copy-start(bf16[4,176,128]{2,1,0:T(8,128)(2,1)S(1)} %pad_maximum_fusion.2.refs_1_) | copy-start | bytes 540676
  127.9 12.1 %collective-permute-start.34 = (bf16[4,176,128]{2,1,0:T(8,128)(2,1)S(1)}, bf16[4,176,128]{2,1,0:T(8,128)(2,1)S(1)}, u32[]{:S(2)}, u32[]{:S(2)}) collective-permute-start(bf16[4,176,128]{2,1,0:T(8,128)(2,1)S(1)} %pad_maximum_fusion.2.refs_1_), channel_id=1, source_target_pairs={{0,4},{4,0},{8,12},{12,8},{16,20},{20,16},{24,28},{28,24},{32,36},... | collective-permute-start | bytes 540680 | tf_op jit(solution)/shard_map/ppermute | solution.py:487
  135.7 0.9 copy-start.3
  (3 other events, 2.2 us)
